TPU v7x, 32 devices: a whole 2x2x4 slice. The times are simulated.
32 devices in a mesh: gx: 8 (over z, x), gy: 4 (over y, core).
Axes of the slice: x: 2, y: 2, z: 4, core: 2. Of those that a mesh axis runs over, the one named last changes fastest.
Arguments:
- rhs: float32 [48, 3, 256, 512], P(None, None, 'gx', 'gy'), may hold values from -13 to 13
- stiffness: float32 [2, 256, 512], P(None, 'gx', 'gy'), may hold values from 0.2 to 5
- coupling: float32 [2, 256, 512], P(None, 'gx', 'gy'), may hold values from 0.1 to 2
- edges: float32 [12, 256, 512], P(None, 'gx', 'gy'), may hold values from -4 to 4
- flip: int32 [256, 512], P('gx', 'gy'), may hold values from 0 to 1
- pinned: int32 [256, 512], P('gx', 'gy'), may hold values 0 or 1
Outputs:
- solution: float32 [48, 3, 256, 512], P(None, None, 'gx', 'gy')
- residual: float32 [48, 3, 256, 512], P(None, None, 'gx', 'gy')
All inputs are finite; a program needn't handle non-finite values. No bound on the sum of `pinned` on one device may be relied on, other than what follows from the above.
Results may differ from a plain program's by a relative error of at most 0.0003.
Values sent between devices are 32-bit elements; how exact they have to be, the bound alone decides.
No kernel may reach another device: no remote copies, remote signals or barrier semaphores. Data moves between devices by JAX's collectives and lax.ppermute only.
A program may use at most 128 MiB of HBM per device.

v0:
```python
import jax
import jax.numpy as jnp
from jax import lax
from jax.sharding import PartitionSpec as P

ITERS = 6


damping = 0.2


def from_behind(block, axis, distance):
    devices = range(lax.axis_size(axis))
    route = [(i - distance, i) for i in devices if i - distance in devices]
    return lax.ppermute(block, axis, route)


def triangle(corner_p, corner_q, corner_r, stiffness, couple, dir_one, dir_two):
    edge_one = corner_q - corner_p
    edge_two = corner_r - corner_p
    stretch = jnp.sum(dir_one * edge_one + dir_two * edge_two, axis=-3, keepdims=True)
    force_one = stiffness * edge_one + couple * stretch * dir_one
    force_two = stiffness * edge_two + couple * stretch * dir_two
    return (force_one, force_two)


def apply_element_hessian(vertex_extended, parameters):
    first_corner = vertex_extended[..., :-1, :-1]
    second_corner = vertex_extended[..., 1:, :-1]
    third_corner = vertex_extended[..., :-1, 1:]
    fourth_corner = vertex_extended[..., 1:, 1:]
    flipped = parameters[16] > 0.5
    force_one, force_two = triangle(
        first_corner,
        second_corner,
        jnp.where(flipped, fourth_corner, third_corner),
        parameters[0],
        parameters[2],
        parameters[4:7],
        parameters[7:10],
    )
    other_one, other_two = triangle(
        jnp.where(flipped, first_corner, fourth_corner),
        jnp.where(flipped, fourth_corner, third_corner),
        jnp.where(flipped, third_corner, second_corner),
        parameters[1],
        parameters[3],
        parameters[10:13],
        parameters[13:16],
    )
    zero_part = jnp.zeros_like(force_one)
    minus_one = -(force_one + force_two)
    minus_two = -(other_one + other_two)
    acc_a = minus_one + jnp.where(flipped, minus_two, zero_part)
    acc_b = force_one + jnp.where(flipped, zero_part, other_two)
    acc_c = jnp.where(flipped, zero_part, force_two) + jnp.where(flipped, other_two, other_one)
    acc_d = jnp.where(flipped, force_two, zero_part) + jnp.where(flipped, other_one, minus_two)
    leading_dims = [(0, 0)] * (vertex_extended.ndim - 2)
    return (
        jnp.pad(acc_a, leading_dims + [(0, 1), (0, 1)])
        + jnp.pad(acc_b, leading_dims + [(1, 0), (0, 1)])
        + jnp.pad(acc_c, leading_dims + [(0, 1), (1, 0)])
        + jnp.pad(acc_d, leading_dims + [(1, 0), (1, 0)])
    )


def inner(left, right):
    return jnp.sum(left * right, axis=(1, 2, 3))


def expand(values):
    return values[:, None, None, None]


def squares(residual):
    return lax.psum(inner(residual, residual), ("gx", "gy"))


def body(rhs, stiffness, coupling, edges, flip, pinned):
    parameters = jnp.concatenate(
        [stiffness, coupling, edges, flip.astype(jnp.float32)[None]], axis=0
    )
    free = (1 - pinned).astype(jnp.float32)
    pin_weight = pinned.astype(jnp.float32)
    solution = jnp.zeros_like(rhs)
    residual = rhs
    direction = rhs
    norm_now = squares(residual)
    for iteration in range(ITERS):
        masked = free * direction
        above = from_behind(masked[:, :, 0:1, :], "gx", -1)
        tall = jnp.concatenate([masked, above], axis=2)
        beside = from_behind(tall[:, :, :, 0:1], "gy", -1)
        extended = jnp.concatenate([tall, beside], axis=3)
        forces = apply_element_hessian(extended, parameters)
        spill_columns = from_behind(forces[:, :, :, -1:], "gy", 1)
        kept = forces[:, :, :, :-1]
        kept = jnp.concatenate([kept[:, :, :, 0:1] + spill_columns, kept[:, :, :, 1:]], axis=3)
        spill_rows = from_behind(kept[:, :, -1:, :], "gx", 1)
        kept = kept[:, :, :-1, :]
        kept = jnp.concatenate([kept[:, :, 0:1, :] + spill_rows, kept[:, :, 1:, :]], axis=2)
        image = free * (kept + damping * direction) + pin_weight * direction
        alpha = norm_now / lax.psum(inner(direction, image), ("gx", "gy"))
        solution = solution + expand(alpha) * direction
        residual = residual - expand(alpha) * image
        norm_next = squares(residual)
        direction = residual + expand(norm_next / norm_now) * direction
        norm_now = norm_next
    return (solution, residual)


def solution(mesh):
    placed = (
        P(None, None, "gx", "gy"),
        P(None, "gx", "gy"),
        P(None, "gx", "gy"),
        P(None, "gx", "gy"),
        P("gx", "gy"),
        P("gx", "gy"),
    )
    return jax.shard_map(
        body,
        mesh=mesh,
        in_specs=placed,
        out_specs=(P(None, None, "gx", "gy"), P(None, None, "gx", "gy")),
        check_vma=False,
    )
```

profile of v0, /device:TPU:0, one launch (start us, length us, event | category | flops | bytes accessed | tf_op | source)
XLA Modules:
  0.0 840.8 jit_solution(3655101437693308249)
XLA Ops:
  1.4 3.1 copy_multiply_fusion
  5.9 5.8 collective-permute-done
  13.4 2.7 copy.9
  21.5 5.7 add_reduce_fusion.11
  27.3 4.0 add_reduce_fusion.10
  39.6 5.0 collective-permute-start.2
  44.5 3.8 slice.377
  51.7 4.6 collective-permute-start.3
  60.4 40.5 %all-reduce.24 = (f32[48]{0:T(128)S(1)}, f32[48]{0:T(128)S(1)}) all-reduce(f32[48]{0:T(128)S(1)} %multiply_reduce_fusion.11, f32[48]{0:T(128)S(1)} %multiply_reduce_fusion.10), channel_id=1, replica_groups=mesh['gx'=8,'gy'=4] {'gx','gy'}, use_global_device_ids=true, to_apply=%region_1.0 | all-reduce | flops 96 | bytes 768 | tf_op jit(solution)/shard_map/psum | solution.py:76
  100.9 5.9 multiply_reduce_fusion.9
  106.9 39.7 %psum.86 = f32[48]{0:T(128)S(1)} all-reduce(f32[48]{0:T(128)S(1)} %get-tuple-element.52), channel_id=1, replica_groups=mesh['gx'=8,'gy'=4] {'gx','gy'}, use_global_device_ids=true, to_apply=%region_7.8 | all-reduce | flops 48 | bytes 384 | tf_op jit(solution)/shard_map/psum | solution.py:76
  146.6 4.7 broadcast_multiply_fusion.4
  152.6 5.2 collective-permute-done.4
  159.4 2.8 copy.19
  167.7 5.7 add_reduce_fusion.9
  173.5 4.0 add_reduce_fusion.8
  185.7 4.7 collective-permute-start.6
  195.1 2.7 slice_add_fusion.4
  198.0 4.9 collective-permute-start.7
  206.1 40.2 %psum.87 = f32[48]{0:T(128)S(1)} all-reduce(f32[48]{0:T(128)S(1)} %multiply_reduce_fusion.8), channel_id=1, replica_groups=mesh['gx'=8,'gy'=4] {'gx','gy'}, use_global_device_ids=true, to_apply=%region_11.12 | all-reduce | flops 48 | bytes 384 | tf_op jit(solution)/shard_map/psum | solution.py:103
  246.2 5.7 multiply_reduce_fusion.7
  251.9 40.1 %psum.88 = f32[48]{0:T(128)S(1)} all-reduce(f32[48]{0:T(128)S(1)} %get-tuple-element.42), channel_id=1, replica_groups=mesh['gx'=8,'gy'=4] {'gx','gy'}, use_global_device_ids=true, to_apply=%region_13.14 | all-reduce | flops 48 | bytes 384 | tf_op jit(solution)/shard_map/psum | solution.py:76
  292.1 4.3 broadcast_multiply_fusion.3
  297.7 5.2 collective-permute-done.8
  304.6 2.7 copy.23
  312.7 5.7 add_reduce_fusion.7
  318.5 4.0 add_reduce_fusion.6
  330.7 4.7 collective-permute-start.10
  340.1 2.7 slice_add_fusion.3
  343.0 4.2 collective-permute-start.11
  350.4 40.4 %psum.89 = f32[48]{0:T(128)S(1)} all-reduce(f32[48]{0:T(128)S(1)} %multiply_reduce_fusion.6), channel_id=1, replica_groups=mesh['gx'=8,'gy'=4] {'gx','gy'}, use_global_device_ids=true, to_apply=%region_17.18 | all-reduce | flops 48 | bytes 384 | tf_op jit(solution)/shard_map/psum | solution.py:103
  390.8 5.7 multiply_reduce_fusion.5
  396.5 40.1 %psum.90 = f32[48]{0:T(128)S(1)} all-reduce(f32[48]{0:T(128)S(1)} %get-tuple-element.32), channel_id=1, replica_groups=mesh['gx'=8,'gy'=4] {'gx','gy'}, use_global_device_ids=true, to_apply=%region_19.20 | all-reduce | flops 48 | bytes 384 | tf_op jit(solution)/shard_map/psum | solution.py:76
  436.6 4.4 broadcast_multiply_fusion.2
  442.3 5.2 collective-permute-done.12
  457.3 5.7 add_reduce_fusion.5
  463.2 4.0 add_reduce_fusion.4
  475.4 4.7 collective-permute-start.14
  484.8 2.7 slice_add_fusion.2
  487.6 4.2 collective-permute-start.15
  495.0 40.2 %psum.91 = f32[48]{0:T(128)S(1)} all-reduce(f32[48]{0:T(128)S(1)} %multiply_reduce_fusion.4), channel_id=1, replica_groups=mesh['gx'=8,'gy'=4] {'gx','gy'}, use_global_device_ids=true, to_apply=%region_23.24 | all-reduce | flops 48 | bytes 384 | tf_op jit(solution)/shard_map/psum | solution.py:103
  535.2 5.7 multiply_reduce_fusion.3
  540.9 40.1 %psum.92 = f32[48]{0:T(128)S(1)} all-reduce(f32[48]{0:T(128)S(1)} %get-tuple-element.22), channel_id=1, replica_groups=mesh['gx'=8,'gy'=4] {'gx','gy'}, use_global_device_ids=true, to_apply=%region_25.26 | all-reduce | flops 48 | bytes 384 | tf_op jit(solution)/shard_map/psum | solution.py:76
  581.1 2.8 broadcast_multiply_fusion.1
  585.2 5.2 collective-permute-done.16
  600.2 7.3 add_reduce_fusion.3
  607.6 4.0 add_reduce_fusion.2
  623.0 4.9 collective-permute-start.18
  627.9 3.8 slice.401
  634.1 2.9 slice_add_fusion.1
  637.3 3.9 collective-permute-start.19
  644.5 40.0 %psum.93 = f32[48]{0:T(128)S(1)} all-reduce(f32[48]{0:T(128)S(1)} %multiply_reduce_fusion.2), channel_id=1, replica_groups=mesh['gx'=8,'gy'=4] {'gx','gy'}, use_global_device_ids=true, to_apply=%region_29.30 | all-reduce | flops 48 | bytes 384 | tf_op jit(solution)/shard_map/psum | solution.py:103
  684.4 5.7 multiply_reduce_fusion.1
  690.1 40.2 %psum.94 = f32[48]{0:T(128)S(1)} all-reduce(f32[48]{0:T(128)S(1)} %get-tuple-element.12), channel_id=1, replica_groups=mesh['gx'=8,'gy'=4] {'gx','gy'}, use_global_device_ids=true, to_apply=%region_31.32 | all-reduce | flops 48 | bytes 384 | tf_op jit(solution)/shard_map/psum | solution.py:76
  733.7 5.2 collective-permute-done.20
  740.5 2.8 copy.35
  748.8 5.7 add_reduce_fusion.1
  754.6 4.0 add_reduce_fusion
  766.9 4.7 collective-permute-start.22
  776.3 2.7 slice_add_fusion
  779.2 3.5 collective-permute-start.23
  784.8 3.1 multiply_reduce_fusion
  787.9 40.9 %psum.95 = f32[48]{0:T(128)S(1)} all-reduce(f32[48]{0:T(128)S(1)} %multiply_reduce_fusion), channel_id=1, replica_groups=mesh['gx'=8,'gy'=4] {'gx','gy'}, use_global_device_ids=true, to_apply=%region_35.36 | all-reduce | flops 48 | bytes 384 | tf_op jit(solution)/shard_map/psum | solution.py:103
  828.8 7.3 multiply_subtract_fusion
  (215 shorter events, 159.6 us)
Async XLA Ops:
  1.4 4.4 copy-start.36
  1.4 4.4 copy-start.35
  1.4 4.5 copy-start.37
  4.5 7.2 collective-permute-start
  13.4 4.0 copy-start.38
  16.1 3.2 collective-permute-start.1
  21.5 5.8 copy-start.29
  36.2 2.2 copy-start.23
  39.6 8.8 %collective-permute-start.2 = (f32[48,3,33,1]{0,2,3,1:T(8,128)S(1)}, f32[48,3,33,1]{0,2,3,1:T(8,128)S(1)}, u32[]{:S(2)}, u32[]{:S(2)}) collective-permute-start(f32[48,3,33,1]{0,2,3,1:T(8,128)S(1)} %copy.11), channel_id=1, source_target_pairs={{0,1},{1,2},{2,3},{4,5},{5,6},{6,7},{8,9},{9,10},{10,11},{12,13},{... | collective-permute-start | bytes 57032 | tf_op jit(solution)/shard_map/ppermute | solution.py:15
  49.2 2.4 copy-start.5
  51.6 6.7 copy-start.8
  51.6 4.7 copy-start
  51.7 6.5 collective-permute-start.3
  100.9 6.0 copy-start.39
  151.2 6.5 copy-start.18
  151.3 6.5 collective-permute-start.4
  159.4 8.3 copy-start.19
  162.2 3.2 collective-permute-start.5
  167.7 5.8 copy-start.30
  182.4 2.2 copy-start.24
  185.7 7.1 collective-permute-start.6
  197.8 7.1 copy-start.9
  197.9 7.0 copy-start.13
  198.0 6.9 collective-permute-start.7
  296.4 6.5 collective-permute-start.8
  307.2 3.2 collective-permute-start.9
  312.7 5.8 copy-start.31
  327.4 2.2 copy-start.25
  330.7 7.1 collective-permute-start.10
  342.9 6.4 copy-start.10
  343.0 6.3 copy-start.14
  343.0 6.2 collective-permute-start.11
  441.1 6.5 collective-permute-start.12
  451.9 3.2 collective-permute-start.13
  457.3 5.8 copy-start.32
  472.0 2.2 copy-start.26
  475.4 7.1 collective-permute-start.14
  487.5 6.4 copy-start.11
  487.6 6.3 copy-start.15
  487.6 6.2 collective-permute-start.15
  583.9 6.5 copy-start.20
  583.9 146.4 %copy-start.2 = (f32[48,3,32,128]{3,0,2,1:T(8,128)}, f32[48,3,32,128]{3,0,2,1:T(8,128)S(1)}, u32[]{:S(2)}) copy-start(f32[48,3,32,128]{3,0,2,1:T(8,128)S(1)} %get-tuple-element.21) | copy-start | bytes 7077892
  583.9 6.5 collective-permute-start.16
  594.7 3.2 collective-permute-start.17
  600.2 7.4 copy-start.21
  600.2 7.4 copy-start.33
  616.5 2.2 copy-start.27
  623.0 8.8 %collective-permute-start.18 = (f32[48,3,33,1]{0,2,3,1:T(8,128)S(1)}, f32[48,3,33,1]{0,2,3,1:T(8,128)S(1)}, u32[]{:S(2)}, u32[]{:S(2)}) collective-permute-start(f32[48,3,33,1]{0,2,3,1:T(8,128)S(1)} %copy.33), channel_id=1, source_target_pairs={{0,1},{1,2},{2,3},{4,5},{5,6},{6,7},{8,9},{9,10},{10,11},{12,13},{... | collective-permute-start | bytes 57032 | tf_op jit(solution)/shard_map/ppermute | solution.py:15
  634.1 3.1 copy-start.7
  637.2 6.1 copy-start.12
  637.3 5.9 collective-permute-start.19
  732.4 6.5 copy-start.16
  732.4 6.5 collective-permute-start.20
  740.5 8.3 copy-start.17
  743.3 3.2 collective-permute-start.21
  748.8 5.8 copy-start.34
  766.9 7.1 collective-permute-start.22
  774.0 10.7 %copy-start.4 = (f32[48,3,33,127]{3,0,2,1:T(8,128)}, f32[48,3,33,127]{3,0,2,1:T(8,128)S(1)}, u32[]{:S(2)}) copy-start(f32[48,3,33,127]{3,0,2,1:T(8,128)S(1)} %slice.407) | copy-start | bytes 7242052
  779.0 5.7 copy-start.6
  779.1 5.6 copy-start.3
  779.2 5.6 copy-start.22
  779.2 5.5 collective-permute-start.23
  784.8 44.1 %copy-start.1 = (f32[48,3,32,128]{3,2,1,0:T(8,128)S(1)}, f32[48,3,32,128]{3,2,1,0:T(8,128)}, u32[]{:S(2)}) copy-start(f32[48,3,32,128]{3,2,1,0:T(8,128)} %param.6) | copy-start | bytes 7077892
  784.8 44.0 %copy-start.40 = (f32[48]{0:T(128)S(1)}, f32[48]{0:T(128)}, u32[]{:S(2)}) copy-start(f32[48]{0:T(128)} %copy-done.39) | copy-start | bytes 580
  (1 other events, 2.2 us)
where the time goes:
time: 852 us; the launch traced here: 841 us
  blocking collectives  442 us (52%)
  other arithmetic  184 us (22%)
  local copies, waits for them, and re-layouts  88 us (10%)
  starting transfers between devices  70 us (8%)
  waiting for transfers between devices  53.8 us (6%)
    psum x6, blocking collectives, squares(): return lax.psum(inner(residual, residual), ('gx', 'gy'))  241 us
    psum x5, blocking collectives, body(): alpha = norm_now / lax.psum(inner(direction, image), ('gx', 'gy'))  202 us
    ppermute x24, starting transfers between devices, from_behind(): return lax.ppermute(block, axis, route)  70 us
    reduce_sum x12, other arithmetic, triangle(): jnp.sum(dir_one * edge_one + dir_two * edge_two, axis=-3, keepdims=True)  59.9 us
    ppermute x24, waiting for transfers between devices, from_behind(): return lax.ppermute(block, axis, route)  53.8 us
    reduce_sum x12, other arithmetic, inner(): return jnp.sum(left * right, axis=(1, 2, 3))  38.8 us
    ppermute x12, local copies, waits for them, and re-layouts, from_behind(): return lax.ppermute(block, axis, route)  26.3 us
    mul x6, other arithmetic, body(): masked = free * direction  21.4 us
  transfers between devices with their start and end apart: 24, of which 18 were waited for; matrix products, arithmetic and copies ran while one was open for 2% of the time, Pallas kernels for 0%

commit v1 on v0

v1 whole, which is shorter than its diff:
```python
import functools
import jax
import jax.numpy as jnp
from jax import lax
from jax.experimental import pallas as pl
from jax.experimental.pallas import tpu as pltpu
from jax.sharding import PartitionSpec as P

DAMP = 0.2
HALO = 6
TOP = 12
PITCH = 32
PER = 4
NCOEF = 20
F32 = jnp.float32


def two_sum(a, b):
    s = a + b
    t = s - a
    return s, (a - (s - t)) + (b - t)


def quick(a, b):
    s = a + b
    return s, b - (s - a)


def halves(a):
    t = 4097.0 * a
    high = t - (t - a)
    return high, a - high


def two_mul(a, b):
    p = a * b
    ah, al = halves(a)
    bh, bl = halves(b)
    return p, ((ah * bh - p) + ah * bl + al * bh) + al * bl


def dd_add(x, y):
    s, e = two_sum(x[0], y[0])
    return quick(s, e + (x[1] + y[1]))


def dd_neg(x):
    return -x[0], -x[1]


def dd_sub(x, y):
    return dd_add(x, dd_neg(y))


def dd_mul(x, y):
    p, e = two_mul(x[0], y[0])
    return quick(p, e + (x[0] * y[1] + x[1] * y[0]))


def dd_div(x, y):
    q = x[0] / y[0]
    p, e = two_mul(q, y[0])
    rest = ((x[0] - p) - e) + (x[1] - q * y[1])
    return quick(q, rest / y[0])


def lift(x):
    return x, jnp.zeros_like(x)


def dd_fma(x, a, y):
    return dd_sub(x, dd_mul(a, y))


def first_block(m):
    one = [dd_div(m[1], m[0])]
    a0 = one[0]
    s1 = {l: dd_fma(m[l + 1], a0, m[l]) for l in range(1, 5)}
    q1 = dd_div(s1[2], s1[1])
    a1 = dd_sub(q1, a0)
    b1 = dd_div(s1[1], m[0])
    s2 = {l: dd_fma(dd_fma(s1[l + 1], a1, s1[l]), b1, m[l]) for l in range(2, 4)}
    a2 = dd_sub(dd_div(s2[3], s2[2]), q1)
    b2 = dd_div(s2[2], s1[1])
    return (a0, a1, a2), (b1, b2), s2[2]


def second_block(nu, a, b, b3):
    a0, a1, a2 = a
    b1, b2 = b
    t2 = {1: nu[0]}
    t2[2] = dd_add(nu[1], dd_mul(a2, t2[1]))
    t12 = nu[0]
    t2[3] = dd_add(dd_add(nu[2], dd_mul(a2, t2[2])), dd_mul(b2, t12))
    t13 = dd_add(t2[2], dd_mul(a1, t12))
    t2[4] = dd_add(dd_add(nu[3], dd_mul(a2, t2[3])), dd_mul(b2, t13))
    a3 = dd_div(nu[1], nu[0])
    t4 = {j: dd_fma(dd_fma(nu[j + 1], a3, nu[j]), b3, t2[j]) for j in range(1, 5)}
    b4 = dd_div(t4[1], nu[0])
    q4 = dd_div(t4[2], t4[1])
    a4 = dd_sub(q4, a3)
    t5 = {j: dd_fma(dd_fma(t4[j + 1], a4, t4[j]), b4, nu[j]) for j in (2, 3)}
    b5 = dd_div(t5[2], t4[1])
    a5 = dd_sub(dd_div(t5[3], t5[2]), q4)
    return (a3, a4, a5), (b4, b5)


def steps_of(a, b, before):
    alphas, sigmas = [], []
    for ak, bk in zip(a, b):
        if before is None:
            alpha = 1.0 / (ak + DAMP)
            sigma = jnp.zeros_like(alpha)
        else:
            ratio = bk * before
            alpha = 1.0 / (ak + DAMP - ratio)
            sigma = alpha * ratio
        alphas.append(alpha)
        sigmas.append(sigma)
        before = alpha
    return alphas, sigmas


def early_residuals(alphas, sigmas):
    one = jnp.ones_like(alphas[0])
    zero = jnp.zeros_like(one)
    polys = [[one, zero, zero, zero]]
    pins = [one]
    for k in range(3):
        now = polys[-1]
        old = polys[-2] if k else [zero] * 4
        lead = 1.0 + sigmas[k] - DAMP * alphas[k]
        polys.append([
            lead * now[i] - (alphas[k] * now[i - 1] if i else zero) - sigmas[k] * old[i]
            for i in range(4)
        ])
        pins.append((1.0 + sigmas[k] - alphas[k]) * pins[-1] - (sigmas[k] * pins[-2] if k else zero))
    return polys, pins


PIN = 1.0 - DAMP


def with_pins(sums, weight):
    out = []
    factor = 1.0
    for k in range(6):
        out.append(dd_add(lift(sums[k]), dd_mul(lift(weight), lift(jnp.full_like(weight, factor)))))
        factor *= PIN
    return out


def row(ref, i):
    return ref[i:i + 1, :]


def middle_scalars(sums_ref, keep_ref):
    sums = [row(sums_ref, i) for i in range(7)]
    m = with_pins(sums, sums[6])
    a, b, top = first_block(m)
    alphas, sigmas = steps_of([x[0] for x in a], [None] + [x[0] for x in b], None)
    polys, pins = early_residuals(alphas, sigmas)
    lead = alphas[0] * alphas[1] * alphas[2]
    values = list(polys[3]) + [pins[3], pins[2]]
    values += [x for pair in a + b for x in pair]
    values += [top[0], sums[6]] + alphas + sigmas + [lead]
    for i, value in enumerate(values):
        keep_ref[i:i + 1, :] = value


def last_scalars(keep_ref, sums_ref, out_ref):
    kept = [row(keep_ref, i) for i in range(25)]
    pins = [kept[5], kept[4]]
    a = [(kept[6 + 2 * i], kept[7 + 2 * i]) for i in range(3)]
    b = [(kept[12 + 2 * i], kept[13 + 2 * i]) for i in range(2)]
    top, weight = kept[16], kept[17]
    alphas, sigmas = kept[18:21], kept[21:24]
    lead = kept[24]
    nu = with_pins([row(sums_ref, i) for i in range(6)], weight * kept[4] * kept[4])
    b3 = dd_div(nu[0], dd_mul(lift(top), dd_mul(lift(lead), lift(lead))))
    a_late, b_late = second_block(nu, a, b, b3)
    more, more_sigmas = steps_of(
        [x[0] for x in a_late], [b3[0]] + [x[0] for x in b_late], alphas[2]
    )
    alphas = alphas + more
    sigmas = sigmas + more_sigmas
    one = jnp.ones_like(top)
    zero = jnp.zeros_like(top)

    def unit(i):
        return [one if j == i else zero for j in range(7)]

    def scale(f, v):
        return [f * x for x in v]

    def plus(*vs):
        total = list(vs[0])
        for v in vs[1:]:
            total = [p + q for p, q in zip(total, v)]
        return total

    residuals = [unit(0), unit(1), unit(2), unit(3)]

    def times_h(v):
        out = [zero] * 7
        for k in range(3):
            image = scale((1.0 + sigmas[k]) / alphas[k] - DAMP, unit(k))
            image[k + 1] = image[k + 1] - 1.0 / alphas[k]
            if k:
                image[k - 1] = image[k - 1] - sigmas[k] / alphas[k]
            out = plus(out, scale(v[k], image))
        for k in range(3, 6):
            out[k + 1] = out[k + 1] + v[k]
        return out

    for k in range(3, 6):
        now, old = residuals[k], residuals[k - 1]
        residuals.append(plus(
            scale(1.0 + sigmas[k] - DAMP * alphas[k], now),
            scale(-alphas[k], times_h(now)),
            scale(-sigmas[k], old),
        ))
        pins.append((1.0 + sigmas[k] - alphas[k]) * pins[-1] - sigmas[k] * pins[-2])
    answers = [[zero] * 7, scale(alphas[0], unit(0))]
    for k in range(1, 6):
        answers.append(plus(
            scale(1.0 + sigmas[k], answers[k]), scale(alphas[k], residuals[k]), scale(-sigmas[k], answers[k - 1])
        ))
    polys, early = early_residuals(alphas[:3], sigmas[:3])
    pins_all = early[:3] + pins[1:]
    pin_answers = [zero, alphas[0]]
    for k in range(1, 6):
        pin_answers.append(
            (1.0 + sigmas[k]) * pin_answers[k] + alphas[k] * pins_all[k] - sigmas[k] * pin_answers[k - 1]
        )
    rows = []
    for v, pin in ((answers[6], pin_answers[6]), (residuals[6], pins_all[6])):
        for i in range(3):
            rows.append(v[0] * polys[0][i] + v[1] * polys[1][i] + v[2] * polys[2][i])
        rows += v[3:] + [pin]
    for i, value in enumerate(rows):
        out_ref[i:i + 1, :] = value


def lanes(rows=8):
    return lax.broadcasted_iota(jnp.int32, (rows, 128), 1)


def prepare_kernel(raw_ref, strip_ref, main_out, strip_out):
    height = raw_ref.shape[2]
    lane = lax.broadcasted_iota(jnp.int32, (height, 128), 1)
    line = lax.broadcasted_iota(jnp.int32, (height, 128), 0)
    near = None
    for which, (src, dst) in enumerate(((strip_ref, strip_out), (raw_ref, main_out))):
        def raw(i):
            return src[i // 3, i % 3]
        flipped = raw(16) > 0.5
        zero = jnp.zeros((height, 128), F32)
        k1, k2 = raw(0), raw(1)
        root1, root2 = jnp.sqrt(raw(2)), jnp.sqrt(raw(3))
        other = jnp.where(flipped, zero, k2)
        left = pltpu.roll(other, 1, 1)
        if which == 1:
            left = jnp.where(lane == 0, near, left)
        else:
            near = pltpu.roll(other, 128 - (HALO - 1), 1)
        below = jnp.where(line == 0, zero, pltpu.roll(other, 1, 0))
        dst[0] = k1 + left
        dst[1] = jnp.where(flipped, k2, k1) + below
        dst[2] = jnp.where(flipped, k1 + k2, zero)
        for c in range(3):
            dst[3 + c] = root1 * raw(4 + c)
            dst[6 + c] = root1 * raw(7 + c)
            one = root2 * raw(10 + c)
            two = root2 * raw(13 + c)
            dst[9 + c] = jnp.where(flipped, zero, two)
            dst[12 + c] = jnp.where(flipped, two, one)
            dst[15 + c] = jnp.where(flipped, one, -(one + two))
        dst[18] = raw(16)
        dst[19] = raw(17)


def dot3(p, q):
    return p[0] * q[0] + p[1] * q[1] + p[2] * q[2]


def tile_step(get, coef, beside, spill, put, put_spill, scratch, first, chunks):
    side, down_b, down_d = scratch
    stop = first + 8 * chunks
    for r in list(range(first, stop, 8)) + [stop - 7]:
        for c in range(3):
            side[c, r:r + 8, :] = beside(c, r, get(c, r))
    for r in range(first, stop, 8):
        def co(i):
            return coef[i, r:r + 8, :]
        flipped = co(18) > 0.5
        base = [get(c, r) for c in range(3)]
        eb = [get(c, r + 1) - base[c] for c in range(3)]
        ec = [side[c, r:r + 8, :] - base[c] for c in range(3)]
        ed = [side[c, r + 1:r + 9, :] - base[c] for c in range(3)]
        ex = [jnp.where(flipped, ed[c], ec[c]) for c in range(3)]
        g1 = [co(3 + c) for c in range(3)]
        g2 = [co(6 + c) for c in range(3)]
        hb = [co(9 + c) for c in range(3)]
        hc = [co(12 + c) for c in range(3)]
        hd = [co(15 + c) for c in range(3)]
        s1 = dot3(g1, eb) + dot3(g2, ex)
        s2 = dot3(hb, eb) + dot3(hc, ec) + dot3(hd, ed)
        zero = jnp.zeros_like(s1)
        s1c = jnp.where(flipped, zero, s1)
        s1d = jnp.where(flipped, s1, zero)
        wv, wh, wd, free = co(0), co(1), co(2), co(19)
        for c in range(3):
            fb = wv * eb[c] + s1 * g1[c] + s2 * hb[c]
            fc = wh * ec[c] + s1c * g2[c] + s2 * hc[c]
            fd = wd * ed[c] + s1d * g2[c] + s2 * hd[c]
            down_b[c, r:r + 8, :] = fb
            down_d[c, r:r + 8, :] = fd
            own = down_b[c, r - 1:r + 7, :] - (fb + fc + fd)
            q = fc + down_d[c, r - 1:r + 7, :]
            if put_spill is not None:
                put_spill(c, r, q)
            put(c, r, free * (own + spill(c, r, q)))


def apply_group(src_main, src_strip, dst_main, dst_strip, coef_main, coef_strip, scratch, first, chunks):
    side, down_b, down_d, strip_q = scratch
    buffers = (side, down_b, down_d)
    lane = lanes()

    def put_strip(c, r, x):
        if dst_strip is not None:
            dst_strip[c, r:r + 8, :] = x

    def put_q(c, r, x):
        strip_q[c, r:r + 8, :] = x

    tile_step(
        lambda c, r: src_strip[c, r:r + 8, :],
        coef_strip,
        lambda c, r, x: pltpu.roll(x, 127, 1),
        lambda c, r, x: pltpu.roll(x, 1, 1),
        put_strip,
        put_q,
        buffers, first, chunks,
    )

    def one(i, carry):
        base = 3 * i
        to_last = (127 - (PITCH * i + 21)) % 128
        to_first = (128 - (PITCH * i + HALO - 1)) % 128

        def beside(c, r, x):
            beyond = pltpu.roll(src_strip[c, r:r + 8, :], to_last, 1)
            return jnp.where(lane == 127, beyond, pltpu.roll(x, 127, 1))

        def spill(c, r, x):
            beyond = pltpu.roll(strip_q[c, r:r + 8, :], to_first, 1)
            return jnp.where(lane == 0, beyond, pltpu.roll(x, 1, 1))

        def put(c, r, x):
            dst_main[base + c, r:r + 8, :] = x

        tile_step(
            lambda c, r: src_main[base + c, r:r + 8, :],
            coef_main, beside, spill, put, None, buffers, first, chunks,
        )
        return carry

    for i in range(PER):
        one(i, 0)


def fold(x):
    return jnp.sum(x, axis=0, keepdims=True)


def inner(p_ref, q_ref, i, p_at, q_at, height):
    total = None
    for c in range(3):
        for r in range(0, height, 8):
            t = p_ref[3 * i + c, p_at + r:p_at + r + 8, :] * q_ref[3 * i + c, q_at + r:q_at + r + 8, :]
            total = t if total is None else total + t
    return fold(total)


def clear(scratch):
    for ref in scratch:
        ref[...] = jnp.zeros(ref.shape, F32)


def first_kernel(height, rhs_ref, u0, s0, cm, cs, u1, u2, u3, s1, s2, s3, sums_ref, side, down_b, down_d, strip_q):
    scratch = (side, down_b, down_d, strip_q)

    @pl.when(pl.program_id(0) == 0)
    def _():
        clear(scratch)

    sv = lambda ref: ref.at[0]
    apply_group(u0, sv(s0), u1, sv(s1), cm, cs, scratch, TOP - 6, (height + 16) // 8)
    apply_group(u1, sv(s1), u2, sv(s2), cm, cs, scratch, TOP - 5, (height + 16) // 8)
    apply_group(u2, sv(s2), u3, sv(s3), cm, cs, scratch, TOP - 4, (height + 8) // 8)
    chain = (u0, u1, u2, u3)
    for i in range(PER):
        rows = []
        for k in range(6):
            rows.append(inner(chain[k // 2], chain[(k + 1) // 2], i, TOP, TOP, height))
        total = None
        for c in range(3):
            for r in range(0, height, 8):
                t = rhs_ref[3 * i + c, r:r + 8, :] - u0[3 * i + c, TOP + r:TOP + r + 8, :]
                t = t * t
                total = t if total is None else total + t
        rows.append(fold(total))
        rows.append(jnp.zeros((1, 128), F32))
        for k in range(8):
            sums_ref[8 * i + k:8 * i + k + 1, :] = rows[k]


def spread(table, load, i):
    return jnp.broadcast_to(table[pl.ds(load, 1), i:i + 1], (8, 128))


def transposed(keep, square, table):
    square[...] = jnp.zeros((128, 128), F32)
    square[0:32, :] = keep[...]
    table[...] = square[...].T


def second_kernel(height, totals_ref, u0, u1, u2, u3, s0, s1, s2, s3, cm, cs,
                  o0, o1, o2, o3, sums_ref, keep_ref, side, down_b, down_d, strip_q,
                  square, table, w0, w1, w2, w3, t0, t1, t2):
    scratch = (side, down_b, down_d, strip_q)
    group = pl.program_id(0)

    @pl.when(group == 0)
    def _():
        clear(scratch)
        clear((w0, w1, w2, w3, t0, t1, t2))
        keep_ref[...] = jnp.zeros(keep_ref.shape, F32)
        middle_scalars(totals_ref, keep_ref)
        transposed(keep_ref, square, table)

    chunks = (height + 8) // 8
    window = range(TOP - 4, TOP - 4 + 8 * chunks, 8)
    segment = lanes() // PITCH
    weights = [[spread(table, group * PER + i, j) for j in range(4)] for i in range(PER)]
    for i in range(PER):
        for c in range(3):
            for r in window:
                w0[3 * i + c, r:r + 8, :] = (
                    weights[i][0] * u0[3 * i + c, r:r + 8, :] + weights[i][1] * u1[3 * i + c, r:r + 8, :]
                    + weights[i][2] * u2[3 * i + c, r:r + 8, :] + weights[i][3] * u3[3 * i + c, r:r + 8, :]
                )
    mixed = []
    for j in range(4):
        m = weights[0][j]
        for i in range(1, PER):
            m = jnp.where(segment == i, weights[i][j], m)
        mixed.append(m)
    for c in range(3):
        for r in window:
            t0[c, r:r + 8, :] = (
                mixed[0] * s0[0, c, r:r + 8, :] + mixed[1] * s1[0, c, r:r + 8, :]
                + mixed[2] * s2[0, c, r:r + 8, :] + mixed[3] * s3[0, c, r:r + 8, :]
            )
    apply_group(w0, t0, w1, t1, cm, cs, scratch, TOP - 4, chunks)
    apply_group(w1, t1, w2, t2, cm, cs, scratch, TOP - 4, chunks)
    apply_group(w2, t2, w3, None, cm, cs, scratch, TOP - 4, chunks)
    chain = (w0, w1, w2, w3)
    for i in range(PER):
        for k in range(6):
            sums_ref[8 * i + k:8 * i + k + 1, :] = inner(chain[k // 2], chain[(k + 1) // 2], i, TOP, TOP, height)
        sums_ref[8 * i + 6:8 * i + 8, :] = jnp.zeros((2, 128), F32)
        for src, dst in zip(chain, (o0, o1, o2, o3)):
            for c in range(3):
                dst[3 * i + c, :, :] = src[3 * i + c, TOP:TOP + height, :]


def last_kernel(height, totals_ref, keep_ref, rhs_ref, u0, u1, u2, w0, w1, w2, w3, x_ref, r_ref, rows, square, table):
    group = pl.program_id(0)

    @pl.when(group == 0)
    def _():
        rows[...] = jnp.zeros(rows.shape, F32)
        last_scalars(keep_ref, totals_ref, rows)
        transposed(rows, square, table)

    for i in range(PER):
        f = [spread(table, group * PER + i, j) for j in range(16)]
        for c in range(3):
            k = 3 * i + c
            for r in range(0, height, 8):
                own = [ref[k, TOP + r:TOP + r + 8, :] for ref in (u0, u1, u2)]
                late = [ref[k, r:r + 8, :] for ref in (w0, w1, w2, w3)]
                pin = rhs_ref[k, r:r + 8, :] - own[0]
                vectors = own + late + [pin]
                for out, at in ((x_ref, 0), (r_ref, 8)):
                    total = f[at] * vectors[0]
                    for j in range(1, 8):
                        total = total + f[at + j] * vectors[j]
                    out[k, r:r + 8, :] = total


def pack_kernel(height, ext, data_ref, up_ref, down_ref, free_ref, u_ref, own_ref, right_ref, left_ref):
    q = pl.program_id(1)
    lane = lanes() % PITCH
    segment = lanes() // PITCH

    @pl.when(q == 0)
    def _():
        right_ref[...] = jnp.zeros(right_ref.shape, F32)
        left_ref[...] = jnp.zeros(left_ref.shape, F32)

    own_ref[...] = jnp.zeros(own_ref.shape, F32)
    for i in range(PER):
        for c in range(3):
            k = 3 * i + c
            u_ref[k, 0:8, :] = jnp.zeros((8, 128), F32)
            u_ref[k, ext - 8:ext, :] = jnp.zeros((8, 128), F32)
            u_ref[k, TOP:TOP + height, :] = data_ref[k, :, :]
            u_ref[k, TOP - HALO:TOP, :] = down_ref[k * HALO:(k + 1) * HALO, :]
            u_ref[k, TOP + height:TOP + height + HALO, :] = up_ref[k * HALO:(k + 1) * HALO, :]
            for r in range(0, ext, 8):
                x = u_ref[k, r:r + 8, :] * free_ref[0, r:r + 8, :]
                u_ref[k, r:r + 8, :] = x
                here = segment == i
                own = own_ref[0, c, r:r + 8, :]
                own = jnp.where(here & (lane >= 6) & (lane < 12), pltpu.roll(x, PITCH * i + 6, 1), own)
                own = jnp.where(here & (lane >= 16) & (lane < 21), pltpu.roll(x, (PITCH * i + 16 - 123) % 128, 1), own)
                own_ref[0, c, r:r + 8, :] = own
                spot = here & (lane >= 8 * q) & (lane < 8 * q + HALO)
                right_ref[0, c, r:r + 8, :] = jnp.where(
                    spot, pltpu.roll(x, (PITCH * i + 8 * q + HALO) % 128, 1), right_ref[0, c, r:r + 8, :])
                left_ref[0, c, r:r + 8, :] = jnp.where(
                    spot, pltpu.roll(x, (PITCH * i + 8 * q) % 128, 1), left_ref[0, c, r:r + 8, :])


def join_kernel(ext, own_ref, from_left_ref, from_right_ref, s_ref):
    q = pl.program_id(0) % 4
    lane = lanes() % PITCH
    for c in range(3):
        for r in range(0, ext, 8):
            x = own_ref[0, c, r:r + 8, :]
            x = jnp.where(lane < HALO, pltpu.roll(from_left_ref[0, c, r:r + 8, :], (128 - 8 * q) % 128, 1), x)
            x = jnp.where(
                (lane >= 21) & (lane < 21 + HALO),
                pltpu.roll(from_right_ref[0, c, r:r + 8, :], (128 + 21 - 8 * q) % 128, 1), x)
            s_ref[0, c, r:r + 8, :] = x


def moved(block, axis, distance):
    n = lax.axis_size(axis)
    return lax.ppermute(block, axis, [(i, i + distance) for i in range(n) if 0 <= i + distance < n])


def summed(x):
    for axis in ("gy", "gx"):
        n = lax.axis_size(axis)
        d = 1
        while d < n:
            x = x + lax.ppermute(x, axis, [(i, i ^ d) for i in range(n)])
            d *= 2
    return x


def totals_of(sums, loads):
    return summed(jnp.pad(jnp.sum(sums.reshape(loads, 8, 128), axis=-1).T, [(0, 0), (0, 128 - loads)]))


def params(limit=48):
    return pltpu.CompilerParams(vmem_limit_bytes=limit * 2**20)


def shape(*dims):
    return jax.ShapeDtypeStruct(dims, F32)


def body(rhs, stiffness, coupling, edges, flip, pinned):
    loads, _, height, width = rhs.shape
    ext = height + 24
    groups = loads // PER
    free = (1 - pinned).astype(F32)[None]
    raw = jnp.concatenate([stiffness, coupling, edges, flip.astype(F32)[None], free], axis=0)
    raw = raw.reshape(6, 3, height, width)
    main = rhs.reshape(loads * 3, height, width)
    both = jnp.concatenate([rhs, raw], axis=0)
    count = (loads + 6) * 3
    up = moved(both[:, :, :HALO, :].reshape(count * HALO, width), "gx", -1)
    down = moved(both[:, :, height - HALO:, :].reshape(count * HALO, width), "gx", 1)
    cut = loads * 3 * HALO

    def rows_of_params(x):
        x = x[cut:].reshape(6, 1, 3, HALO, width)
        return jnp.broadcast_to(x, (6, PER, 3, HALO, width)).reshape(-1, width)

    free_ext = jnp.concatenate([
        jnp.zeros((TOP - HALO, width), F32), down[-HALO:], raw[5, 2], up[-HALO:], jnp.zeros((TOP - HALO, width), F32)
    ], axis=0)
    ones = jnp.ones((ext, width), F32)
    masks = jnp.stack([free_ext, ones])
    raw_wide = jnp.broadcast_to(raw[:, None], (6, PER, 3, height, width)).reshape(6 * PER * 3, height, width)

    def pack(data, up_rows, down_rows, mask):
        n = data.shape[0] // (3 * PER)
        merged = (n + 3) // 4
        last = n - 1
        return pl.pallas_call(
            functools.partial(pack_kernel, height, ext),
            grid=(merged, 4),
            in_specs=[
                pl.BlockSpec((3 * PER, height, width), lambda h, q: (jnp.minimum(4 * h + q, last), 0, 0)),
                pl.BlockSpec((3 * PER * HALO, width), lambda h, q: (jnp.minimum(4 * h + q, last), 0)),
                pl.BlockSpec((3 * PER * HALO, width), lambda h, q: (jnp.minimum(4 * h + q, last), 0)),
                pl.BlockSpec((1, ext, width), lambda h, q: (0, 0, 0)),
            ],
            out_specs=[
                pl.BlockSpec((3 * PER, ext, width), lambda h, q: (jnp.minimum(4 * h + q, last), 0, 0)),
                pl.BlockSpec((1, 3, ext, width), lambda h, q: (jnp.minimum(4 * h + q, last), 0, 0, 0)),
                pl.BlockSpec((1, 3, ext, width), lambda h, q: (h, 0, 0, 0)),
                pl.BlockSpec((1, 3, ext, width), lambda h, q: (h, 0, 0, 0)),
            ],
            out_shape=[
                shape(n * 3 * PER, ext, width), shape(n, 3, ext, width),
                shape(merged, 3, ext, width), shape(merged, 3, ext, width),
            ],
            compiler_params=params(),
        )(data, up_rows, down_rows, mask)

    u0, own, to_right, to_left = pack(main, up[:cut], down[:cut], masks[:1])
    p0, p_own, p_right, p_left = pack(raw_wide, rows_of_params(up), rows_of_params(down), masks[1:])
    m = to_right.shape[0]
    all_left = moved(jnp.concatenate([to_right, p_right]), "gy", 1)
    all_right = moved(jnp.concatenate([to_left, p_left]), "gy", -1)

    def join(own_part, from_left, from_right):
        n = own_part.shape[0]
        block = pl.BlockSpec((1, 3, ext, width), lambda g: (g, 0, 0, 0))
        quarter = pl.BlockSpec((1, 3, ext, width), lambda g: (g // 4, 0, 0, 0))
        return pl.pallas_call(
            functools.partial(join_kernel, ext),
            grid=(n,),
            in_specs=[block, quarter, quarter],
            out_specs=block,
            out_shape=shape(n, 3, ext, width),
            compiler_params=params(),
        )(own_part, from_left, from_right)

    s0 = join(own, all_left[:m], all_right[:m])
    p_strip = join(p_own, all_left[m:], all_right[m:])
    p_main = p0.reshape(6, PER, 3, ext, width)[:, 0]
    cm, cs = pl.pallas_call(
        prepare_kernel,
        out_shape=[shape(NCOEF, ext, width), shape(NCOEF, ext, width)],
        compiler_params=params(),
    )(p_main, p_strip)

    tile = pl.BlockSpec((3 * PER, ext, width), lambda g: (g, 0, 0))
    own_tile = pl.BlockSpec((3 * PER, height, width), lambda g: (g, 0, 0))
    strip = pl.BlockSpec((1, 3, ext, width), lambda g: (g, 0, 0, 0))
    table = pl.BlockSpec((NCOEF, ext, width), lambda g: (0, 0, 0))
    part = pl.BlockSpec((8 * PER, width), lambda g: (g, 0))
    tile_shape = shape(loads * 3, ext, width)
    own_shape = shape(loads * 3, height, width)
    strip_shape = shape(groups, 3, ext, width)
    sums_shape = shape(8 * loads, width)
    small = [pltpu.VMEM((3, ext, width), F32)] * 4
    u1, u2, u3, s1, s2, s3, sums = pl.pallas_call(
        functools.partial(first_kernel, height),
        grid=(groups,),
        in_specs=[own_tile, tile, strip, table, table],
        out_specs=[tile] * 3 + [strip] * 3 + [part],
        out_shape=[tile_shape] * 3 + [strip_shape] * 3 + [sums_shape],
        scratch_shapes=small,
        compiler_params=params(),
    )(main, u0, s0, cm, cs)
    totals = totals_of(sums, loads)
    fixed = pl.BlockSpec((8, 128), lambda g: (0, 0))
    kept = pl.BlockSpec((32, 128), lambda g: (0, 0))
    w0, w1, w2, w3, sums, keep = pl.pallas_call(
        functools.partial(second_kernel, height),
        grid=(groups,),
        in_specs=[fixed] + [tile] * 4 + [strip] * 4 + [table] * 2,
        out_specs=[own_tile] * 4 + [part, kept],
        out_shape=[own_shape] * 4 + [sums_shape, shape(32, 128)],
        scratch_shapes=small + [pltpu.VMEM((128, 128), F32)] * 2
        + [pltpu.VMEM((3 * PER, ext, width), F32)] * 4 + [pltpu.VMEM((3, ext, width), F32)] * 3,
        compiler_params=params(),
    )(totals, u0, u1, u2, u3, s0, s1, s2, s3, cm, cs)
    totals = totals_of(sums, loads)
    x, r = pl.pallas_call(
        functools.partial(last_kernel, height),
        grid=(groups,),
        in_specs=[fixed, kept, own_tile] + [tile] * 3 + [own_tile] * 4,
        out_specs=[own_tile] * 2,
        out_shape=[own_shape] * 2,
        scratch_shapes=[pltpu.VMEM((32, 128), F32), pltpu.VMEM((128, 128), F32), pltpu.VMEM((128, 128), F32)],
        compiler_params=params(),
    )(totals, keep, main, u0, u1, u2, w0, w1, w2, w3)
    return x.reshape(rhs.shape), r.reshape(rhs.shape)


def solution(mesh):
    placed = (
        P(None, None, "gx", "gy"),
        P(None, "gx", "gy"),
        P(None, "gx", "gy"),
        P(None, "gx", "gy"),
        P("gx", "gy"),
        P("gx", "gy"),
    )
    return jax.shard_map(
        body,
        mesh=mesh,
        in_specs=placed,
        out_specs=(P(None, None, "gx", "gy"), P(None, None, "gx", "gy")),
        check_vma=False,
    )
```

time: 852 us -> 182 us (0.21); the launches traced: 841 us -> 181 us
  blocking collectives: 442 us -> 0 us
  other arithmetic: 184 us -> 4.09 us
  Pallas kernels: 0 us -> 90 us
  local copies, waits for them, and re-layouts: 88 us -> 14.7 us
  starting transfers between devices: 70 us -> 33.7 us
  waiting for transfers between devices: 53.8 us -> 37.6 us
    psum x11 -> x0, blocking collectives: 442 us -> none  [the longest x6 241 us: squares(): return lax.psum(inner(residual, residual), ('gx', 'gy'))]
    reduce_sum x24 -> x2, other arithmetic: 98.7 us -> 1.21 us  [totals_of(): jnp.sum(sums.reshape(loads, 8, 128), axis=-1)]
    pallas_call x0 -> x8, Pallas kernels: none -> 90 us  [the longest x1 31.8 us: body(): pl.pallas_call(functools.partial(second_kernel, height), grid=(groups,),...]
    add x24 -> x10, other arithmetic: 45.1 us -> 0.04 us  [summed(): x = x + lax.ppermute(x, axis, [(i, i ^ d) for i in range(n)])]
    slice x31 -> x10, local copies, waits for them, and re-layouts: 43.8 us -> 0.14 us  [the longest x2 0.06 us: body(): u0, own, to_right, to_left = pack(main, up[:cut], down[:cut], masks[:1])]
    ppermute x24 -> x14, starting transfers between devices: 70 us -> 33.7 us  [the longest x10 22.6 us: summed(): x = x + lax.ppermute(x, axis, [(i, i ^ d) for i in range(n)])]
    ppermute x12 -> x0, local copies, waits for them, and re-layouts: 26.3 us -> none  [from_behind(): return lax.ppermute(block, axis, route)]
    mul x17 -> x0, other arithmetic: 22.1 us -> none  [the longest x6 21.4 us: body(): masked = free * direction]
  transfers between devices with their start and end apart: 24 -> 14, of which waited for: 18 -> 13; matrix products, arithmetic and copies ran while one was open for 2% -> 0% of each run, Pallas kernels for 0% -> 0%
where the time goes in v1:
time: 182 us; the launch traced here: 181 us
  Pallas kernels  90 us (49%)
  waiting for transfers between devices  37.6 us (21%)
  starting transfers between devices  33.7 us (19%)
  local copies, waits for them, and re-layouts  14.7 us (8%)
  other arithmetic  4.09 us (2%)
    pallas_call x1, Pallas kernels, body(): pl.pallas_call(functools.partial(second_kernel, height), grid=(groups,),...  31.8 us
    pallas_call x1, Pallas kernels, body(): pl.pallas_call(functools.partial(first_kernel, height), grid=(groups,), i...  31.4 us
    ppermute x10, starting transfers between devices, summed(): x = x + lax.ppermute(x, axis, [(i, i ^ d) for i in range(n)])  22.6 us
    ppermute x4, waiting for transfers between devices, moved(): lax.ppermute(block, axis, [(i, i + distance) for i in range(n) if 0 <= i...  21.4 us
    ppermute x10, waiting for transfers between devices, summed(): x = x + lax.ppermute(x, axis, [(i, i ^ d) for i in range(n)])  16.2 us
    unnamed x31, local copies, waits for them, and re-layouts  13.5 us
    pallas_call x1, Pallas kernels, body(): pl.pallas_call(functools.partial(last_kernel, height), grid=(groups,), in...  13.1 us
    pallas_call x2, Pallas kernels, pack(): pl.pallas_call(functools.partial(pack_kernel, height, ext), grid=(merged,...  11.2 us
  transfers between devices with their start and end apart: 14, of which 13 were waited for; matrix products, arithmetic and copies ran while one was open for 0% of the time, Pallas kernels for 0%

profile of v1, /device:TPU:0, one launch (start us, length us, event | category | flops | bytes accessed | tf_op | source)
XLA Modules:
  0.0 181.1 jit_solution(1024060327308118847)
XLA Ops:
  0.6 0.8 constant_dynamic-update-slice_fusion.2
  1.4 0.8 constant_dynamic-update-slice_fusion.1
  2.2 0.9 constant_dynamic-update-slice_fusion
  3.1 0.7 bitcast_dynamic-update-slice_fusion.1
  3.8 0.7 bitcast_dynamic-update-slice_fusion
  4.5 1.3 pad_maximum_fusion
  5.9 0.1 reshape.45
  5.9 1.3 collective-permute-start
  7.2 0.1 reshape.46
  7.3 5.5 %collective-permute-start.1 = (f32[972,128]{1,0:T(8,128)S(1)}, f32[972,128]{1,0:T(8,128)S(1)}, u32[]{:S(2)}, u32[]{:S(2)}) collective-permute-start(f32[972,128]{1,0:T(8,128)S(1)} %reshape.46), channel_id=1, source_target_pairs={{0,4},{4,8},{8,12},{12,16},{16,20},{20,24},{24,28},{1,5},{5,9},{9,... | collective-permute-start | bytes 1493000 | tf_op jit(solution)/shard_map/ppermute | solution.py:554
  12.8 9.3 %collective-permute-done = f32[972,128]{1,0:T(8,128)S(1)} collective-permute-done((f32[972,128]{1,0:T(8,128)S(1)}, f32[972,128]{1,0:T(8,128)S(1)}, u32[]{:S(2)}, u32[]{:S(2)}) %collective-permute-start) | collective-permute-done | bytes 497696 | tf_op jit(solution)/shard_map/ppermute | solution.py:554
  22.3 10.8 %collective-permute-done.1 = f32[972,128]{1,0:T(8,128)S(1)} collective-permute-done((f32[972,128]{1,0:T(8,128)S(1)}, f32[972,128]{1,0:T(8,128)S(1)}, u32[]{:S(2)}, u32[]{:S(2)}) %collective-permute-start.1) | collective-permute-done | bytes 497696 | tf_op jit(solution)/shard_map/ppermute | solution.py:554
  33.2 0.3 concatenate.17
  33.5 0.0 copy-start
  33.5 0.1 broadcast_in_dim.27
  33.7 4.2 %shard_map.78 = (f32[72,56,128]{2,1,0:T(8,128)S(1)}, f32[6,3,56,128]{3,2,1,0:T(8,128)S(1)}, f32[2,3,56,128]{3,2,1,0:T(8,128)S(1)}, f32[2,3,56,128]{3,2,1,0:T(8,128)S(1)}) custom-call(f32[72,32,128]{2,1,0:T(8,128)S(1)} %bitcast.22, f32[432,128]{1,0:T(8,128)S(1)} %reshape.48.up_ref, f32[432,128]{1,0:T(8,128)S(1)} %reshape.49.down_ref, ...), custom_call_target="tpu_custom_call" | custom-call | tf_op jit(solution)/shard_map/pallas_call | solution.py:608
  37.9 7.1 %shard_map.77 = (f32[144,56,128]{2,1,0:T(8,128)}, f32[12,3,56,128]{3,2,1,0:T(8,128)S(1)}, f32[3,3,56,128]{3,2,1,0:T(8,128)S(1)}, f32[3,3,56,128]{3,2,1,0:T(8,128)S(1)}) custom-call(f32[144,32,128]{2,1,0:T(8,128)S(1)} %bitcast.20, f32[864,128]{1,0:T(8,128)S(1)} %slice.56.up_ref, f32[864,128]{1,0:T(8,128)S(1)} %slice.57.down_ref, f32[1,56,128]{2,1,0:T(8,128)S(1)} %bitcast.24), custom_call_target="tpu_custom_call" | custom-call | tf_op jit(solution)/shard_map/pallas_call | solution.py:608
  45.0 1.3 collective-permute-start.3
  46.3 3.1 %collective-permute-start.2 = (f32[5,3,56,128]{3,2,1,0:T(8,128)S(1)}, f32[5,3,56,128]{3,2,1,0:T(8,128)S(1)}, u32[]{:S(2)}, u32[]{:S(2)}) collective-permute-start(f32[5,3,56,128]{3,2,1,0:T(8,128)S(1)} %pad_maximum_fusion.2), channel_id=1, source_target_pairs={{0,1},{1,2},{2,3},{4,5},{5,6},{6,7},{8,9},{9,10},{10,11},{12,13},{... | collective-permute-start | bytes 1290248 | tf_op jit(solution)/shard_map/ppermute | solution.py:554
  49.5 0.0 collective-permute-done.3
  49.5 1.3 collective-permute-done.2
  50.8 0.8 shard_map.80.strip_ref
  51.6 0.1 shard_map.81
  51.8 1.5 shard_map.79.s0
  53.3 31.4 %shard_map.82 = (f32[144,56,128]{2,1,0:T(8,128)}, f32[144,56,128]{2,1,0:T(8,128)}, f32[144,56,128]{2,1,0:T(8,128)}, f32[12,3,56,128]{3,2,1,0:T(8,128)S(1)}, f32[...) custom-call(f32[144,32,128]{2,1,0:T(8,128)} %bitcast.19, ...), custom_call_target="tpu_custom_call" | custom-call | tf_op jit(solution)/shard_map/pallas_call | solution.py:668
  84.7 0.0 copy-start.7
  84.7 1.0 copy-done.7
  85.7 1.0 copy-done.9
  86.6 1.0 copy-done.11
  87.6 0.1 reduce_sum.22
  87.8 0.1 reduce_sum.23
  87.9 0.1 copy.9
  87.9 5.0 %collective-permute-start.4 = (f32[8,128]{1,0:T(8,128)S(1)}, f32[8,128]{1,0:T(8,128)S(1)}, u32[]{:S(2)}, u32[]{:S(2)}) collective-permute-start(f32[8,128]{1,0:T(8,128)S(1)} %pad.7), channel_id=1, source_target_pairs={{0,1},{1,0},{2,3},{3,2},{4,5},{5,4},{6,7},{7,6},{8,9},{9,8},{10,11... | collective-permute-start | bytes 12296 | tf_op jit(solution)/shard_map/ppermute | solution.py:562
  92.9 0.8 collective-permute-done.4
  93.7 2.7 %collective-permute-start.5 = (f32[8,128]{1,0:T(8,128)S(1)}, f32[8,128]{1,0:T(8,128)S(1)}, u32[]{:S(2)}, u32[]{:S(2)}) collective-permute-start(f32[8,128]{1,0:T(8,128)S(1)} %pad_add_fusion.1), channel_id=1, source_target_pairs={{0,2},{1,3},{2,0},{3,1},{4,6},{5,7},{6,4},{7,5},{8,10},{9,11},{10,... | collective-permute-start | bytes 12296 | tf_op jit(solution)/shard_map/ppermute | solution.py:562
  96.4 1.6 collective-permute-done.5
  98.0 2.5 %collective-permute-start.6 = (f32[8,128]{1,0:T(8,128)S(1)}, f32[8,128]{1,0:T(8,128)S(1)}, u32[]{:S(2)}, u32[]{:S(2)}) collective-permute-start(f32[8,128]{1,0:T(8,128)S(1)} %add.35), channel_id=1, source_target_pairs={{0,4},{4,0},{8,12},{12,8},{16,20},{20,16},{24,28},{28,24},{1,5},{5... | collective-permute-start | bytes 12296 | tf_op jit(solution)/shard_map/ppermute | solution.py:562
  100.5 1.6 collective-permute-done.6
  102.1 1.6 collective-permute-start.7
  103.7 2.0 %collective-permute-done.7 = f32[8,128]{1,0:T(8,128)S(1)} collective-permute-done((f32[8,128]{1,0:T(8,128)S(1)}, f32[8,128]{1,0:T(8,128)S(1)}, u32[]{:S(2)}, u32[]{:S(2)}) %collective-permute-start.7) | collective-permute-done | bytes 4128 | tf_op jit(solution)/shard_map/ppermute | solution.py:562
  105.7 2.6 %collective-permute-start.8 = (f32[8,128]{1,0:T(8,128)S(1)}, f32[8,128]{1,0:T(8,128)S(1)}, u32[]{:S(2)}, u32[]{:S(2)}) collective-permute-start(f32[8,128]{1,0:T(8,128)S(1)} %add.37), channel_id=1, source_target_pairs={{0,16},{4,20},{8,24},{12,28},{16,0},{20,4},{24,8},{28,12},{1,17},{... | collective-permute-start | bytes 12296 | tf_op jit(solution)/shard_map/ppermute | solution.py:562
  108.3 1.9 %collective-permute-done.8 = f32[8,128]{1,0:T(8,128)S(1)} collective-permute-done((f32[8,128]{1,0:T(8,128)S(1)}, f32[8,128]{1,0:T(8,128)S(1)}, u32[]{:S(2)}, u32[]{:S(2)}) %collective-permute-start.8) | collective-permute-done | bytes 4128 | tf_op jit(solution)/shard_map/ppermute | solution.py:562
  110.2 1.1 copy-done.4
  111.3 1.1 copy-done.6
  112.4 1.2 copy-done.8
  113.6 1.2 copy-done.10
  114.8 1.2 copy-done.12
  116.0 31.8 %shard_map.83 = (f32[144,32,128]{2,1,0:T(8,128)}, f32[144,32,128]{2,1,0:T(8,128)}, f32[144,32,128]{2,1,0:T(8,128)}, f32[144,32,128]{2,1,0:T(8,128)}, f32[384,128]{1,0:T(8,128)S(1)}, /*index=5*/f32[32,128]{1,0:T(8,128)S(1)}) custom-call(f32[8,128]{1,0:T(8,128)S(1)} %add.38.totals_ref, f32[144,56,128]{2,1,0:T(8,128)} %get-tuple-element.27.u0, ...), custom_call_target="tpu_custom_call" | custom-call | tf_op jit(solution)/shard_map/pallas_call | solution.py:680
  147.9 0.7 copy-done.13
  148.5 1.1 reduce_sum.24
  149.6 0.1 reduce_sum.25
  149.7 0.1 copy.10
  149.8 0.0 collective-permute-start.9
  149.8 1.2 collective-permute-done.9
  151.0 2.0 %collective-permute-start.10 = (f32[8,128]{1,0:T(8,128)S(1)}, f32[8,128]{1,0:T(8,128)S(1)}, u32[]{:S(2)}, u32[]{:S(2)}) collective-permute-start(f32[8,128]{1,0:T(8,128)S(1)} %pad_add_fusion), channel_id=1, source_target_pairs={{0,2},{1,3},{2,0},{3,1},{4,6},{5,7},{6,4},{7,5},{8,10},{9,11},{10,... | collective-permute-start | bytes 12296 | tf_op jit(solution)/shard_map/ppermute | solution.py:562
  153.0 1.6 collective-permute-done.10
  154.6 2.0 %collective-permute-start.11 = (f32[8,128]{1,0:T(8,128)S(1)}, f32[8,128]{1,0:T(8,128)S(1)}, u32[]{:S(2)}, u32[]{:S(2)}) collective-permute-start(f32[8,128]{1,0:T(8,128)S(1)} %add.40), channel_id=1, source_target_pairs={{0,4},{4,0},{8,12},{12,8},{16,20},{20,16},{24,28},{28,24},{1,5},{5... | collective-permute-start | bytes 12296 | tf_op jit(solution)/shard_map/ppermute | solution.py:562
  156.6 1.6 collective-permute-done.11
  158.2 1.6 collective-permute-start.12
  159.8 2.0 %collective-permute-done.12 = f32[8,128]{1,0:T(8,128)S(1)} collective-permute-done((f32[8,128]{1,0:T(8,128)S(1)}, f32[8,128]{1,0:T(8,128)S(1)}, u32[]{:S(2)}, u32[]{:S(2)}) %collective-permute-start.12) | collective-permute-done | bytes 4128 | tf_op jit(solution)/shard_map/ppermute | solution.py:562
  161.8 2.6 %collective-permute-start.13 = (f32[8,128]{1,0:T(8,128)S(1)}, f32[8,128]{1,0:T(8,128)S(1)}, u32[]{:S(2)}, u32[]{:S(2)}) collective-permute-start(f32[8,128]{1,0:T(8,128)S(1)} %add.42), channel_id=1, source_target_pairs={{0,16},{4,20},{8,24},{12,28},{16,0},{20,4},{24,8},{28,12},{1,17},{... | collective-permute-start | bytes 12296 | tf_op jit(solution)/shard_map/ppermute | solution.py:562
  164.4 1.9 %collective-permute-done.13 = f32[8,128]{1,0:T(8,128)S(1)} collective-permute-done((f32[8,128]{1,0:T(8,128)S(1)}, f32[8,128]{1,0:T(8,128)S(1)}, u32[]{:S(2)}, u32[]{:S(2)}) %collective-permute-start.13) | collective-permute-done | bytes 4128 | tf_op jit(solution)/shard_map/ppermute | solution.py:562
  166.3 1.7 copy-done.2
  168.0 13.1 %shard_map.84 = (f32[144,32,128]{2,1,0:T(8,128)}, f32[144,32,128]{2,1,0:T(8,128)}) custom-call(f32[8,128]{1,0:T(8,128)S(1)} %add.43.totals_ref, f32[32,128]{1,0:T(8,128)S(1)} %get-tuple-element.45.keep_ref, f32[144,32,128]{2,1,0:T(8,128)S(1)} %bitcast.21, f32[144,56,128]{2,1,0:T(8,128)} %get-tuple-element.27.u0, f32[144,56,128]{2,1,0:T(8,128)} %get-tuple-element.38.u1, ...), custom_call_target="tpu_custom_call" | custom-call | tf_op jit(solution)/shard_map/pallas_call | solution.py:691
  (50 shorter events, 0.4 us)
Async XLA Ops:
  5.9 16.2 %collective-permute-start = (f32[972,128]{1,0:T(8,128)S(1)}, f32[972,128]{1,0:T(8,128)S(1)}, u32[]{:S(2)}, u32[]{:S(2)}) collective-permute-start(f32[972,128]{1,0:T(8,128)S(1)} %reshape.45), channel_id=1, source_target_pairs={{4,0},{8,4},{12,8},{16,12},{20,16},{24,20},{28,24},{5,1},{9,5},{13... | collective-permute-start | bytes 1493000 | tf_op jit(solution)/shard_map/ppermute | solution.py:554
  7.3 25.7 %collective-permute-start.1 = (f32[972,128]{1,0:T(8,128)S(1)}, f32[972,128]{1,0:T(8,128)S(1)}, u32[]{:S(2)}, u32[]{:S(2)}) collective-permute-start(f32[972,128]{1,0:T(8,128)S(1)} %reshape.46), channel_id=1, source_target_pairs={{0,4},{4,8},{8,12},{12,16},{16,20},{20,24},{24,28},{1,5},{5,9},{9,... | collective-permute-start | bytes 1493000 | tf_op jit(solution)/shard_map/ppermute | solution.py:554
  33.5 4.4 %copy-start = (f32[48,3,32,128]{3,2,1,0:T(8,128)S(1)}, f32[48,3,32,128]{3,2,1,0:T(8,128)}, u32[]{:S(2)}) copy-start(f32[48,3,32,128]{3,2,1,0:T(8,128)} %param.6) | copy-start | bytes 7077892
  45.0 4.5 %collective-permute-start.3 = (f32[5,3,56,128]{3,2,1,0:T(8,128)S(1)}, f32[5,3,56,128]{3,2,1,0:T(8,128)S(1)}, u32[]{:S(2)}, u32[]{:S(2)}) collective-permute-start(f32[5,3,56,128]{3,2,1,0:T(8,128)S(1)} %pad_maximum_fusion.3), channel_id=1, source_target_pairs={{1,0},{2,1},{3,2},{5,4},{6,5},{7,6},{9,8},{10,9},{11,10},{13,12},{... | collective-permute-start | bytes 1290248 | tf_op jit(solution)/shard_map/ppermute | solution.py:554
  46.3 4.4 %collective-permute-start.2 = (f32[5,3,56,128]{3,2,1,0:T(8,128)S(1)}, f32[5,3,56,128]{3,2,1,0:T(8,128)S(1)}, u32[]{:S(2)}, u32[]{:S(2)}) collective-permute-start(f32[5,3,56,128]{3,2,1,0:T(8,128)S(1)} %pad_maximum_fusion.2), channel_id=1, source_target_pairs={{0,1},{1,2},{2,3},{4,5},{5,6},{6,7},{8,9},{9,10},{10,11},{12,13},{... | collective-permute-start | bytes 1290248 | tf_op jit(solution)/shard_map/ppermute | solution.py:554
  51.7 33.0 %copy-start.3 = (f32[20,56,128]{2,1,0:T(8,128)}, f32[20,56,128]{2,1,0:T(8,128)S(1)}, u32[]{:S(2)}) copy-start(f32[20,56,128]{2,1,0:T(8,128)S(1)} %get-tuple-element.35.cm) | copy-start | bytes 1720324
  51.7 33.0 %copy-start.5 = (f32[20,56,128]{2,1,0:T(8,128)}, f32[20,56,128]{2,1,0:T(8,128)S(1)}, u32[]{:S(2)}) copy-start(f32[20,56,128]{2,1,0:T(8,128)S(1)} %get-tuple-element.36.cs) | copy-start | bytes 1720324
  84.7 1.0 copy-start.7
  85.7 1.0 copy-start.9
  86.6 1.0 copy-start.11
  87.9 5.8 %collective-permute-start.4 = (f32[8,128]{1,0:T(8,128)S(1)}, f32[8,128]{1,0:T(8,128)S(1)}, u32[]{:S(2)}, u32[]{:S(2)}) collective-permute-start(f32[8,128]{1,0:T(8,128)S(1)} %pad.7), channel_id=1, source_target_pairs={{0,1},{1,0},{2,3},{3,2},{4,5},{5,4},{6,7},{7,6},{8,9},{9,8},{10,11... | collective-permute-start | bytes 12296 | tf_op jit(solution)/shard_map/ppermute | solution.py:562
  93.7 4.3 %collective-permute-start.5 = (f32[8,128]{1,0:T(8,128)S(1)}, f32[8,128]{1,0:T(8,128)S(1)}, u32[]{:S(2)}, u32[]{:S(2)}) collective-permute-start(f32[8,128]{1,0:T(8,128)S(1)} %pad_add_fusion.1), channel_id=1, source_target_pairs={{0,2},{1,3},{2,0},{3,1},{4,6},{5,7},{6,4},{7,5},{8,10},{9,11},{10,... | collective-permute-start | bytes 12296 | tf_op jit(solution)/shard_map/ppermute | solution.py:562
  98.0 4.1 %collective-permute-start.6 = (f32[8,128]{1,0:T(8,128)S(1)}, f32[8,128]{1,0:T(8,128)S(1)}, u32[]{:S(2)}, u32[]{:S(2)}) collective-permute-start(f32[8,128]{1,0:T(8,128)S(1)} %add.35), channel_id=1, source_target_pairs={{0,4},{4,0},{8,12},{12,8},{16,20},{20,16},{24,28},{28,24},{1,5},{5... | collective-permute-start | bytes 12296 | tf_op jit(solution)/shard_map/ppermute | solution.py:562
  102.1 3.6 %collective-permute-start.7 = (f32[8,128]{1,0:T(8,128)S(1)}, f32[8,128]{1,0:T(8,128)S(1)}, u32[]{:S(2)}, u32[]{:S(2)}) collective-permute-start(f32[8,128]{1,0:T(8,128)S(1)} %add.36), channel_id=1, source_target_pairs={{0,8},{4,12},{8,0},{12,4},{16,24},{20,28},{24,16},{28,20},{1,9},{5... | collective-permute-start | bytes 12296 | tf_op jit(solution)/shard_map/ppermute | solution.py:562
  105.7 4.5 %collective-permute-start.8 = (f32[8,128]{1,0:T(8,128)S(1)}, f32[8,128]{1,0:T(8,128)S(1)}, u32[]{:S(2)}, u32[]{:S(2)}) collective-permute-start(f32[8,128]{1,0:T(8,128)S(1)} %add.37), channel_id=1, source_target_pairs={{0,16},{4,20},{8,24},{12,28},{16,0},{20,4},{24,8},{28,12},{1,17},{... | collective-permute-start | bytes 12296 | tf_op jit(solution)/shard_map/ppermute | solution.py:562
  110.2 1.1 copy-start.4
  111.3 1.1 copy-start.6
  112.3 1.2 copy-start.8
  113.6 1.2 copy-start.10
  114.8 1.2 copy-start.12
  116.0 50.3 %copy-start.1 = (f32[48,3,32,128]{3,2,1,0:T(8,128)S(1)}, f32[48,3,32,128]{3,2,1,0:T(8,128)}, u32[]{:S(2)}) copy-start(f32[48,3,32,128]{3,2,1,0:T(8,128)} %param.6) | copy-start | bytes 7077892
  147.9 0.7 copy-start.13
  149.8 1.2 collective-permute-start.9
  151.0 3.6 %collective-permute-start.10 = (f32[8,128]{1,0:T(8,128)S(1)}, f32[8,128]{1,0:T(8,128)S(1)}, u32[]{:S(2)}, u32[]{:S(2)}) collective-permute-start(f32[8,128]{1,0:T(8,128)S(1)} %pad_add_fusion), channel_id=1, source_target_pairs={{0,2},{1,3},{2,0},{3,1},{4,6},{5,7},{6,4},{7,5},{8,10},{9,11},{10,... | collective-permute-start | bytes 12296 | tf_op jit(solution)/shard_map/ppermute | solution.py:562
  154.6 3.6 %collective-permute-start.11 = (f32[8,128]{1,0:T(8,128)S(1)}, f32[8,128]{1,0:T(8,128)S(1)}, u32[]{:S(2)}, u32[]{:S(2)}) collective-permute-start(f32[8,128]{1,0:T(8,128)S(1)} %add.40), channel_id=1, source_target_pairs={{0,4},{4,0},{8,12},{12,8},{16,20},{20,16},{24,28},{28,24},{1,5},{5... | collective-permute-start | bytes 12296 | tf_op jit(solution)/shard_map/ppermute | solution.py:562
  158.2 3.6 %collective-permute-start.12 = (f32[8,128]{1,0:T(8,128)S(1)}, f32[8,128]{1,0:T(8,128)S(1)}, u32[]{:S(2)}, u32[]{:S(2)}) collective-permute-start(f32[8,128]{1,0:T(8,128)S(1)} %add.41), channel_id=1, source_target_pairs={{0,8},{4,12},{8,0},{12,4},{16,24},{20,28},{24,16},{28,20},{1,9},{5... | collective-permute-start | bytes 12296 | tf_op jit(solution)/shard_map/ppermute | solution.py:562
  161.8 4.5 %collective-permute-start.13 = (f32[8,128]{1,0:T(8,128)S(1)}, f32[8,128]{1,0:T(8,128)S(1)}, u32[]{:S(2)}, u32[]{:S(2)}) collective-permute-start(f32[8,128]{1,0:T(8,128)S(1)} %add.42), channel_id=1, source_target_pairs={{0,16},{4,20},{8,24},{12,28},{16,0},{20,4},{24,8},{28,12},{1,17},{... | collective-permute-start | bytes 12296 | tf_op jit(solution)/shard_map/ppermute | solution.py:562
  166.3 1.7 copy-start.2

commit v2 on v1

v2 whole, which is shorter than its diff:
```python
import functools
import jax
import jax.numpy as jnp
from jax import lax
from jax.experimental import pallas as pl
from jax.experimental.pallas import tpu as pltpu
from jax.sharding import PartitionSpec as P

DAMP = 0.2
HALO = 6
TOP = 12
PITCH = 32
PER = 4
NCOEF = 20
PAIR = 2
F32 = jnp.float32


def two_sum(a, b):
    s = a + b
    t = s - a
    return s, (a - (s - t)) + (b - t)


def quick(a, b):
    s = a + b
    return s, b - (s - a)


def halves(a):
    t = 4097.0 * a
    high = t - (t - a)
    return high, a - high


def two_mul(a, b):
    p = a * b
    ah, al = halves(a)
    bh, bl = halves(b)
    return p, ((ah * bh - p) + ah * bl + al * bh) + al * bl


def dd_add(x, y):
    s, e = two_sum(x[0], y[0])
    return quick(s, e + (x[1] + y[1]))


def dd_neg(x):
    return -x[0], -x[1]


def dd_sub(x, y):
    return dd_add(x, dd_neg(y))


def dd_mul(x, y):
    p, e = two_mul(x[0], y[0])
    return quick(p, e + (x[0] * y[1] + x[1] * y[0]))


def dd_div(x, y):
    q = x[0] / y[0]
    p, e = two_mul(q, y[0])
    rest = ((x[0] - p) - e) + (x[1] - q * y[1])
    return quick(q, rest / y[0])


def lift(x):
    return x, jnp.zeros_like(x)


def dd_fma(x, a, y):
    return dd_sub(x, dd_mul(a, y))


def first_block(m):
    one = [dd_div(m[1], m[0])]
    a0 = one[0]
    s1 = {l: dd_fma(m[l + 1], a0, m[l]) for l in range(1, 5)}
    q1 = dd_div(s1[2], s1[1])
    a1 = dd_sub(q1, a0)
    b1 = dd_div(s1[1], m[0])
    s2 = {l: dd_fma(dd_fma(s1[l + 1], a1, s1[l]), b1, m[l]) for l in range(2, 4)}
    a2 = dd_sub(dd_div(s2[3], s2[2]), q1)
    b2 = dd_div(s2[2], s1[1])
    return (a0, a1, a2), (b1, b2), s2[2]


def second_block(nu, a, b, b3):
    a0, a1, a2 = a
    b1, b2 = b
    t2 = {1: nu[0]}
    t2[2] = dd_add(nu[1], dd_mul(a2, t2[1]))
    t12 = nu[0]
    t2[3] = dd_add(dd_add(nu[2], dd_mul(a2, t2[2])), dd_mul(b2, t12))
    t13 = dd_add(t2[2], dd_mul(a1, t12))
    t2[4] = dd_add(dd_add(nu[3], dd_mul(a2, t2[3])), dd_mul(b2, t13))
    a3 = dd_div(nu[1], nu[0])
    t4 = {j: dd_fma(dd_fma(nu[j + 1], a3, nu[j]), b3, t2[j]) for j in range(1, 5)}
    b4 = dd_div(t4[1], nu[0])
    q4 = dd_div(t4[2], t4[1])
    a4 = dd_sub(q4, a3)
    t5 = {j: dd_fma(dd_fma(t4[j + 1], a4, t4[j]), b4, nu[j]) for j in (2, 3)}
    b5 = dd_div(t5[2], t4[1])
    a5 = dd_sub(dd_div(t5[3], t5[2]), q4)
    return (a3, a4, a5), (b4, b5)


def steps_of(a, b, before):
    alphas, sigmas = [], []
    for ak, bk in zip(a, b):
        if before is None:
            alpha = 1.0 / (ak + DAMP)
            sigma = jnp.zeros_like(alpha)
        else:
            ratio = bk * before
            alpha = 1.0 / (ak + DAMP - ratio)
            sigma = alpha * ratio
        alphas.append(alpha)
        sigmas.append(sigma)
        before = alpha
    return alphas, sigmas


def early_residuals(alphas, sigmas):
    one = jnp.ones_like(alphas[0])
    zero = jnp.zeros_like(one)
    polys = [[one, zero, zero, zero]]
    pins = [one]
    for k in range(3):
        now = polys[-1]
        old = polys[-2] if k else [zero] * 4
        lead = 1.0 + sigmas[k] - DAMP * alphas[k]
        polys.append([
            lead * now[i] - (alphas[k] * now[i - 1] if i else zero) - sigmas[k] * old[i]
            for i in range(4)
        ])
        pins.append((1.0 + sigmas[k] - alphas[k]) * pins[-1] - (sigmas[k] * pins[-2] if k else zero))
    return polys, pins


PIN = 1.0 - DAMP


def with_pins(sums, weight):
    out = []
    factor = 1.0
    for k in range(6):
        out.append(dd_add(sums[k], dd_mul(weight, lift(jnp.full_like(weight[0], factor)))))
        factor *= PIN
    return out


def row(ref, i):
    return ref[i:i + 1, :]


def middle_scalars(sums_ref, keep_ref):
    sums = [(row(sums_ref, i), row(sums_ref, 8 + i)) for i in range(7)]
    m = with_pins(sums, sums[6])
    a, b, top = first_block(m)
    alphas, sigmas = steps_of([x[0] for x in a], [None] + [x[0] for x in b], None)
    polys, pins = early_residuals(alphas, sigmas)
    lead = alphas[0] * alphas[1] * alphas[2]
    values = list(polys[3]) + [pins[3], pins[2]]
    values += [x for pair in a + b for x in pair]
    values += [top[0], sums[6][0]] + alphas + sigmas + [lead]
    for i, value in enumerate(values):
        keep_ref[i:i + 1, :] = value


def last_scalars(keep_ref, sums_ref, out_ref):
    kept = [row(keep_ref, i) for i in range(25)]
    pins = [kept[5], kept[4]]
    a = [(kept[6 + 2 * i], kept[7 + 2 * i]) for i in range(3)]
    b = [(kept[12 + 2 * i], kept[13 + 2 * i]) for i in range(2)]
    top, weight = kept[16], kept[17]
    alphas, sigmas = kept[18:21], kept[21:24]
    lead = kept[24]
    nu = with_pins([(row(sums_ref, i), row(sums_ref, 8 + i)) for i in range(6)], lift(weight * kept[4] * kept[4]))
    b3 = dd_div(nu[0], dd_mul(lift(top), dd_mul(lift(lead), lift(lead))))
    a_late, b_late = second_block(nu, a, b, b3)
    more, more_sigmas = steps_of(
        [x[0] for x in a_late], [b3[0]] + [x[0] for x in b_late], alphas[2]
    )
    alphas = alphas + more
    sigmas = sigmas + more_sigmas
    one = jnp.ones_like(top)
    zero = jnp.zeros_like(top)

    def unit(i):
        return [one if j == i else zero for j in range(7)]

    def scale(f, v):
        return [f * x for x in v]

    def plus(*vs):
        total = list(vs[0])
        for v in vs[1:]:
            total = [p + q for p, q in zip(total, v)]
        return total

    residuals = [unit(0), unit(1), unit(2), unit(3)]

    def times_h(v):
        out = [zero] * 7
        for k in range(3):
            image = scale((1.0 + sigmas[k]) / alphas[k] - DAMP, unit(k))
            image[k + 1] = image[k + 1] - 1.0 / alphas[k]
            if k:
                image[k - 1] = image[k - 1] - sigmas[k] / alphas[k]
            out = plus(out, scale(v[k], image))
        for k in range(3, 6):
            out[k + 1] = out[k + 1] + v[k]
        return out

    for k in range(3, 6):
        now, old = residuals[k], residuals[k - 1]
        residuals.append(plus(
            scale(1.0 + sigmas[k] - DAMP * alphas[k], now),
            scale(-alphas[k], times_h(now)),
            scale(-sigmas[k], old),
        ))
        pins.append((1.0 + sigmas[k] - alphas[k]) * pins[-1] - sigmas[k] * pins[-2])
    answers = [[zero] * 7, scale(alphas[0], unit(0))]
    for k in range(1, 6):
        answers.append(plus(
            scale(1.0 + sigmas[k], answers[k]), scale(alphas[k], residuals[k]), scale(-sigmas[k], answers[k - 1])
        ))
    polys, early = early_residuals(alphas[:3], sigmas[:3])
    pins_all = early[:3] + pins[1:]
    pin_answers = [zero, alphas[0]]
    for k in range(1, 6):
        pin_answers.append(
            (1.0 + sigmas[k]) * pin_answers[k] + alphas[k] * pins_all[k] - sigmas[k] * pin_answers[k - 1]
        )
    rows = []
    for v, pin in ((answers[6], pin_answers[6]), (residuals[6], pins_all[6])):
        for i in range(3):
            rows.append(v[0] * polys[0][i] + v[1] * polys[1][i] + v[2] * polys[2][i])
        rows += v[3:] + [pin]
    for i, value in enumerate(rows):
        out_ref[i:i + 1, :] = value


def lanes(rows=8):
    return lax.broadcasted_iota(jnp.int32, (rows, 128), 1)


def field(refs, i, rows):
    stiffness, coupling, edges, flip, pinned = refs
    if i < 2:
        return stiffness[i, rows, :]
    if i < 4:
        return coupling[i - 2, rows, :]
    if i < 16:
        return edges[i - 4, rows, :]
    if i == 16:
        return flip[rows, :].astype(F32)
    return (1 - pinned[rows, :]).astype(F32)


def join_rows(dst, lead, own, up, down, height):
    ext = dst.shape[-2]
    dst[lead + (slice(0, 8),)] = jnp.zeros((8, 128), F32)
    dst[lead + (slice(ext - 8, ext),)] = jnp.zeros((8, 128), F32)
    dst[lead + (slice(TOP, TOP + height),)] = own
    dst[lead + (slice(TOP - HALO, TOP),)] = down
    dst[lead + (slice(TOP + height, TOP + height + HALO),)] = up


def own_columns(x, i, kept):
    lane = lanes() % PITCH
    here = lanes() // PITCH == i
    kept = jnp.where(here & (lane >= 6) & (lane < 12), pltpu.roll(x, PITCH * i + 6, 1), kept)
    return jnp.where(here & (lane >= 16) & (lane < 21), pltpu.roll(x, (PITCH * i + 16 - 123) % 128, 1), kept)


def other_columns(left, right, q, kept):
    lane = lanes() % PITCH
    kept = jnp.where(lane < HALO, pltpu.roll(left, (128 - 8 * q) % 128, 1), kept)
    return jnp.where(
        (lane >= 21) & (lane < 21 + HALO), pltpu.roll(right, (128 + 21 - 8 * q) % 128, 1), kept)


def join_sides(sides, column, lead, merged, corners, height):
    for n in range(2):
        join_rows(sides, (n, column), merged[n][lead + (slice(None),)], corners[n][lead + (slice(8, 8 + HALO),)],
                  corners[n][lead + (slice(0, HALO),)], height)


def prepare_kernel(loads, merged, stiffness, coupling, edges, flip, pinned, up_ref, down_ref, left_ref, right_ref, left_ends, right_ends,
                   main_out, strip_out, wide, strip, sides):
    refs = (stiffness, coupling, edges, flip, pinned)
    height = flip.shape[0]
    ext = wide.shape[2]
    for p in range(6):
        for c in range(3):
            k = 3 * (loads + p) + c
            join_rows(wide, (p, c), field(refs, 3 * p + c, slice(0, height)), up_ref[k * HALO:(k + 1) * HALO, :],
                      down_ref[k * HALO:(k + 1) * HALO, :], height)
            join_sides(sides, c, (merged + p // 4, c), (left_ref, right_ref), (left_ends, right_ends), height)
            for r in range(0, ext, 8):
                x = wide[p, c, r:r + 8, :]
                total = jnp.zeros((8, 128), F32)
                for i in range(PER):
                    total = own_columns(x, i, total)
                strip[p, c, r:r + 8, :] = other_columns(
                    sides[0, c, r:r + 8, :], sides[1, c, r:r + 8, :], p % 4, total)
    lane = lax.broadcasted_iota(jnp.int32, (ext, 128), 1)
    line = lax.broadcasted_iota(jnp.int32, (ext, 128), 0)
    near = None
    for which, (src, dst) in enumerate(((strip, strip_out), (wide, main_out))):
        def raw(i):
            return src[i // 3, i % 3]
        flipped = raw(16) > 0.5
        zero = jnp.zeros((ext, 128), F32)
        k1, k2 = raw(0), raw(1)
        root1, root2 = jnp.sqrt(raw(2)), jnp.sqrt(raw(3))
        other = jnp.where(flipped, zero, k2)
        left = pltpu.roll(other, 1, 1)
        if which == 1:
            left = jnp.where(lane == 0, near, left)
        else:
            near = pltpu.roll(other, 128 - (HALO - 1), 1)
        below = jnp.where(line == 0, zero, pltpu.roll(other, 1, 0))
        dst[0] = k1 + left
        dst[1] = jnp.where(flipped, k2, k1) + below
        dst[2] = jnp.where(flipped, k1 + k2, zero)
        for c in range(3):
            dst[3 + c] = root1 * raw(4 + c)
            dst[6 + c] = root1 * raw(7 + c)
            one = root2 * raw(10 + c)
            two = root2 * raw(13 + c)
            dst[9 + c] = jnp.where(flipped, zero, two)
            dst[12 + c] = jnp.where(flipped, two, one)
            dst[15 + c] = jnp.where(flipped, one, -(one + two))
        dst[18] = raw(16)
        dst[19] = raw(17)


def dot3(p, q):
    return p[0] * q[0] + p[1] * q[1] + p[2] * q[2]


def tile_step(tiles, coef, first, chunks):
    stop = first + 8 * chunks
    for r in list(range(first, stop, 8)) + [stop - 7]:
        for side, get, beside, _, _, _ in tiles:
            for c in range(3):
                side[c, r:r + 8, :] = beside(c, r, get(c, r))
    top = lax.broadcasted_iota(jnp.int32, (8, 128), 0) == 0
    before = [None] * len(tiles)
    for r in range(first, stop, 8):
        def co(i):
            return coef[i, r:r + 8, :]
        flipped = co(18) > 0.5
        g1 = [co(3 + c) for c in range(3)]
        g2 = [co(6 + c) for c in range(3)]
        hb = [co(9 + c) for c in range(3)]
        hc = [co(12 + c) for c in range(3)]
        hd = [co(15 + c) for c in range(3)]
        wv, wh, wd, free = co(0), co(1), co(2), co(19)
        forces = []
        for side, get, _, _, _, _ in tiles:
            base = [get(c, r) for c in range(3)]
            eb = [get(c, r + 1) - base[c] for c in range(3)]
            ec = [side[c, r:r + 8, :] - base[c] for c in range(3)]
            ed = [side[c, r + 1:r + 9, :] - base[c] for c in range(3)]
            ex = [jnp.where(flipped, ed[c], ec[c]) for c in range(3)]
            s1 = dot3(g1, eb) + dot3(g2, ex)
            s2 = dot3(hb, eb) + dot3(hc, ec) + dot3(hd, ed)
            zero = jnp.zeros_like(s1)
            s1c = jnp.where(flipped, zero, s1)
            s1d = jnp.where(flipped, s1, zero)
            forces.append([(
                wv * eb[c] + s1 * g1[c] + s2 * hb[c],
                wh * ec[c] + s1c * g2[c] + s2 * hc[c],
                wd * ed[c] + s1d * g2[c] + s2 * hd[c],
            ) for c in range(3)])
        for n, (_, _, _, spill, put, put_spill) in enumerate(tiles):
            rolled = []
            for c in range(3):
                fb, fc, fd = forces[n][c]
                down_b, down_d = pltpu.roll(fb, 1, 0), pltpu.roll(fd, 1, 0)
                rolled.append((down_b, down_d))
                if before[n] is not None:
                    down_b = jnp.where(top, before[n][c][0], down_b)
                    down_d = jnp.where(top, before[n][c][1], down_d)
                own = down_b - (fb + fc + fd)
                q = fc + down_d
                if put_spill is not None:
                    put_spill(c, r, q)
                put(c, r, free * (own + spill(c, r, q)))
            before[n] = rolled


def apply_group(src_main, src_strip, dst_main, dst_strip, coef_main, coef_strip, scratch, first, chunks):
    side, strip_q = scratch
    lane = lanes()

    def put_strip(c, r, x):
        if dst_strip is not None:
            dst_strip[c, r:r + 8, :] = x

    def put_q(c, r, x):
        strip_q[c, r:r + 8, :] = x

    tile_step([(
        side.at[0],
        lambda c, r: src_strip[c, r:r + 8, :],
        lambda c, r, x: pltpu.roll(x, 127, 1),
        lambda c, r, x: pltpu.roll(x, 1, 1),
        put_strip,
        put_q,
    )], coef_strip, first, chunks)

    def tile(i, slot):
        base = 3 * i
        to_last = (127 - (PITCH * i + 21)) % 128
        to_first = (128 - (PITCH * i + HALO - 1)) % 128

        def get(c, r):
            return src_main[base + c, r:r + 8, :]

        def beside(c, r, x):
            beyond = pltpu.roll(src_strip[c, r:r + 8, :], to_last, 1)
            return jnp.where(lane == 127, beyond, pltpu.roll(x, 127, 1))

        def spill(c, r, x):
            beyond = pltpu.roll(strip_q[c, r:r + 8, :], to_first, 1)
            return jnp.where(lane == 0, beyond, pltpu.roll(x, 1, 1))

        def put(c, r, x):
            dst_main[base + c, r:r + 8, :] = x

        return side.at[slot], get, beside, spill, put, None

    for i in range(0, PER, PAIR):
        tile_step([tile(i + n, n) for n in range(PAIR)], coef_main, first, chunks)


def add_up(sums, totals_ref):
    totals_ref[...] = jnp.zeros(totals_ref.shape, F32)
    for k in range(7):
        totals_ref[k:k + 1, :] = jnp.sum(sums[k].T, axis=0, keepdims=True)


def fold(x):
    return jnp.sum(x, axis=0, keepdims=True)


def inner(p_ref, q_ref, i, p_at, q_at, height):
    total = None
    for c in range(3):
        for r in range(0, height, 8):
            t = p_ref[3 * i + c, p_at + r:p_at + r + 8, :] * q_ref[3 * i + c, q_at + r:q_at + r + 8, :]
            total = t if total is None else total + t
    return fold(total)


def clear(scratch):
    for ref in scratch:
        ref[...] = jnp.zeros(ref.shape, F32)


def first_kernel(height, rhs_ref, up_ref, down_ref, left_ref, right_ref, left_ends, right_ends, cm, cs,
                 u0_all, u1_all, u2_all, u3_all, s0_all, s1_all, s2_all, s3_all, totals_out, side, strip_q, sides, sums):
    scratch = (side, strip_q)
    group = pl.program_id(0)
    ext = cm.shape[1]

    @pl.when(group == 0)
    def _():
        clear(scratch)
        clear((sums,))

    mine = pl.ds(group * 3 * PER, 3 * PER)
    u0, u1, u2, u3 = (ref.at[mine] for ref in (u0_all, u1_all, u2_all, u3_all))
    s0, s1, s2, s3 = (ref.at[group] for ref in (s0_all, s1_all, s2_all, s3_all))
    q = group % 4
    for c in range(3):
        join_sides(sides, c, (0, c), (left_ref, right_ref), (left_ends, right_ends), height)
        for i in range(PER):
            k = 3 * i + c
            join_rows(u0, (k,), rhs_ref[k, :, :], up_ref[k * HALO:(k + 1) * HALO, :],
                      down_ref[k * HALO:(k + 1) * HALO, :], height)
        for r in range(0, ext, 8):
            total = jnp.zeros((8, 128), F32)
            for i in range(PER):
                x = u0[3 * i + c, r:r + 8, :] * cm[19, r:r + 8, :]
                u0[3 * i + c, r:r + 8, :] = x
                total = own_columns(x, i, total)
            total = other_columns(sides[0, c, r:r + 8, :], sides[1, c, r:r + 8, :], q, total)
            s0[c, r:r + 8, :] = total * cs[19, r:r + 8, :]
    apply_group(u0, s0, u1, s1, cm, cs, scratch, TOP - 6, (height + 16) // 8)
    apply_group(u1, s1, u2, s2, cm, cs, scratch, TOP - 5, (height + 16) // 8)
    apply_group(u2, s2, u3, s3, cm, cs, scratch, TOP - 4, (height + 8) // 8)
    chain = (u0, u1, u2, u3)
    for i in range(PER):
        rows = []
        for k in range(6):
            rows.append(inner(chain[k // 2], chain[(k + 1) // 2], i, TOP, TOP, height))
        total = None
        for c in range(3):
            for r in range(0, height, 8):
                t = rhs_ref[3 * i + c, r:r + 8, :] - u0[3 * i + c, TOP + r:TOP + r + 8, :]
                t = t * t
                total = t if total is None else total + t
        rows.append(fold(total))
        for k in range(7):
            sums[k, pl.ds(group * PER + i, 1), :] = rows[k]

    @pl.when(group == pl.num_programs(0) - 1)
    def _():
        add_up(sums, totals_out)


def spread(table, load, i):
    return jnp.broadcast_to(table[pl.ds(load, 1), i:i + 1], (8, 128))


def transposed(keep, square, table):
    square[...] = jnp.zeros((128, 128), F32)
    square[0:32, :] = keep[...]
    table[...] = square[...].T


def second_kernel(height, totals_ref, u0_all, u1_all, u2_all, u3_all, s0_all, s1_all, s2_all, s3_all, cm, cs,
                  w0_all, w1_all, w2_all, w3_all, totals_out, keep_ref, side, strip_q, square, table, t0, t1, t2, sums):
    scratch = (side, strip_q)
    group = pl.program_id(0)

    @pl.when(group == 0)
    def _():
        clear(scratch)
        clear((sums,))
        keep_ref[...] = jnp.zeros(keep_ref.shape, F32)
        middle_scalars(totals_ref, keep_ref)
        transposed(keep_ref, square, table)

    mine = pl.ds(group * 3 * PER, 3 * PER)
    u0, u1, u2, u3 = (ref.at[mine] for ref in (u0_all, u1_all, u2_all, u3_all))
    w0, w1, w2, w3 = (ref.at[mine] for ref in (w0_all, w1_all, w2_all, w3_all))
    s0, s1, s2, s3 = (ref.at[group] for ref in (s0_all, s1_all, s2_all, s3_all))
    chunks = (height + 8) // 8
    window = range(TOP - 4, TOP - 4 + 8 * chunks, 8)
    segment = lanes() // PITCH
    weights = [[spread(table, group * PER + i, j) for j in range(4)] for i in range(PER)]
    for i in range(PER):
        for c in range(3):
            for r in window:
                w0[3 * i + c, r:r + 8, :] = (
                    weights[i][0] * u0[3 * i + c, r:r + 8, :] + weights[i][1] * u1[3 * i + c, r:r + 8, :]
                    + weights[i][2] * u2[3 * i + c, r:r + 8, :] + weights[i][3] * u3[3 * i + c, r:r + 8, :]
                )
    mixed = []
    for j in range(4):
        m = weights[0][j]
        for i in range(1, PER):
            m = jnp.where(segment == i, weights[i][j], m)
        mixed.append(m)
    for c in range(3):
        for r in window:
            t0[c, r:r + 8, :] = (
                mixed[0] * s0[c, r:r + 8, :] + mixed[1] * s1[c, r:r + 8, :]
                + mixed[2] * s2[c, r:r + 8, :] + mixed[3] * s3[c, r:r + 8, :]
            )
    apply_group(w0, t0, w1, t1, cm, cs, scratch, TOP - 4, chunks)
    apply_group(w1, t1, w2, t2, cm, cs, scratch, TOP - 4, chunks)
    apply_group(w2, t2, w3, None, cm, cs, scratch, TOP - 4, chunks)
    chain = (w0, w1, w2, w3)
    for i in range(PER):
        for k in range(6):
            sums[k, pl.ds(group * PER + i, 1), :] = inner(chain[k // 2], chain[(k + 1) // 2], i, TOP, TOP, height)

    @pl.when(group == pl.num_programs(0) - 1)
    def _():
        add_up(sums, totals_out)


def last_kernel(height, totals_ref, keep_ref, rhs_ref, u0_all, u1_all, u2_all, w0_all, w1_all, w2_all, w3_all,
                x_ref, r_ref, rows, square, table):
    group = pl.program_id(0)

    @pl.when(group == 0)
    def _():
        rows[...] = jnp.zeros(rows.shape, F32)
        last_scalars(keep_ref, totals_ref, rows)
        transposed(rows, square, table)

    mine = pl.ds(group * 3 * PER, 3 * PER)
    basis = [ref.at[mine] for ref in (u0_all, u1_all, u2_all, w0_all, w1_all, w2_all, w3_all)]
    for i in range(PER):
        f = [spread(table, group * PER + i, j) for j in range(16)]
        for c in range(3):
            k = 3 * i + c
            for r in range(0, height, 8):
                vectors = [ref[k, TOP + r:TOP + r + 8, :] for ref in basis]
                vectors.append(rhs_ref[k, r:r + 8, :] - vectors[0])
                for out, at in ((x_ref, 0), (r_ref, 8)):
                    total = f[at] * vectors[0]
                    for j in range(1, 8):
                        total = total + f[at + j] * vectors[j]
                    out[k, r:r + 8, :] = total


def rows_kernel(*refs):
    low_refs, high_refs, outs = refs[:6], refs[6:12], refs[12:]
    loads = low_refs[0].shape[0]
    for j in range(loads + 18):
        to = slice(j * HALO, (j + 1) * HALO)
        for source, rows, out in ((low_refs, slice(0, HALO), outs[0]), (high_refs, slice(8 - HALO, 8), outs[1])):
            if j < loads:
                out[to, :] = source[0][j, rows, :]
            else:
                out[to, :] = field(source[1:], j - loads, rows)


def cut(get, rows, quarters, right_ref, left_ref):
    lane = lanes() % PITCH
    segment = lanes() // PITCH
    for c in range(3):
        for r in rows:
            right = jnp.zeros((8, 128), F32)
            left = right
            for q in range(quarters):
                for i in range(PER):
                    spot = (segment == i) & (lane >= 8 * q) & (lane < 8 * q + HALO)
                    x = get(q, i, c, r)
                    right = jnp.where(spot, pltpu.roll(x, (PITCH * i + 8 * q + HALO) % 128, 1), right)
                    left = jnp.where(spot, pltpu.roll(x, (PITCH * i + 8 * q) % 128, 1), left)
            right_ref[0, c, r:r + 8, :] = right
            left_ref[0, c, r:r + 8, :] = left


def each_group(merged, load_rows, raw_rows, rows, outs):
    group = pl.program_id(0)

    @pl.when(group < merged)
    def _():
        cut(lambda q, i, c, r: load_rows(3 * (PER * q + i) + c, r), rows, 4, *outs)

    for p in (0, 4):
        @pl.when(group == merged + p // 4)
        def _():
            cut(lambda q, i, c, r: raw_rows(3 * (p + q) + c, r), rows, min(4, 6 - p), *outs)


def columns_kernel(merged, height, data_ref, *refs):
    each_group(
        merged, lambda k, r: data_ref[k, r:r + 8, :], lambda k, r: field(refs[:5], k, slice(r, r + 8)),
        range(0, height, 8), refs[5:],
    )


def ends_kernel(merged, fields, down_ref, up_ref, all_down, all_up, right_ref, left_ref, one):
    one[...] = jnp.zeros(one.shape, F32)

    def load_rows(k, r):
        one[0:HALO, :] = (down_ref, up_ref)[r // 8][k * HALO:(k + 1) * HALO, :]
        return one[...]

    def raw_rows(k, r):
        k = k + fields
        one[0:HALO, :] = (all_down, all_up)[r // 8][k * HALO:(k + 1) * HALO, :]
        return one[...]

    each_group(merged, load_rows, raw_rows, (0, 8), (right_ref, left_ref))


def moved(block, axis, distance):
    n = lax.axis_size(axis)
    return lax.ppermute(block, axis, [(i, i + distance) for i in range(n) if 0 <= i + distance < n])


def summed(x):
    half = x.shape[0] // 2
    for axis in ("gy", "gx"):
        n = lax.axis_size(axis)
        d = 1
        while d < n:
            y = lax.ppermute(x, axis, [(i, i ^ d) for i in range(n)])
            s, e = two_sum(x[:half], y[:half])
            x = jnp.concatenate([s, (x[half:] + y[half:]) + e])
            d *= 2
    return x


def params(limit=8):
    return pltpu.CompilerParams(vmem_limit_bytes=limit * 2**20)


def shape(*dims):
    return jax.ShapeDtypeStruct(dims, F32)


def body(rhs, stiffness, coupling, edges, flip, pinned):
    loads, _, height, width = rhs.shape
    ext = height + 24
    groups = loads // PER
    merged = (groups + 3) // 4
    main = rhs.reshape(loads * 3, height, width)
    raw = (stiffness, coupling, edges, flip, pinned)
    fields = loads * 3 + 18

    def end_block(x, at):
        block = x.shape[:-2] + (8, width)
        lead = (0,) * (x.ndim - 2)
        return pl.BlockSpec(block, lambda g: lead + (at, 0))

    low, high = pl.pallas_call(
        rows_kernel,
        grid=(1,),
        in_specs=[end_block(x, at) for at in (0, height // 8 - 1) for x in (main,) + raw],
        out_specs=[pl.BlockSpec((fields * HALO, width), lambda g: (0, 0))] * 2,
        out_shape=[shape(fields * HALO, width)] * 2,
        compiler_params=params(),
    )(main, *raw, main, *raw)
    up = moved(low, "gx", -1)
    down = moved(high, "gx", 1)

    count = merged + 2
    wide = 4 * 3 * PER

    def send_columns(kernel, in_specs, rows, scratch, *operands):
        part = pl.BlockSpec((1, 3, rows, width), lambda h: (h, 0, 0, 0))
        right, left = pl.pallas_call(
            kernel,
            grid=(count,),
            in_specs=in_specs,
            out_specs=[part] * 2,
            out_shape=[shape(count, 3, rows, width)] * 2,
            scratch_shapes=scratch,
            compiler_params=params(),
        )(*operands)
        return moved(right, "gy", 1), moved(left, "gy", -1)

    resident = pl.BlockSpec(memory_space=pltpu.VMEM)
    from_left, from_right = send_columns(
        functools.partial(columns_kernel, merged, height),
        [pl.BlockSpec((wide, height, width), lambda h: (jnp.minimum(h, merged - 1), 0, 0))] + [resident] * 5,
        height, [], main, *raw,
    )
    line = pl.BlockSpec((wide * HALO, width), lambda h: (jnp.minimum(h, merged - 1), 0))
    left_ends, right_ends = send_columns(
        functools.partial(ends_kernel, merged, loads * 3),
        [line] * 2 + [resident] * 2,
        16, [pltpu.VMEM((8, width), F32)], down, up, down, up,
    )
    cm, cs = pl.pallas_call(
        functools.partial(prepare_kernel, loads, merged),
        out_shape=[shape(NCOEF, ext, width), shape(NCOEF, ext, width)],
        scratch_shapes=[pltpu.VMEM((6, 3, ext, width), F32)] * 2 + [pltpu.VMEM((2, 3, ext, width), F32)],
        compiler_params=params(),
    )(*raw, up, down, from_left, from_right, left_ends, right_ends)

    own_tile = pl.BlockSpec((3 * PER, height, width), lambda g: (g, 0, 0))
    line = pl.BlockSpec((3 * PER * HALO, width), lambda g: (g, 0))
    quarter = pl.BlockSpec((1, 3, height, width), lambda g: (g // 4, 0, 0, 0))
    corner = pl.BlockSpec((1, 3, 16, width), lambda g: (g // 4, 0, 0, 0))
    part = pl.BlockSpec((16, 128), lambda g: (0, 0))
    tiles = pltpu.VMEM((loads * 3, ext, width), F32)
    strips = pltpu.VMEM((groups, 3, ext, width), F32)
    own_shape = shape(loads * 3, height, width)
    sums_shape = shape(16, 128)
    sums_buffer = pltpu.VMEM((7, 128, 128), F32)
    small = [pltpu.VMEM((PAIR, 3, ext, width), F32), pltpu.VMEM((3, ext, width), F32)]
    u0, u1, u2, u3, s0, s1, s2, s3, sums = pl.pallas_call(
        functools.partial(first_kernel, height),
        grid=(groups,),
        in_specs=[own_tile, line, line, quarter, quarter] + [corner] * 2 + [resident] * 2,
        out_specs=[resident] * 8 + [part],
        out_shape=[tiles] * 4 + [strips] * 4 + [sums_shape],
        scratch_shapes=small + [pltpu.VMEM((2, 3, ext, width), F32), sums_buffer],
        compiler_params=params(),
    )(main, up, down, from_left, from_right, left_ends, right_ends, cm, cs)
    totals = summed(sums)
    fixed = part
    kept = pl.BlockSpec((32, 128), lambda g: (0, 0))
    w0, w1, w2, w3, sums, keep = pl.pallas_call(
        functools.partial(second_kernel, height),
        grid=(groups,),
        in_specs=[fixed] + [resident] * 10,
        out_specs=[resident] * 4 + [part, kept],
        out_shape=[tiles] * 4 + [sums_shape, shape(32, 128)],
        scratch_shapes=small + [pltpu.VMEM((128, 128), F32)] * 2 + [pltpu.VMEM((3, ext, width), F32)] * 3
        + [sums_buffer],
        compiler_params=params(),
    )(totals, u0, u1, u2, u3, s0, s1, s2, s3, cm, cs)
    totals = summed(sums)
    x, r = pl.pallas_call(
        functools.partial(last_kernel, height),
        grid=(groups,),
        in_specs=[fixed, kept, own_tile] + [resident] * 7,
        out_specs=[own_tile] * 2,
        out_shape=[own_shape] * 2,
        scratch_shapes=[pltpu.VMEM((32, 128), F32), pltpu.VMEM((128, 128), F32), pltpu.VMEM((128, 128), F32)],
        compiler_params=params(),
    )(totals, keep, main, u0, u1, u2, w0, w1, w2, w3)
    return x.reshape(rhs.shape), r.reshape(rhs.shape)


def solution(mesh):
    placed = (
        P(None, None, "gx", "gy"),
        P(None, "gx", "gy"),
        P(None, "gx", "gy"),
        P(None, "gx", "gy"),
        P("gx", "gy"),
        P("gx", "gy"),
    )
    return jax.shard_map(
        body,
        mesh=mesh,
        in_specs=placed,
        out_specs=(P(None, None, "gx", "gy"), P(None, None, "gx", "gy")),
        check_vma=False,
    )
```

time: 182 us -> 142 us (0.78)
  Pallas kernels: 90 us -> 65.9 us
  local copies, waits for them, and re-layouts: 14.7 us -> 5.55 us
  other arithmetic: 4.09 us -> 0.14 us
  starting transfers between devices: 33.7 us -> 30.1 us
    pallas_call x1, Pallas kernels: 31.8 us -> 23.1 us  [body(): pl.pallas_call(functools.partial(second_kernel, height), grid=(groups,),...]
    unnamed x31 -> x16, local copies, waits for them, and re-layouts: 13.5 us -> 5.55 us
    pallas_call x5 -> x4, Pallas kernels: 13.6 us -> 6.87 us  [the longest x2 5.13 us: send_columns(): pl.pallas_call(kernel, grid=(count,), in_specs=in_specs, out_specs=[part]...]
    pallas_call x1, Pallas kernels: 13.1 us -> 6.9 us  [body(): pl.pallas_call(functools.partial(last_kernel, height), grid=(groups,), in...]
    ppermute x10, starting transfers between devices: 22.6 us -> 17.2 us  [summed(): y = lax.ppermute(x, axis, [(i, i ^ d) for i in range(n)])]
    ppermute x10, waiting for transfers between devices: 16.2 us -> 20.4 us  [summed(): y = lax.ppermute(x, axis, [(i, i ^ d) for i in range(n)])]
    ppermute x4 -> x6, waiting for transfers between devices: 21.4 us -> 18.3 us  [moved(): lax.ppermute(block, axis, [(i, i + distance) for i in range(n) if 0 <= i...]
    pallas_call x1, Pallas kernels: 31.4 us -> 29 us  [body(): pl.pallas_call(functools.partial(first_kernel, height), grid=(groups,), i...]
  transfers between devices with their start and end apart: 14 -> 16, of which waited for: 13 -> 13; matrix products, arithmetic and copies ran while one was open for 0% -> 0% of each run, Pallas kernels for 0% -> 4%
where the time goes in v2:
time: 142 us; the launch traced here: 141 us
  Pallas kernels  65.9 us (46%)
  waiting for transfers between devices  38.6 us (27%)
  starting transfers between devices  30.1 us (21%)
  local copies, waits for them, and re-layouts  5.55 us (4%)
    pallas_call x1, Pallas kernels, body(): pl.pallas_call(functools.partial(first_kernel, height), grid=(groups,), i...  29 us
    pallas_call x1, Pallas kernels, body(): pl.pallas_call(functools.partial(second_kernel, height), grid=(groups,),...  23.1 us
    ppermute x10, waiting for transfers between devices, summed(): y = lax.ppermute(x, axis, [(i, i ^ d) for i in range(n)])  20.4 us
    ppermute x6, waiting for transfers between devices, moved(): lax.ppermute(block, axis, [(i, i + distance) for i in range(n) if 0 <= i...  18.3 us
    ppermute x10, starting transfers between devices, summed(): y = lax.ppermute(x, axis, [(i, i ^ d) for i in range(n)])  17.2 us
    ppermute x6, starting transfers between devices, moved(): lax.ppermute(block, axis, [(i, i + distance) for i in range(n) if 0 <= i...  12.9 us
    pallas_call x1, Pallas kernels, body(): pl.pallas_call(functools.partial(last_kernel, height), grid=(groups,), in...  6.9 us
    unnamed x16, local copies, waits for them, and re-layouts  5.55 us
  transfers between devices with their start and end apart: 16, of which 13 were waited for; matrix products, arithmetic and copies ran while one was open for 0% of the time, Pallas kernels for 4%

profile of v2, /device:TPU:0, one launch (start us, length us, event | category | flops | bytes accessed | tf_op | source)
XLA Modules:
  0.0 141.1 jit_solution(7754776074661135904)
XLA Ops:
  0.6 0.0 copy-start
  0.6 1.7 %copy-done = f32[48,3,32,128]{3,2,1,0:T(8,128)S(1)} copy-done((f32[48,3,32,128]{3,2,1,0:T(8,128)S(1)}, f32[48,3,32,128]{3,2,1,0:T(8,128)}, u32[]{:S(2)}) %copy-start) | copy-done | bytes 2359320
  2.3 0.0 copy-start.2
  2.3 0.9 copy-done.2
  3.2 0.0 copy-start.4
  3.2 0.8 copy-done.4
  4.0 0.0 copy-start.5
  4.0 0.8 copy-done.5
  4.7 0.0 copy-start.6
  4.7 0.7 copy-done.6
  5.5 0.0 copy-start.7
  5.5 0.7 copy-done.7
  6.2 0.0 copy-start.3
  6.2 0.2 shard_map.77
  6.4 0.0 copy-start.1
  6.4 1.4 %collective-permute-start = (f32[972,128]{1,0:T(8,128)S(1)}, f32[972,128]{1,0:T(8,128)S(1)}, u32[]{:S(2)}, u32[]{:S(2)}) collective-permute-start(f32[972,128]{1,0:T(8,128)S(1)} %get-tuple-element.27), channel_id=1, source_target_pairs={{4,0},{8,4},{12,8},{16,12},{20,16},{24,20},{28,24},{5,1},{9,5},{13... | collective-permute-start | bytes 1493000 | tf_op jit(solution)/shard_map/ppermute | solution.py:674
  7.9 5.5 %collective-permute-start.1 = (f32[972,128]{1,0:T(8,128)S(1)}, f32[972,128]{1,0:T(8,128)S(1)}, u32[]{:S(2)}, u32[]{:S(2)}) collective-permute-start(f32[972,128]{1,0:T(8,128)S(1)} %get-tuple-element.28), channel_id=1, source_target_pairs={{0,4},{4,8},{8,12},{12,16},{16,20},{20,24},{24,28},{1,5},{5,9},{9,... | collective-permute-start | bytes 1493000 | tf_op jit(solution)/shard_map/ppermute | solution.py:674
  13.4 2.3 %shard_map.78 = (f32[5,3,32,128]{3,2,1,0:T(8,128)S(1)}, f32[5,3,32,128]{3,2,1,0:T(8,128)S(1)}) custom-call(f32[144,32,128]{2,1,0:T(8,128)S(1)} %bitcast.5, f32[2,32,128]{2,1,0:T(8,128)S(1)} %copy-done.4, f32[2,32,128]{2,1,0:T(8,128)S(1)} %copy-done.5, f32[12,32,128]{2,1,0:T(8,128)S(1)} %copy-done.2, s32[32,128]{1,0:T(8,128)S(1)} %copy-done.6, ...), custom_call_target="tpu_custom_call" | custom-call | tf_op jit(solution)/shard_map/pallas_call | solution.py:728
  15.6 1.5 %collective-permute-start.2 = (f32[5,3,32,128]{3,2,1,0:T(8,128)S(1)}, f32[5,3,32,128]{3,2,1,0:T(8,128)S(1)}, u32[]{:S(2)}, u32[]{:S(2)}) collective-permute-start(f32[5,3,32,128]{3,2,1,0:T(8,128)S(1)} %get-tuple-element.29), channel_id=1, source_target_pairs={{0,1},{1,2},{2,3},{4,5},{5,6},{6,7},{8,9},{9,10},{10,11},{12,13},{... | collective-permute-start | bytes 737288 | tf_op jit(solution)/shard_map/ppermute | solution.py:674
  17.1 1.3 collective-permute-start.3
  18.4 4.4 %collective-permute-done.up_ref.all_up = f32[972,128]{1,0:T(8,128)S(1)} collective-permute-done((f32[972,128]{1,0:T(8,128)S(1)}, f32[972,128]{1,0:T(8,128)S(1)}, u32[]{:S(2)}, u32[]{:S(2)}) %collective-permute-start) | collective-permute-done | bytes 497696 | tf_op jit(solution)/shard_map/ppermute | solution.py:674
  22.8 10.9 %collective-permute-done.1.down_ref.all_down = f32[972,128]{1,0:T(8,128)S(1)} collective-permute-done((f32[972,128]{1,0:T(8,128)S(1)}, f32[972,128]{1,0:T(8,128)S(1)}, u32[]{:S(2)}, u32[]{:S(2)}) %collective-permute-start.1) | collective-permute-done | bytes 497696 | tf_op jit(solution)/shard_map/ppermute | solution.py:674
  33.7 2.9 %shard_map.79 = (f32[5,3,16,128]{3,2,1,0:T(8,128)S(1)}, f32[5,3,16,128]{3,2,1,0:T(8,128)S(1)}) custom-call(f32[972,128]{1,0:T(8,128)S(1)} %collective-permute-done.1.down_ref.all_down, f32[972,128]{1,0:T(8,128)S(1)} %collective-permute-done.up_ref.all_up, f32[972,128]{1,0:T(8,128)S(1)} %collective-permute-done.1.down_ref.all_down, ...), custom_call_target="tpu_custom_call" | custom-call | tf_op jit(solution)/shard_map/pallas_call | solution.py:728
  36.5 1.9 %collective-permute-start.4 = (f32[5,3,16,128]{3,2,1,0:T(8,128)S(1)}, f32[5,3,16,128]{3,2,1,0:T(8,128)S(1)}, u32[]{:S(2)}, u32[]{:S(2)}) collective-permute-start(f32[5,3,16,128]{3,2,1,0:T(8,128)S(1)} %get-tuple-element.31), channel_id=1, source_target_pairs={{0,1},{1,2},{2,3},{4,5},{5,6},{6,7},{8,9},{9,10},{10,11},{12,13},{... | collective-permute-start | bytes 368648 | tf_op jit(solution)/shard_map/ppermute | solution.py:674
  38.4 1.3 collective-permute-start.5
  39.7 0.0 collective-permute-done.2.left_ref
  39.8 0.0 collective-permute-done.3.right_ref
  39.8 0.0 collective-permute-done.4.left_ends
  39.8 3.0 %collective-permute-done.5.right_ends = f32[5,3,16,128]{3,2,1,0:T(8,128)S(1)} collective-permute-done((f32[5,3,16,128]{3,2,1,0:T(8,128)S(1)}, f32[5,3,16,128]{3,2,1,0:T(8,128)S(1)}, u32[]{:S(2)}, u32[]{:S(2)}) %collective-permute-start.5) | collective-permute-done | bytes 122912 | tf_op jit(solution)/shard_map/ppermute | solution.py:674
  42.8 0.0 copy-done.3
  42.8 1.5 %shard_map.80 = (f32[20,56,128]{2,1,0:T(8,128)S(1)}, f32[20,56,128]{2,1,0:T(8,128)S(1)}) custom-call(f32[2,32,128]{2,1,0:T(8,128)S(1)} %copy-done.4, f32[2,32,128]{2,1,0:T(8,128)S(1)} %copy-done.5, f32[12,32,128]{2,1,0:T(8,128)S(1)} %copy-done.3, s32[32,128]{1,0:T(8,128)S(1)} %copy-done.6, s32[32,128]{1,0:T(8,128)S(1)} %copy-done.7, ...), custom_call_target="tpu_custom_call" | custom-call | tf_op jit(solution)/shard_map/pallas_call | solution.py:751
  44.3 0.0 copy-done.1
  44.3 29.0 %shard_map.81 = (f32[144,56,128]{2,1,0:T(8,128)S(1)}, f32[144,56,128]{2,1,0:T(8,128)S(1)}, f32[144,56,128]{2,1,0:T(8,128)S(1)}, f32[144,56,128]{2,1,0:T(8,128)S(...) custom-call(f32[144,32,128]{2,1,0:T(8,128)S(1)} %bitcast.6, ...), custom_call_target="tpu_custom_call" | custom-call | tf_op jit(solution)/shard_map/pallas_call | solution.py:769
  73.3 3.5 %collective-permute-start.6 = (f32[16,128]{1,0:T(8,128)S(1)}, f32[16,128]{1,0:T(8,128)S(1)}, u32[]{:S(2)}, u32[]{:S(2)}) collective-permute-start(f32[16,128]{1,0:T(8,128)S(1)} %get-tuple-element.35), channel_id=1, source_target_pairs={{0,1},{1,0},{2,3},{3,2},{4,5},{5,4},{6,7},{7,6},{8,9},{9,8},{10,11... | collective-permute-start | bytes 24584 | tf_op jit(solution)/shard_map/ppermute | solution.py:683
  76.9 0.8 collective-permute-done.6
  77.7 0.2 collective-permute-start.7
  77.9 3.5 %collective-permute-done.7 = f32[16,128]{1,0:T(8,128)S(1)} collective-permute-done((f32[16,128]{1,0:T(8,128)S(1)}, f32[16,128]{1,0:T(8,128)S(1)}, u32[]{:S(2)}, u32[]{:S(2)}) %collective-permute-start.7) | collective-permute-done | bytes 8224 | tf_op jit(solution)/shard_map/ppermute | solution.py:683
  81.4 2.5 %collective-permute-start.8 = (f32[16,128]{1,0:T(8,128)S(1)}, f32[16,128]{1,0:T(8,128)S(1)}, u32[]{:S(2)}, u32[]{:S(2)}) collective-permute-start(f32[16,128]{1,0:T(8,128)S(1)} %pad_maximum_fusion.1), channel_id=1, source_target_pairs={{0,4},{4,0},{8,12},{12,8},{16,20},{20,16},{24,28},{28,24},{1,5},{5... | collective-permute-start | bytes 24584 | tf_op jit(solution)/shard_map/ppermute | solution.py:683
  84.0 1.6 %collective-permute-done.8 = f32[16,128]{1,0:T(8,128)S(1)} collective-permute-done((f32[16,128]{1,0:T(8,128)S(1)}, f32[16,128]{1,0:T(8,128)S(1)}, u32[]{:S(2)}, u32[]{:S(2)}) %collective-permute-start.8) | collective-permute-done | bytes 8224 | tf_op jit(solution)/shard_map/ppermute | solution.py:683
  85.6 1.6 %collective-permute-start.9 = (f32[16,128]{1,0:T(8,128)S(1)}, f32[16,128]{1,0:T(8,128)S(1)}, u32[]{:S(2)}, u32[]{:S(2)}) collective-permute-start(f32[16,128]{1,0:T(8,128)S(1)} %pad_maximum_fusion.2), channel_id=1, source_target_pairs={{0,8},{4,12},{8,0},{12,4},{16,24},{20,28},{24,16},{28,20},{1,9},{5... | collective-permute-start | bytes 24584 | tf_op jit(solution)/shard_map/ppermute | solution.py:683
  87.3 2.1 %collective-permute-done.9 = f32[16,128]{1,0:T(8,128)S(1)} collective-permute-done((f32[16,128]{1,0:T(8,128)S(1)}, f32[16,128]{1,0:T(8,128)S(1)}, u32[]{:S(2)}, u32[]{:S(2)}) %collective-permute-start.9) | collective-permute-done | bytes 8224 | tf_op jit(solution)/shard_map/ppermute | solution.py:683
  89.4 2.7 %collective-permute-start.10 = (f32[16,128]{1,0:T(8,128)S(1)}, f32[16,128]{1,0:T(8,128)S(1)}, u32[]{:S(2)}, u32[]{:S(2)}) collective-permute-start(f32[16,128]{1,0:T(8,128)S(1)} %pad_maximum_fusion.3), channel_id=1, source_target_pairs={{0,16},{4,20},{8,24},{12,28},{16,0},{20,4},{24,8},{28,12},{1,17},{... | collective-permute-start | bytes 24584 | tf_op jit(solution)/shard_map/ppermute | solution.py:683
  92.0 2.0 %collective-permute-done.10 = f32[16,128]{1,0:T(8,128)S(1)} collective-permute-done((f32[16,128]{1,0:T(8,128)S(1)}, f32[16,128]{1,0:T(8,128)S(1)}, u32[]{:S(2)}, u32[]{:S(2)}) %collective-permute-start.10) | collective-permute-done | bytes 8224 | tf_op jit(solution)/shard_map/ppermute | solution.py:683
  94.0 23.1 %shard_map.82 = (f32[144,56,128]{2,1,0:T(8,128)S(1)}, f32[144,56,128]{2,1,0:T(8,128)S(1)}, f32[144,56,128]{2,1,0:T(8,128)S(1)}, f32[144,56,128]{2,1,0:T(8,128)S(...) custom-call(f32[16,128]{1,0:T(8,128)S(1)} %pad_maximum_fusion.4.totals_ref, ...), custom_call_target="tpu_custom_call" | custom-call | tf_op jit(solution)/shard_map/pallas_call | solution.py:781
  117.1 0.1 collective-permute-start.11
  117.2 1.2 collective-permute-done.11
  118.3 0.2 collective-permute-start.12
  118.5 3.5 %collective-permute-done.12 = f32[16,128]{1,0:T(8,128)S(1)} collective-permute-done((f32[16,128]{1,0:T(8,128)S(1)}, f32[16,128]{1,0:T(8,128)S(1)}, u32[]{:S(2)}, u32[]{:S(2)}) %collective-permute-start.12) | collective-permute-done | bytes 8224 | tf_op jit(solution)/shard_map/ppermute | solution.py:683
  122.1 2.1 %collective-permute-start.13 = (f32[16,128]{1,0:T(8,128)S(1)}, f32[16,128]{1,0:T(8,128)S(1)}, u32[]{:S(2)}, u32[]{:S(2)}) collective-permute-start(f32[16,128]{1,0:T(8,128)S(1)} %pad_maximum_fusion.6), channel_id=1, source_target_pairs={{0,4},{4,0},{8,12},{12,8},{16,20},{20,16},{24,28},{28,24},{1,5},{5... | collective-permute-start | bytes 24584 | tf_op jit(solution)/shard_map/ppermute | solution.py:683
  124.2 1.6 %collective-permute-done.13 = f32[16,128]{1,0:T(8,128)S(1)} collective-permute-done((f32[16,128]{1,0:T(8,128)S(1)}, f32[16,128]{1,0:T(8,128)S(1)}, u32[]{:S(2)}, u32[]{:S(2)}) %collective-permute-start.13) | collective-permute-done | bytes 8224 | tf_op jit(solution)/shard_map/ppermute | solution.py:683
  125.8 1.6 %collective-permute-start.14 = (f32[16,128]{1,0:T(8,128)S(1)}, f32[16,128]{1,0:T(8,128)S(1)}, u32[]{:S(2)}, u32[]{:S(2)}) collective-permute-start(f32[16,128]{1,0:T(8,128)S(1)} %pad_maximum_fusion.7), channel_id=1, source_target_pairs={{0,8},{4,12},{8,0},{12,4},{16,24},{20,28},{24,16},{28,20},{1,9},{5... | collective-permute-start | bytes 24584 | tf_op jit(solution)/shard_map/ppermute | solution.py:683
  127.4 2.1 %collective-permute-done.14 = f32[16,128]{1,0:T(8,128)S(1)} collective-permute-done((f32[16,128]{1,0:T(8,128)S(1)}, f32[16,128]{1,0:T(8,128)S(1)}, u32[]{:S(2)}, u32[]{:S(2)}) %collective-permute-start.14) | collective-permute-done | bytes 8224 | tf_op jit(solution)/shard_map/ppermute | solution.py:683
  129.5 2.7 %collective-permute-start.15 = (f32[16,128]{1,0:T(8,128)S(1)}, f32[16,128]{1,0:T(8,128)S(1)}, u32[]{:S(2)}, u32[]{:S(2)}) collective-permute-start(f32[16,128]{1,0:T(8,128)S(1)} %pad_maximum_fusion.8), channel_id=1, source_target_pairs={{0,16},{4,20},{8,24},{12,28},{16,0},{20,4},{24,8},{28,12},{1,17},{... | collective-permute-start | bytes 24584 | tf_op jit(solution)/shard_map/ppermute | solution.py:683
  132.2 2.0 %collective-permute-done.15 = f32[16,128]{1,0:T(8,128)S(1)} collective-permute-done((f32[16,128]{1,0:T(8,128)S(1)}, f32[16,128]{1,0:T(8,128)S(1)}, u32[]{:S(2)}, u32[]{:S(2)}) %collective-permute-start.15) | collective-permute-done | bytes 8224 | tf_op jit(solution)/shard_map/ppermute | solution.py:683
  134.2 6.9 %shard_map.83 = (f32[144,32,128]{2,1,0:T(8,128)}, f32[144,32,128]{2,1,0:T(8,128)}) custom-call(f32[16,128]{1,0:T(8,128)S(1)} %pad_maximum_fusion.9.totals_ref, f32[32,128]{1,0:T(8,128)S(1)} %get-tuple-element.45.keep_ref, f32[144,32,128]{2,1,0:T(8,128)S(1)} %bitcast.7, f32[144,56,128]{2,1,0:T(8,128)S(1)} %get-tuple-element.36.u0_all, ...), custom_call_target="tpu_custom_call" | custom-call | tf_op jit(solution)/shard_map/pallas_call | solution.py:792
  (20 shorter events, 0.1 us)
Async XLA Ops:
  0.6 1.7 %copy-start = (f32[48,3,32,128]{3,2,1,0:T(8,128)S(1)}, f32[48,3,32,128]{3,2,1,0:T(8,128)}, u32[]{:S(2)}) copy-start(f32[48,3,32,128]{3,2,1,0:T(8,128)} %param.6) | copy-start | bytes 7077892
  2.3 0.9 copy-start.2
  3.2 0.8 copy-start.4
  4.0 0.8 copy-start.5
  4.7 0.7 copy-start.6
  5.5 0.7 copy-start.7
  6.2 36.6 %copy-start.3 = (f32[12,32,128]{2,1,0:T(8,128)S(1)}, f32[12,32,128]{2,1,0:T(8,128)}, u32[]{:S(2)}) copy-start(f32[12,32,128]{2,1,0:T(8,128)} %edges.1) | copy-start | bytes 589828
  6.4 37.9 %copy-start.1 = (f32[48,3,32,128]{3,2,1,0:T(8,128)S(1)}, f32[48,3,32,128]{3,2,1,0:T(8,128)}, u32[]{:S(2)}) copy-start(f32[48,3,32,128]{3,2,1,0:T(8,128)} %param.6) | copy-start | bytes 7077892
  6.4 16.4 %collective-permute-start = (f32[972,128]{1,0:T(8,128)S(1)}, f32[972,128]{1,0:T(8,128)S(1)}, u32[]{:S(2)}, u32[]{:S(2)}) collective-permute-start(f32[972,128]{1,0:T(8,128)S(1)} %get-tuple-element.27), channel_id=1, source_target_pairs={{4,0},{8,4},{12,8},{16,12},{20,16},{24,20},{28,24},{5,1},{9,5},{13... | collective-permute-start | bytes 1493000 | tf_op jit(solution)/shard_map/ppermute | solution.py:674
  7.9 25.8 %collective-permute-start.1 = (f32[972,128]{1,0:T(8,128)S(1)}, f32[972,128]{1,0:T(8,128)S(1)}, u32[]{:S(2)}, u32[]{:S(2)}) collective-permute-start(f32[972,128]{1,0:T(8,128)S(1)} %get-tuple-element.28), channel_id=1, source_target_pairs={{0,4},{4,8},{8,12},{12,16},{16,20},{20,24},{24,28},{1,5},{5,9},{9,... | collective-permute-start | bytes 1493000 | tf_op jit(solution)/shard_map/ppermute | solution.py:674
  15.6 24.1 %collective-permute-start.2 = (f32[5,3,32,128]{3,2,1,0:T(8,128)S(1)}, f32[5,3,32,128]{3,2,1,0:T(8,128)S(1)}, u32[]{:S(2)}, u32[]{:S(2)}) collective-permute-start(f32[5,3,32,128]{3,2,1,0:T(8,128)S(1)} %get-tuple-element.29), channel_id=1, source_target_pairs={{0,1},{1,2},{2,3},{4,5},{5,6},{6,7},{8,9},{9,10},{10,11},{12,13},{... | collective-permute-start | bytes 737288 | tf_op jit(solution)/shard_map/ppermute | solution.py:674
  17.1 22.6 %collective-permute-start.3 = (f32[5,3,32,128]{3,2,1,0:T(8,128)S(1)}, f32[5,3,32,128]{3,2,1,0:T(8,128)S(1)}, u32[]{:S(2)}, u32[]{:S(2)}) collective-permute-start(f32[5,3,32,128]{3,2,1,0:T(8,128)S(1)} %get-tuple-element.30), channel_id=1, source_target_pairs={{1,0},{2,1},{3,2},{5,4},{6,5},{7,6},{9,8},{10,9},{11,10},{13,12},{... | collective-permute-start | bytes 737288 | tf_op jit(solution)/shard_map/ppermute | solution.py:674
  36.5 3.2 %collective-permute-start.4 = (f32[5,3,16,128]{3,2,1,0:T(8,128)S(1)}, f32[5,3,16,128]{3,2,1,0:T(8,128)S(1)}, u32[]{:S(2)}, u32[]{:S(2)}) collective-permute-start(f32[5,3,16,128]{3,2,1,0:T(8,128)S(1)} %get-tuple-element.31), channel_id=1, source_target_pairs={{0,1},{1,2},{2,3},{4,5},{5,6},{6,7},{8,9},{9,10},{10,11},{12,13},{... | collective-permute-start | bytes 368648 | tf_op jit(solution)/shard_map/ppermute | solution.py:674
  38.4 4.3 %collective-permute-start.5 = (f32[5,3,16,128]{3,2,1,0:T(8,128)S(1)}, f32[5,3,16,128]{3,2,1,0:T(8,128)S(1)}, u32[]{:S(2)}, u32[]{:S(2)}) collective-permute-start(f32[5,3,16,128]{3,2,1,0:T(8,128)S(1)} %get-tuple-element.32), channel_id=1, source_target_pairs={{1,0},{2,1},{3,2},{5,4},{6,5},{7,6},{9,8},{10,9},{11,10},{13,12},{... | collective-permute-start | bytes 368648 | tf_op jit(solution)/shard_map/ppermute | solution.py:674
  73.3 4.4 %collective-permute-start.6 = (f32[16,128]{1,0:T(8,128)S(1)}, f32[16,128]{1,0:T(8,128)S(1)}, u32[]{:S(2)}, u32[]{:S(2)}) collective-permute-start(f32[16,128]{1,0:T(8,128)S(1)} %get-tuple-element.35), channel_id=1, source_target_pairs={{0,1},{1,0},{2,3},{3,2},{4,5},{5,4},{6,7},{7,6},{8,9},{9,8},{10,11... | collective-permute-start | bytes 24584 | tf_op jit(solution)/shard_map/ppermute | solution.py:683
  77.7 3.7 %collective-permute-start.7 = (f32[16,128]{1,0:T(8,128)S(1)}, f32[16,128]{1,0:T(8,128)S(1)}, u32[]{:S(2)}, u32[]{:S(2)}) collective-permute-start(f32[16,128]{1,0:T(8,128)S(1)} %pad_maximum_fusion), channel_id=1, source_target_pairs={{0,2},{1,3},{2,0},{3,1},{4,6},{5,7},{6,4},{7,5},{8,10},{9,11},{10,... | collective-permute-start | bytes 24584 | tf_op jit(solution)/shard_map/ppermute | solution.py:683
  81.4 4.2 %collective-permute-start.8 = (f32[16,128]{1,0:T(8,128)S(1)}, f32[16,128]{1,0:T(8,128)S(1)}, u32[]{:S(2)}, u32[]{:S(2)}) collective-permute-start(f32[16,128]{1,0:T(8,128)S(1)} %pad_maximum_fusion.1), channel_id=1, source_target_pairs={{0,4},{4,0},{8,12},{12,8},{16,20},{20,16},{24,28},{28,24},{1,5},{5... | collective-permute-start | bytes 24584 | tf_op jit(solution)/shard_map/ppermute | solution.py:683
  85.6 3.7 %collective-permute-start.9 = (f32[16,128]{1,0:T(8,128)S(1)}, f32[16,128]{1,0:T(8,128)S(1)}, u32[]{:S(2)}, u32[]{:S(2)}) collective-permute-start(f32[16,128]{1,0:T(8,128)S(1)} %pad_maximum_fusion.2), channel_id=1, source_target_pairs={{0,8},{4,12},{8,0},{12,4},{16,24},{20,28},{24,16},{28,20},{1,9},{5... | collective-permute-start | bytes 24584 | tf_op jit(solution)/shard_map/ppermute | solution.py:683
  89.4 4.6 %collective-permute-start.10 = (f32[16,128]{1,0:T(8,128)S(1)}, f32[16,128]{1,0:T(8,128)S(1)}, u32[]{:S(2)}, u32[]{:S(2)}) collective-permute-start(f32[16,128]{1,0:T(8,128)S(1)} %pad_maximum_fusion.3), channel_id=1, source_target_pairs={{0,16},{4,20},{8,24},{12,28},{16,0},{20,4},{24,8},{28,12},{1,17},{... | collective-permute-start | bytes 24584 | tf_op jit(solution)/shard_map/ppermute | solution.py:683
  117.1 1.2 collective-permute-start.11
  118.3 3.7 %collective-permute-start.12 = (f32[16,128]{1,0:T(8,128)S(1)}, f32[16,128]{1,0:T(8,128)S(1)}, u32[]{:S(2)}, u32[]{:S(2)}) collective-permute-start(f32[16,128]{1,0:T(8,128)S(1)} %pad_maximum_fusion.5), channel_id=1, source_target_pairs={{0,2},{1,3},{2,0},{3,1},{4,6},{5,7},{6,4},{7,5},{8,10},{9,11},{10,... | collective-permute-start | bytes 24584 | tf_op jit(solution)/shard_map/ppermute | solution.py:683
  122.1 3.7 %collective-permute-start.13 = (f32[16,128]{1,0:T(8,128)S(1)}, f32[16,128]{1,0:T(8,128)S(1)}, u32[]{:S(2)}, u32[]{:S(2)}) collective-permute-start(f32[16,128]{1,0:T(8,128)S(1)} %pad_maximum_fusion.6), channel_id=1, source_target_pairs={{0,4},{4,0},{8,12},{12,8},{16,20},{20,16},{24,28},{28,24},{1,5},{5... | collective-permute-start | bytes 24584 | tf_op jit(solution)/shard_map/ppermute | solution.py:683
  125.8 3.7 %collective-permute-start.14 = (f32[16,128]{1,0:T(8,128)S(1)}, f32[16,128]{1,0:T(8,128)S(1)}, u32[]{:S(2)}, u32[]{:S(2)}) collective-permute-start(f32[16,128]{1,0:T(8,128)S(1)} %pad_maximum_fusion.7), channel_id=1, source_target_pairs={{0,8},{4,12},{8,0},{12,4},{16,24},{20,28},{24,16},{28,20},{1,9},{5... | collective-permute-start | bytes 24584 | tf_op jit(solution)/shard_map/ppermute | solution.py:683
  129.5 4.6 %collective-permute-start.15 = (f32[16,128]{1,0:T(8,128)S(1)}, f32[16,128]{1,0:T(8,128)S(1)}, u32[]{:S(2)}, u32[]{:S(2)}) collective-permute-start(f32[16,128]{1,0:T(8,128)S(1)} %pad_maximum_fusion.8), channel_id=1, source_target_pairs={{0,16},{4,20},{8,24},{12,28},{16,0},{20,4},{24,8},{28,12},{1,17},{... | collective-permute-start | bytes 24584 | tf_op jit(solution)/shard_map/ppermute | solution.py:683

commit v3 on v2

--- a/solution.py
+++ b/solution.py
@@ -155,8 +155,18 @@
     return ref[i:i + 1, :]
 
 
-def middle_scalars(sums_ref, keep_ref):
-    sums = [(row(sums_ref, i), row(sums_ref, 8 + i)) for i in range(7)]
+def pair_sums(parts_ref):
+    def step(d, total):
+        high, low = total
+        high, error = two_sum(high, parts_ref[d])
+        return high, low + error
+    zero = jnp.zeros(parts_ref.shape[1:], F32)
+    high, low = lax.fori_loop(1, parts_ref.shape[0], step, (parts_ref[0], zero))
+    return [quick(high[i:i + 1, :], low[i:i + 1, :]) for i in range(7)]
+
+
+def middle_scalars(parts_ref, keep_ref):
+    sums = pair_sums(parts_ref)
     m = with_pins(sums, sums[6])
     a, b, top = first_block(m)
     alphas, sigmas = steps_of([x[0] for x in a], [None] + [x[0] for x in b], None)
@@ -169,7 +179,7 @@
         keep_ref[i:i + 1, :] = value
 
 
-def last_scalars(keep_ref, sums_ref, out_ref):
+def last_scalars(keep_ref, parts_ref, out_ref):
     kept = [row(keep_ref, i) for i in range(25)]
     pins = [kept[5], kept[4]]
     a = [(kept[6 + 2 * i], kept[7 + 2 * i]) for i in range(3)]
@@ -177,7 +187,7 @@
     top, weight = kept[16], kept[17]
     alphas, sigmas = kept[18:21], kept[21:24]
     lead = kept[24]
-    nu = with_pins([(row(sums_ref, i), row(sums_ref, 8 + i)) for i in range(6)], lift(weight * kept[4] * kept[4]))
+    nu = with_pins(pair_sums(parts_ref), lift(weight * kept[4] * kept[4]))
     b3 = dd_div(nu[0], dd_mul(lift(top), dd_mul(lift(lead), lift(lead))))
     a_late, b_late = second_block(nu, a, b, b3)
     more, more_sigmas = steps_of(
@@ -395,49 +405,53 @@
             before[n] = rolled
 
 
-def apply_group(src_main, src_strip, dst_main, dst_strip, coef_main, coef_strip, scratch, first, chunks):
+def apply_groups(src_mains, src_strips, dst_mains, dst_strips, coef_main, coef_strip, scratch, first, chunks):
     side, strip_q = scratch
     lane = lanes()
 
-    def put_strip(c, r, x):
-        if dst_strip is not None:
-            dst_strip[c, r:r + 8, :] = x
-
-    def put_q(c, r, x):
-        strip_q[c, r:r + 8, :] = x
-
-    tile_step([(
-        side.at[0],
-        lambda c, r: src_strip[c, r:r + 8, :],
-        lambda c, r, x: pltpu.roll(x, 127, 1),
-        lambda c, r, x: pltpu.roll(x, 1, 1),
-        put_strip,
-        put_q,
-    )], coef_strip, first, chunks)
-
-    def tile(i, slot):
+    def strip_tile(n):
+        def put(c, r, x):
+            if dst_strips is not None:
+                dst_strips[n][c, r:r + 8, :] = x
+
+        def put_q(c, r, x):
+            strip_q[n, c, r:r + 8, :] = x
+
+        return (
+            side.at[n],
+            lambda c, r: src_strips[n][c, r:r + 8, :],
+            lambda c, r, x: pltpu.roll(x, 127, 1),
+            lambda c, r, x: pltpu.roll(x, 1, 1),
+            put,
+            put_q,
+        )
+
+    tile_step([strip_tile(n) for n in range(PAIR)], coef_strip, first, chunks)
+
+    def tile(n, i, slot):
         base = 3 * i
         to_last = (127 - (PITCH * i + 21)) % 128
         to_first = (128 - (PITCH * i + HALO - 1)) % 128
 
         def get(c, r):
-            return src_main[base + c, r:r + 8, :]
+            return src_mains[n][base + c, r:r + 8, :]
 
         def beside(c, r, x):
-            beyond = pltpu.roll(src_strip[c, r:r + 8, :], to_last, 1)
+            beyond = pltpu.roll(src_strips[n][c, r:r + 8, :], to_last, 1)
             return jnp.where(lane == 127, beyond, pltpu.roll(x, 127, 1))
 
         def spill(c, r, x):
-            beyond = pltpu.roll(strip_q[c, r:r + 8, :], to_first, 1)
+            beyond = pltpu.roll(strip_q[n, c, r:r + 8, :], to_first, 1)
             return jnp.where(lane == 0, beyond, pltpu.roll(x, 1, 1))
 
         def put(c, r, x):
-            dst_main[base + c, r:r + 8, :] = x
+            dst_mains[n][base + c, r:r + 8, :] = x
 
         return side.at[slot], get, beside, spill, put, None
 
-    for i in range(0, PER, PAIR):
-        tile_step([tile(i + n, n) for n in range(PAIR)], coef_main, first, chunks)
+    for n in range(PAIR):
+        for i in range(0, PER, PAIR):
+            tile_step([tile(n, i + j, j) for j in range(PAIR)], coef_main, first, chunks)
 
 
 def add_up(sums, totals_ref):
@@ -459,6 +473,10 @@
     return fold(total)
 
 
+def mine(ref, groups):
+    return [ref.at[pl.ds(g * 3 * PER, 3 * PER)] for g in groups]
+
+
 def clear(scratch):
     for ref in scratch:
         ref[...] = jnp.zeros(ref.shape, F32)
@@ -475,41 +493,40 @@
         clear(scratch)
         clear((sums,))
 
-    mine = pl.ds(group * 3 * PER, 3 * PER)
-    u0, u1, u2, u3 = (ref.at[mine] for ref in (u0_all, u1_all, u2_all, u3_all))
-    s0, s1, s2, s3 = (ref.at[group] for ref in (s0_all, s1_all, s2_all, s3_all))
-    q = group % 4
-    for c in range(3):
-        join_sides(sides, c, (0, c), (left_ref, right_ref), (left_ends, right_ends), height)
+    groups = [group * PAIR + n for n in range(PAIR)]
+    chain = [mine(ref, groups) for ref in (u0_all, u1_all, u2_all, u3_all)]
+    strips = [[ref.at[g] for g in groups] for ref in (s0_all, s1_all, s2_all, s3_all)]
+    for n, g in enumerate(groups):
+        u0, s0 = chain[0][n], strips[0][n]
+        for c in range(3):
+            join_sides(sides, c, (0, c), (left_ref, right_ref), (left_ends, right_ends), height)
+            for i in range(PER):
+                k = 3 * (n * PER + i) + c
+                join_rows(u0, (3 * i + c,), rhs_ref[k, :, :], up_ref[k * HALO:(k + 1) * HALO, :],
+                          down_ref[k * HALO:(k + 1) * HALO, :], height)
+            for r in range(0, ext, 8):
+                total = jnp.zeros((8, 128), F32)
+                for i in range(PER):
+                    x = u0[3 * i + c, r:r + 8, :] * cm[19, r:r + 8, :]
+                    u0[3 * i + c, r:r + 8, :] = x
+                    total = own_columns(x, i, total)
+                total = other_columns(sides[0, c, r:r + 8, :], sides[1, c, r:r + 8, :], g % 4, total)
+                s0[c, r:r + 8, :] = total * cs[19, r:r + 8, :]
+    for j, (first, rows) in enumerate(((TOP - 6, height + 16), (TOP - 5, height + 16), (TOP - 4, height + 8))):
+        apply_groups(chain[j], strips[j], chain[j + 1], strips[j + 1], cm, cs, scratch, first, rows // 8)
+    for n, g in enumerate(groups):
+        vectors = [v[n] for v in chain]
         for i in range(PER):
-            k = 3 * i + c
-            join_rows(u0, (k,), rhs_ref[k, :, :], up_ref[k * HALO:(k + 1) * HALO, :],
-                      down_ref[k * HALO:(k + 1) * HALO, :], height)
-        for r in range(0, ext, 8):
-            total = jnp.zeros((8, 128), F32)
-            for i in range(PER):
-                x = u0[3 * i + c, r:r + 8, :] * cm[19, r:r + 8, :]
-                u0[3 * i + c, r:r + 8, :] = x
-                total = own_columns(x, i, total)
-            total = other_columns(sides[0, c, r:r + 8, :], sides[1, c, r:r + 8, :], q, total)
-            s0[c, r:r + 8, :] = total * cs[19, r:r + 8, :]
-    apply_group(u0, s0, u1, s1, cm, cs, scratch, TOP - 6, (height + 16) // 8)
-    apply_group(u1, s1, u2, s2, cm, cs, scratch, TOP - 5, (height + 16) // 8)
-    apply_group(u2, s2, u3, s3, cm, cs, scratch, TOP - 4, (height + 8) // 8)
-    chain = (u0, u1, u2, u3)
-    for i in range(PER):
-        rows = []
-        for k in range(6):
-            rows.append(inner(chain[k // 2], chain[(k + 1) // 2], i, TOP, TOP, height))
-        total = None
-        for c in range(3):
-            for r in range(0, height, 8):
-                t = rhs_ref[3 * i + c, r:r + 8, :] - u0[3 * i + c, TOP + r:TOP + r + 8, :]
-                t = t * t
-                total = t if total is None else total + t
-        rows.append(fold(total))
-        for k in range(7):
-            sums[k, pl.ds(group * PER + i, 1), :] = rows[k]
+            rows = [inner(vectors[k // 2], vectors[(k + 1) // 2], i, TOP, TOP, height) for k in range(6)]
+            total = None
+            for c in range(3):
+                for r in range(0, height, 8):
+                    t = rhs_ref[3 * (n * PER + i) + c, r:r + 8, :] - vectors[0][3 * i + c, TOP + r:TOP + r + 8, :]
+                    t = t * t
+                    total = t if total is None else total + t
+            rows.append(fold(total))
+            for k in range(7):
+                sums[k, pl.ds(g * PER + i, 1), :] = rows[k]
 
     @pl.when(group == pl.num_programs(0) - 1)
     def _():
@@ -539,40 +556,43 @@
         middle_scalars(totals_ref, keep_ref)
         transposed(keep_ref, square, table)
 
-    mine = pl.ds(group * 3 * PER, 3 * PER)
-    u0, u1, u2, u3 = (ref.at[mine] for ref in (u0_all, u1_all, u2_all, u3_all))
-    w0, w1, w2, w3 = (ref.at[mine] for ref in (w0_all, w1_all, w2_all, w3_all))
-    s0, s1, s2, s3 = (ref.at[group] for ref in (s0_all, s1_all, s2_all, s3_all))
+    groups = [group * PAIR + n for n in range(PAIR)]
+    early = [mine(ref, groups) for ref in (u0_all, u1_all, u2_all, u3_all)]
+    chain = [mine(ref, groups) for ref in (w0_all, w1_all, w2_all, w3_all)]
+    strips = [[ref.at[g] for g in groups] for ref in (s0_all, s1_all, s2_all, s3_all)]
     chunks = (height + 8) // 8
     window = range(TOP - 4, TOP - 4 + 8 * chunks, 8)
     segment = lanes() // PITCH
-    weights = [[spread(table, group * PER + i, j) for j in range(4)] for i in range(PER)]
-    for i in range(PER):
+    for n, g in enumerate(groups):
+        weights = [[spread(table, g * PER + i, j) for j in range(4)] for i in range(PER)]
+        for i in range(PER):
+            for c in range(3):
+                for r in window:
+                    x = weights[i][0] * early[0][n][3 * i + c, r:r + 8, :]
+                    for j in range(1, 4):
+                        x = x + weights[i][j] * early[j][n][3 * i + c, r:r + 8, :]
+                    chain[0][n][3 * i + c, r:r + 8, :] = x
+        mixed = []
+        for j in range(4):
+            m = weights[0][j]
+            for i in range(1, PER):
+                m = jnp.where(segment == i, weights[i][j], m)
+            mixed.append(m)
         for c in range(3):
             for r in window:
-                w0[3 * i + c, r:r + 8, :] = (
-                    weights[i][0] * u0[3 * i + c, r:r + 8, :] + weights[i][1] * u1[3 * i + c, r:r + 8, :]
-                    + weights[i][2] * u2[3 * i + c, r:r + 8, :] + weights[i][3] * u3[3 * i + c, r:r + 8, :]
-                )
-    mixed = []
-    for j in range(4):
-        m = weights[0][j]
-        for i in range(1, PER):
-            m = jnp.where(segment == i, weights[i][j], m)
-        mixed.append(m)
-    for c in range(3):
-        for r in window:
-            t0[c, r:r + 8, :] = (
-                mixed[0] * s0[c, r:r + 8, :] + mixed[1] * s1[c, r:r + 8, :]
-                + mixed[2] * s2[c, r:r + 8, :] + mixed[3] * s3[c, r:r + 8, :]
-            )
-    apply_group(w0, t0, w1, t1, cm, cs, scratch, TOP - 4, chunks)
-    apply_group(w1, t1, w2, t2, cm, cs, scratch, TOP - 4, chunks)
-    apply_group(w2, t2, w3, None, cm, cs, scratch, TOP - 4, chunks)
-    chain = (w0, w1, w2, w3)
-    for i in range(PER):
-        for k in range(6):
-            sums[k, pl.ds(group * PER + i, 1), :] = inner(chain[k // 2], chain[(k + 1) // 2], i, TOP, TOP, height)
+                x = mixed[0] * strips[0][n][c, r:r + 8, :]
+                for j in range(1, 4):
+                    x = x + mixed[j] * strips[j][n][c, r:r + 8, :]
+                t0[n, c, r:r + 8, :] = x
+    late = [[t.at[n] for n in range(PAIR)] for t in (t0, t1, t2)] + [None]
+    for j in range(3):
+        apply_groups(chain[j], late[j], chain[j + 1], late[j + 1], cm, cs, scratch, TOP - 4, chunks)
+    for n, g in enumerate(groups):
+        vectors = [v[n] for v in chain]
+        for i in range(PER):
+            for k in range(6):
+                sums[k, pl.ds(g * PER + i, 1), :] = inner(
+                    vectors[k // 2], vectors[(k + 1) // 2], i, TOP, TOP, height)
 
     @pl.when(group == pl.num_programs(0) - 1)
     def _():
@@ -674,17 +694,9 @@
     return lax.ppermute(block, axis, [(i, i + distance) for i in range(n) if 0 <= i + distance < n])
 
 
-def summed(x):
-    half = x.shape[0] // 2
-    for axis in ("gy", "gx"):
-        n = lax.axis_size(axis)
-        d = 1
-        while d < n:
-            y = lax.ppermute(x, axis, [(i, i ^ d) for i in range(n)])
-            s, e = two_sum(x[:half], y[:half])
-            x = jnp.concatenate([s, (x[half:] + y[half:]) + e])
-            d *= 2
-    return x
+def gathered(x):
+    n = lax.axis_size("gx") * lax.axis_size("gy")
+    return lax.all_to_all(jnp.broadcast_to(x[None], (n,) + x.shape), ("gx", "gy"), 0, 0, tiled=True)
 
 
 def params(limit=8):
@@ -715,7 +727,7 @@
         in_specs=[end_block(x, at) for at in (0, height // 8 - 1) for x in (main,) + raw],
         out_specs=[pl.BlockSpec((fields * HALO, width), lambda g: (0, 0))] * 2,
         out_shape=[shape(fields * HALO, width)] * 2,
-        compiler_params=params(),
+        compiler_params=params(60),
     )(main, *raw, main, *raw)
     up = moved(low, "gx", -1)
     down = moved(high, "gx", 1)
@@ -756,39 +768,40 @@
     )(*raw, up, down, from_left, from_right, left_ends, right_ends)
 
     own_tile = pl.BlockSpec((3 * PER, height, width), lambda g: (g, 0, 0))
-    line = pl.BlockSpec((3 * PER * HALO, width), lambda g: (g, 0))
-    quarter = pl.BlockSpec((1, 3, height, width), lambda g: (g // 4, 0, 0, 0))
-    corner = pl.BlockSpec((1, 3, 16, width), lambda g: (g // 4, 0, 0, 0))
-    part = pl.BlockSpec((16, 128), lambda g: (0, 0))
+    own_tiles = pl.BlockSpec((3 * PER * PAIR, height, width), lambda g: (g, 0, 0))
+    line = pl.BlockSpec((3 * PER * PAIR * HALO, width), lambda g: (g, 0))
+    quarter = pl.BlockSpec((1, 3, height, width), lambda g: (PAIR * g // 4, 0, 0, 0))
+    corner = pl.BlockSpec((1, 3, 16, width), lambda g: (PAIR * g // 4, 0, 0, 0))
+    part = pl.BlockSpec((8, 128), lambda g: (0, 0))
     tiles = pltpu.VMEM((loads * 3, ext, width), F32)
     strips = pltpu.VMEM((groups, 3, ext, width), F32)
     own_shape = shape(loads * 3, height, width)
-    sums_shape = shape(16, 128)
+    sums_shape = shape(8, 128)
     sums_buffer = pltpu.VMEM((7, 128, 128), F32)
-    small = [pltpu.VMEM((PAIR, 3, ext, width), F32), pltpu.VMEM((3, ext, width), F32)]
+    small = [pltpu.VMEM((PAIR, 3, ext, width), F32)] * 2
     u0, u1, u2, u3, s0, s1, s2, s3, sums = pl.pallas_call(
         functools.partial(first_kernel, height),
-        grid=(groups,),
-        in_specs=[own_tile, line, line, quarter, quarter] + [corner] * 2 + [resident] * 2,
+        grid=(groups // PAIR,),
+        in_specs=[own_tiles, line, line, quarter, quarter] + [corner] * 2 + [resident] * 2,
         out_specs=[resident] * 8 + [part],
         out_shape=[tiles] * 4 + [strips] * 4 + [sums_shape],
         scratch_shapes=small + [pltpu.VMEM((2, 3, ext, width), F32), sums_buffer],
         compiler_params=params(),
     )(main, up, down, from_left, from_right, left_ends, right_ends, cm, cs)
-    totals = summed(sums)
-    fixed = part
+    totals = gathered(sums)
+    fixed = resident
     kept = pl.BlockSpec((32, 128), lambda g: (0, 0))
     w0, w1, w2, w3, sums, keep = pl.pallas_call(
         functools.partial(second_kernel, height),
-        grid=(groups,),
+        grid=(groups // PAIR,),
         in_specs=[fixed] + [resident] * 10,
         out_specs=[resident] * 4 + [part, kept],
         out_shape=[tiles] * 4 + [sums_shape, shape(32, 128)],
-        scratch_shapes=small + [pltpu.VMEM((128, 128), F32)] * 2 + [pltpu.VMEM((3, ext, width), F32)] * 3
+        scratch_shapes=small + [pltpu.VMEM((128, 128), F32)] * 2 + [pltpu.VMEM((PAIR, 3, ext, width), F32)] * 3
         + [sums_buffer],
         compiler_params=params(),
     )(totals, u0, u1, u2, u3, s0, s1, s2, s3, cm, cs)
-    totals = summed(sums)
+    totals = gathered(sums)
     x, r = pl.pallas_call(
         functools.partial(last_kernel, height),
         grid=(groups,),

time: 142 us -> 124 us (0.87)
  blocking collectives: 0 us -> 25.9 us
  waiting for transfers between devices: 38.6 us -> 18.5 us
  starting transfers between devices: 30.1 us -> 12.8 us
  local copies, waits for them, and re-layouts: 5.55 us -> 0.05 us
    all_to_all x0 -> x2, blocking collectives: none -> 25.9 us  [gathered(): lax.all_to_all(jnp.broadcast_to(x[None], (n,) + x.shape), ('gx', 'gy'), 0...]
    ppermute x10 -> x0, waiting for transfers between devices: 20.4 us -> none  [summed(): y = lax.ppermute(x, axis, [(i, i ^ d) for i in range(n)])]
    ppermute x10 -> x0, starting transfers between devices: 17.2 us -> none  [summed(): y = lax.ppermute(x, axis, [(i, i ^ d) for i in range(n)])]
    unnamed x16 -> x12, local copies, waits for them, and re-layouts: 5.55 us -> 0.03 us
    pallas_call x2, Pallas kernels: 52.1 us -> 49.5 us  [the longest x1 27.2 us: body(): pl.pallas_call(functools.partial(first_kernel, height), grid=(groups // P...]
    pallas_call x1, Pallas kernels: 0.23 us -> 2.58 us  [body(): pl.pallas_call(rows_kernel, grid=(1,), in_specs=[end_block(x, at) for at...]
  transfers between devices with their start and end apart: 16 -> 6, of which waited for: 13 -> 3; matrix products, arithmetic and copies ran while one was open for 0% -> 0% of each run, Pallas kernels for 4% -> 4%
where the time goes in v3:
time: 124 us
  Pallas kernels  66 us (53%)
  blocking collectives  25.9 us (21%)
  waiting for transfers between devices  18.5 us (15%)
  starting transfers between devices  12.8 us (10%)
    pallas_call x1, Pallas kernels, body(): pl.pallas_call(functools.partial(first_kernel, height), grid=(groups // P...  27.2 us
    all_to_all x2, blocking collectives, gathered(): lax.all_to_all(jnp.broadcast_to(x[None], (n,) + x.shape), ('gx', 'gy'), 0...  25.9 us
    pallas_call x1, Pallas kernels, body(): pl.pallas_call(functools.partial(second_kernel, height), grid=(groups //...  22.3 us
    ppermute x6, waiting for transfers between devices, moved(): lax.ppermute(block, axis, [(i, i + distance) for i in range(n) if 0 <= i...  18.5 us
    ppermute x6, starting transfers between devices, moved(): lax.ppermute(block, axis, [(i, i + distance) for i in range(n) if 0 <= i...  12.8 us
    pallas_call x1, Pallas kernels, body(): pl.pallas_call(functools.partial(last_kernel, height), grid=(groups,), in...  7.23 us
    pallas_call x2, Pallas kernels, send_columns(): pl.pallas_call(kernel, grid=(count,), in_specs=in_specs, out_specs=[part]...  5.13 us
    pallas_call x1, Pallas kernels, body(): pl.pallas_call(rows_kernel, grid=(1,), in_specs=[end_block(x, at) for at...  2.58 us
  transfers between devices with their start and end apart: 6, of which 3 were waited for; matrix products, arithmetic and copies ran while one was open for 0% of the time, Pallas kernels for 4%

profile of v3, /device:TPU:0, one launch (start us, length us, event | category | flops | bytes accessed | tf_op | source)
XLA Modules:
  0.0 124.0 jit_solution(6939062755037890124)
XLA Ops:
  0.6 0.0 copy-start.5
  0.6 0.0 copy-start.4
  0.7 0.0 copy-start.1
  0.7 0.0 copy-start.3
  0.7 0.0 copy-start.2
  0.7 0.0 copy-start
  0.7 2.6 %shard_map.77 = (f32[972,128]{1,0:T(8,128)}, f32[972,128]{1,0:T(8,128)}) custom-call(f32[144,32,128]{2,1,0:T(8,128)} %bitcast.3, f32[2,32,128]{2,1,0:T(8,128)} %stiffness.1, f32[2,32,128]{2,1,0:T(8,128)} %coupling.1, f32[12,32,128]{2,1,0:T(8,128)} %edges.1, s32[32,128]{1,0:T(8,128)} %flip.1, s32[32,128]{1,0:T(8,128)} %pinned.1, f32[144,32,128]{2,1,0:T(8,128)} %bitcast.4, ...), custom_call_target="tpu_custom_call" | custom-call | tf_op jit(solution)/shard_map/pallas_call | solution.py:724
  3.3 1.3 %collective-permute-start = (f32[972,128]{1,0:T(8,128)}, f32[972,128]{1,0:T(8,128)S(1)}, u32[]{:S(2)}, u32[]{:S(2)}) collective-permute-start(f32[972,128]{1,0:T(8,128)} %get-tuple-element.27), channel_id=1, source_target_pairs={{4,0},{8,4},{12,8},{16,12},{20,16},{24,20},{28,24},{5,1},{9,5},{13... | collective-permute-start | bytes 1493000 | tf_op jit(solution)/shard_map/ppermute | solution.py:694
  4.6 5.5 %collective-permute-start.1 = (f32[972,128]{1,0:T(8,128)}, f32[972,128]{1,0:T(8,128)S(1)}, u32[]{:S(2)}, u32[]{:S(2)}) collective-permute-start(f32[972,128]{1,0:T(8,128)} %get-tuple-element.28), channel_id=1, source_target_pairs={{0,4},{4,8},{8,12},{12,16},{16,20},{20,24},{24,28},{1,5},{5,9},{9,... | collective-permute-start | bytes 1493000 | tf_op jit(solution)/shard_map/ppermute | solution.py:694
  10.1 0.0 copy-done.5
  10.1 0.0 copy-done.4
  10.1 0.0 copy-done.1
  10.1 0.0 copy-done.3
  10.1 0.0 copy-done.2
  10.1 0.0 copy-done
  10.1 2.3 %shard_map.78 = (f32[5,3,32,128]{3,2,1,0:T(8,128)S(1)}, f32[5,3,32,128]{3,2,1,0:T(8,128)S(1)}) custom-call(f32[144,32,128]{2,1,0:T(8,128)S(1)} %bitcast.5, f32[2,32,128]{2,1,0:T(8,128)S(1)} %copy-done.2, f32[2,32,128]{2,1,0:T(8,128)S(1)} %copy-done.3, f32[12,32,128]{2,1,0:T(8,128)S(1)} %copy-done.1, s32[32,128]{1,0:T(8,128)S(1)} %copy-done.4, ...), custom_call_target="tpu_custom_call" | custom-call | tf_op jit(solution)/shard_map/pallas_call | solution.py:740
  12.4 1.5 %collective-permute-start.2 = (f32[5,3,32,128]{3,2,1,0:T(8,128)S(1)}, f32[5,3,32,128]{3,2,1,0:T(8,128)S(1)}, u32[]{:S(2)}, u32[]{:S(2)}) collective-permute-start(f32[5,3,32,128]{3,2,1,0:T(8,128)S(1)} %get-tuple-element.29), channel_id=1, source_target_pairs={{0,1},{1,2},{2,3},{4,5},{5,6},{6,7},{8,9},{9,10},{10,11},{12,13},{... | collective-permute-start | bytes 737288 | tf_op jit(solution)/shard_map/ppermute | solution.py:694
  13.9 1.3 %collective-permute-start.3 = (f32[5,3,32,128]{3,2,1,0:T(8,128)S(1)}, f32[5,3,32,128]{3,2,1,0:T(8,128)S(1)}, u32[]{:S(2)}, u32[]{:S(2)}) collective-permute-start(f32[5,3,32,128]{3,2,1,0:T(8,128)S(1)} %get-tuple-element.30), channel_id=1, source_target_pairs={{1,0},{2,1},{3,2},{5,4},{6,5},{7,6},{9,8},{10,9},{11,10},{13,12},{... | collective-permute-start | bytes 737288 | tf_op jit(solution)/shard_map/ppermute | solution.py:694
  15.2 4.5 %collective-permute-done.up_ref.all_up = f32[972,128]{1,0:T(8,128)S(1)} collective-permute-done((f32[972,128]{1,0:T(8,128)}, f32[972,128]{1,0:T(8,128)S(1)}, u32[]{:S(2)}, u32[]{:S(2)}) %collective-permute-start) | collective-permute-done | bytes 497696 | tf_op jit(solution)/shard_map/ppermute | solution.py:694
  19.7 11.0 %collective-permute-done.1.down_ref.all_down = f32[972,128]{1,0:T(8,128)S(1)} collective-permute-done((f32[972,128]{1,0:T(8,128)}, f32[972,128]{1,0:T(8,128)S(1)}, u32[]{:S(2)}, u32[]{:S(2)}) %collective-permute-start.1) | collective-permute-done | bytes 497696 | tf_op jit(solution)/shard_map/ppermute | solution.py:694
  30.7 2.9 %shard_map.79 = (f32[5,3,16,128]{3,2,1,0:T(8,128)S(1)}, f32[5,3,16,128]{3,2,1,0:T(8,128)S(1)}) custom-call(f32[972,128]{1,0:T(8,128)S(1)} %collective-permute-done.1.down_ref.all_down, f32[972,128]{1,0:T(8,128)S(1)} %collective-permute-done.up_ref.all_up, f32[972,128]{1,0:T(8,128)S(1)} %collective-permute-done.1.down_ref.all_down, ...), custom_call_target="tpu_custom_call" | custom-call | tf_op jit(solution)/shard_map/pallas_call | solution.py:740
  33.5 1.9 %collective-permute-start.4 = (f32[5,3,16,128]{3,2,1,0:T(8,128)S(1)}, f32[5,3,16,128]{3,2,1,0:T(8,128)S(1)}, u32[]{:S(2)}, u32[]{:S(2)}) collective-permute-start(f32[5,3,16,128]{3,2,1,0:T(8,128)S(1)} %get-tuple-element.31), channel_id=1, source_target_pairs={{0,1},{1,2},{2,3},{4,5},{5,6},{6,7},{8,9},{9,10},{10,11},{12,13},{... | collective-permute-start | bytes 368648 | tf_op jit(solution)/shard_map/ppermute | solution.py:694
  35.5 1.3 %collective-permute-start.5 = (f32[5,3,16,128]{3,2,1,0:T(8,128)S(1)}, f32[5,3,16,128]{3,2,1,0:T(8,128)S(1)}, u32[]{:S(2)}, u32[]{:S(2)}) collective-permute-start(f32[5,3,16,128]{3,2,1,0:T(8,128)S(1)} %get-tuple-element.32), channel_id=1, source_target_pairs={{1,0},{2,1},{3,2},{5,4},{6,5},{7,6},{9,8},{10,9},{11,10},{13,12},{... | collective-permute-start | bytes 368648 | tf_op jit(solution)/shard_map/ppermute | solution.py:694
  36.8 0.0 collective-permute-done.2.left_ref
  36.8 0.0 collective-permute-done.3.right_ref
  36.8 0.0 collective-permute-done.4.left_ends
  36.8 3.0 %collective-permute-done.5.right_ends = f32[5,3,16,128]{3,2,1,0:T(8,128)S(1)} collective-permute-done((f32[5,3,16,128]{3,2,1,0:T(8,128)S(1)}, f32[5,3,16,128]{3,2,1,0:T(8,128)S(1)}, u32[]{:S(2)}, u32[]{:S(2)}) %collective-permute-start.5) | collective-permute-done | bytes 122912 | tf_op jit(solution)/shard_map/ppermute | solution.py:694
  39.8 1.5 %shard_map.80 = (f32[20,56,128]{2,1,0:T(8,128)S(1)}, f32[20,56,128]{2,1,0:T(8,128)S(1)}) custom-call(f32[2,32,128]{2,1,0:T(8,128)S(1)} %copy-done.2, f32[2,32,128]{2,1,0:T(8,128)S(1)} %copy-done.3, f32[12,32,128]{2,1,0:T(8,128)S(1)} %copy-done.1, s32[32,128]{1,0:T(8,128)S(1)} %copy-done.4, s32[32,128]{1,0:T(8,128)S(1)} %copy-done.5, ...), custom_call_target="tpu_custom_call" | custom-call | tf_op jit(solution)/shard_map/pallas_call | solution.py:763
  41.3 27.2 %shard_map.81 = (f32[144,56,128]{2,1,0:T(8,128)S(1)}, f32[144,56,128]{2,1,0:T(8,128)S(1)}, f32[144,56,128]{2,1,0:T(8,128)S(1)}, f32[144,56,128]{2,1,0:T(8,128)S(...) custom-call(f32[144,32,128]{2,1,0:T(8,128)S(1)} %bitcast.6, ...), custom_call_target="tpu_custom_call" | custom-call | tf_op jit(solution)/shard_map/pallas_call | solution.py:782
  68.6 15.9 %all_to_all.10.totals_ref = f32[32,8,128]{2,1,0:T(8,128)S(1)} all-to-all(f32[32,8,128]{2,1,0:T(8,128)S(1)} %broadcast_in_dim.4), channel_id=1, replica_groups=mesh['gx'=8,'gy'=4] {'gx','gy'}, dimensions={0} | all-to-all | bytes 262144 | tf_op jit(solution)/shard_map/all_to_all | solution.py:699
  84.4 22.3 %shard_map.82 = (f32[144,56,128]{2,1,0:T(8,128)S(1)}, f32[144,56,128]{2,1,0:T(8,128)S(1)}, f32[144,56,128]{2,1,0:T(8,128)S(1)}, f32[144,56,128]{2,1,0:T(8,128)S(...) custom-call(f32[32,8,128]{2,1,0:T(8,128)S(1)} %all_to_all.10.totals_ref, f32[144,56,128]{2,1,0:T(8,128)S(1)} %get-tuple-element.36.u0_all, ...), custom_call_target="tpu_custom_call" | custom-call | tf_op jit(solution)/shard_map/pallas_call | solution.py:794
  106.8 10.0 %all_to_all.11.totals_ref = f32[32,8,128]{2,1,0:T(8,128)S(1)} all-to-all(f32[32,8,128]{2,1,0:T(8,128)S(1)} %broadcast_in_dim.5), channel_id=1, replica_groups=mesh['gx'=8,'gy'=4] {'gx','gy'}, dimensions={0} | all-to-all | bytes 262144 | tf_op jit(solution)/shard_map/all_to_all | solution.py:699
  116.8 7.2 %shard_map.83 = (f32[144,32,128]{2,1,0:T(8,128)}, f32[144,32,128]{2,1,0:T(8,128)}) custom-call(f32[32,8,128]{2,1,0:T(8,128)S(1)} %all_to_all.11.totals_ref, f32[32,128]{1,0:T(8,128)S(1)} %get-tuple-element.45.keep_ref, f32[144,32,128]{2,1,0:T(8,128)S(1)} %bitcast.7, f32[144,56,128]{2,1,0:T(8,128)S(1)} %get-tuple-element.36.u0_all, ...), custom_call_target="tpu_custom_call" | custom-call | tf_op jit(solution)/shard_map/pallas_call | solution.py:805
  (2 shorter events, 0.0 us)
Async XLA Ops:
  0.6 9.4 %copy-start.5 = (s32[32,128]{1,0:T(8,128)S(1)}, s32[32,128]{1,0:T(8,128)}, u32[]{:S(2)}) copy-start(s32[32,128]{1,0:T(8,128)} %pinned.1) | copy-start | bytes 49156
  0.6 9.4 %copy-start.4 = (s32[32,128]{1,0:T(8,128)S(1)}, s32[32,128]{1,0:T(8,128)}, u32[]{:S(2)}) copy-start(s32[32,128]{1,0:T(8,128)} %flip.1) | copy-start | bytes 49156
  0.7 9.4 %copy-start.1 = (f32[12,32,128]{2,1,0:T(8,128)S(1)}, f32[12,32,128]{2,1,0:T(8,128)}, u32[]{:S(2)}) copy-start(f32[12,32,128]{2,1,0:T(8,128)} %edges.1) | copy-start | bytes 589828
  0.7 9.4 %copy-start.3 = (f32[2,32,128]{2,1,0:T(8,128)S(1)}, f32[2,32,128]{2,1,0:T(8,128)}, u32[]{:S(2)}) copy-start(f32[2,32,128]{2,1,0:T(8,128)} %coupling.1) | copy-start | bytes 98308
  0.7 9.4 %copy-start.2 = (f32[2,32,128]{2,1,0:T(8,128)S(1)}, f32[2,32,128]{2,1,0:T(8,128)}, u32[]{:S(2)}) copy-start(f32[2,32,128]{2,1,0:T(8,128)} %stiffness.1) | copy-start | bytes 98308
  0.7 9.4 %copy-start = (f32[48,3,32,128]{3,2,1,0:T(8,128)S(1)}, f32[48,3,32,128]{3,2,1,0:T(8,128)}, u32[]{:S(2)}) copy-start(f32[48,3,32,128]{3,2,1,0:T(8,128)} %param.6) | copy-start | bytes 7077892
  3.3 16.4 %collective-permute-start = (f32[972,128]{1,0:T(8,128)}, f32[972,128]{1,0:T(8,128)S(1)}, u32[]{:S(2)}, u32[]{:S(2)}) collective-permute-start(f32[972,128]{1,0:T(8,128)} %get-tuple-element.27), channel_id=1, source_target_pairs={{4,0},{8,4},{12,8},{16,12},{20,16},{24,20},{28,24},{5,1},{9,5},{13... | collective-permute-start | bytes 1493000 | tf_op jit(solution)/shard_map/ppermute | solution.py:694
  4.6 26.1 %collective-permute-start.1 = (f32[972,128]{1,0:T(8,128)}, f32[972,128]{1,0:T(8,128)S(1)}, u32[]{:S(2)}, u32[]{:S(2)}) collective-permute-start(f32[972,128]{1,0:T(8,128)} %get-tuple-element.28), channel_id=1, source_target_pairs={{0,4},{4,8},{8,12},{12,16},{16,20},{20,24},{24,28},{1,5},{5,9},{9,... | collective-permute-start | bytes 1493000 | tf_op jit(solution)/shard_map/ppermute | solution.py:694
  12.4 24.4 %collective-permute-start.2 = (f32[5,3,32,128]{3,2,1,0:T(8,128)S(1)}, f32[5,3,32,128]{3,2,1,0:T(8,128)S(1)}, u32[]{:S(2)}, u32[]{:S(2)}) collective-permute-start(f32[5,3,32,128]{3,2,1,0:T(8,128)S(1)} %get-tuple-element.29), channel_id=1, source_target_pairs={{0,1},{1,2},{2,3},{4,5},{5,6},{6,7},{8,9},{9,10},{10,11},{12,13},{... | collective-permute-start | bytes 737288 | tf_op jit(solution)/shard_map/ppermute | solution.py:694
  13.9 22.9 %collective-permute-start.3 = (f32[5,3,32,128]{3,2,1,0:T(8,128)S(1)}, f32[5,3,32,128]{3,2,1,0:T(8,128)S(1)}, u32[]{:S(2)}, u32[]{:S(2)}) collective-permute-start(f32[5,3,32,128]{3,2,1,0:T(8,128)S(1)} %get-tuple-element.30), channel_id=1, source_target_pairs={{1,0},{2,1},{3,2},{5,4},{6,5},{7,6},{9,8},{10,9},{11,10},{13,12},{... | collective-permute-start | bytes 737288 | tf_op jit(solution)/shard_map/ppermute | solution.py:694
  33.5 3.2 %collective-permute-start.4 = (f32[5,3,16,128]{3,2,1,0:T(8,128)S(1)}, f32[5,3,16,128]{3,2,1,0:T(8,128)S(1)}, u32[]{:S(2)}, u32[]{:S(2)}) collective-permute-start(f32[5,3,16,128]{3,2,1,0:T(8,128)S(1)} %get-tuple-element.31), channel_id=1, source_target_pairs={{0,1},{1,2},{2,3},{4,5},{5,6},{6,7},{8,9},{9,10},{10,11},{12,13},{... | collective-permute-start | bytes 368648 | tf_op jit(solution)/shard_map/ppermute | solution.py:694
  35.5 4.3 %collective-permute-start.5 = (f32[5,3,16,128]{3,2,1,0:T(8,128)S(1)}, f32[5,3,16,128]{3,2,1,0:T(8,128)S(1)}, u32[]{:S(2)}, u32[]{:S(2)}) collective-permute-start(f32[5,3,16,128]{3,2,1,0:T(8,128)S(1)} %get-tuple-element.32), channel_id=1, source_target_pairs={{1,0},{2,1},{3,2},{5,4},{6,5},{7,6},{9,8},{10,9},{11,10},{13,12},{... | collective-permute-start | bytes 368648 | tf_op jit(solution)/shard_map/ppermute | solution.py:694

commit v4 on v3

--- a/solution.py
+++ b/solution.py
@@ -674,19 +674,22 @@
     )
 
 
-def ends_kernel(merged, fields, down_ref, up_ref, all_down, all_up, right_ref, left_ref, one):
-    one[...] = jnp.zeros(one.shape, F32)
-
-    def load_rows(k, r):
-        one[0:HALO, :] = (down_ref, up_ref)[r // 8][k * HALO:(k + 1) * HALO, :]
-        return one[...]
-
-    def raw_rows(k, r):
-        k = k + fields
-        one[0:HALO, :] = (all_down, all_up)[r // 8][k * HALO:(k + 1) * HALO, :]
-        return one[...]
-
-    each_group(merged, load_rows, raw_rows, (0, 8), (right_ref, left_ref))
+def ends_kernel(merged, loads, down_ref, up_ref, right_ref, left_ref):
+    stop = down_ref.shape[0]
+
+    def rows_at(k, r):
+        ref = (down_ref, up_ref)[r // 8]
+        if k * HALO + 8 > stop:
+            return pltpu.roll(ref[stop - 8:stop, :], HALO, 0)
+        return ref[k * HALO:k * HALO + 8, :]
+
+    for h in range(merged):
+        cut(lambda q, i, c, r: rows_at(3 * (PER * (4 * h + q) + i) + c, r), (0, 8), 4,
+            right_ref.at[h:h + 1], left_ref.at[h:h + 1])
+    for p in (0, 4):
+        h = merged + p // 4
+        cut(lambda q, i, c, r: rows_at(3 * (loads + p + q) + c, r), (0, 8), min(4, 6 - p),
+            right_ref.at[h:h + 1], left_ref.at[h:h + 1])
 
 
 def moved(block, axis, distance):
@@ -735,31 +738,24 @@
     count = merged + 2
     wide = 4 * 3 * PER
 
-    def send_columns(kernel, in_specs, rows, scratch, *operands):
-        part = pl.BlockSpec((1, 3, rows, width), lambda h: (h, 0, 0, 0))
-        right, left = pl.pallas_call(
-            kernel,
-            grid=(count,),
-            in_specs=in_specs,
-            out_specs=[part] * 2,
-            out_shape=[shape(count, 3, rows, width)] * 2,
-            scratch_shapes=scratch,
-            compiler_params=params(),
-        )(*operands)
+    def sent(right, left):
         return moved(right, "gy", 1), moved(left, "gy", -1)
 
     resident = pl.BlockSpec(memory_space=pltpu.VMEM)
-    from_left, from_right = send_columns(
+    part = pl.BlockSpec((1, 3, height, width), lambda h: (h, 0, 0, 0))
+    from_left, from_right = sent(*pl.pallas_call(
         functools.partial(columns_kernel, merged, height),
-        [pl.BlockSpec((wide, height, width), lambda h: (jnp.minimum(h, merged - 1), 0, 0))] + [resident] * 5,
-        height, [], main, *raw,
-    )
-    line = pl.BlockSpec((wide * HALO, width), lambda h: (jnp.minimum(h, merged - 1), 0))
-    left_ends, right_ends = send_columns(
-        functools.partial(ends_kernel, merged, loads * 3),
-        [line] * 2 + [resident] * 2,
-        16, [pltpu.VMEM((8, width), F32)], down, up, down, up,
-    )
+        grid=(count,),
+        in_specs=[pl.BlockSpec((wide, height, width), lambda h: (jnp.minimum(h, merged - 1), 0, 0))] + [resident] * 5,
+        out_specs=[part] * 2,
+        out_shape=[shape(count, 3, height, width)] * 2,
+        compiler_params=params(),
+    )(main, *raw))
+    left_ends, right_ends = sent(*pl.pallas_call(
+        functools.partial(ends_kernel, merged, loads),
+        out_shape=[shape(count, 3, 16, width)] * 2,
+        compiler_params=params(),
+    )(down, up))
     cm, cs = pl.pallas_call(
         functools.partial(prepare_kernel, loads, merged),
         out_shape=[shape(NCOEF, ext, width), shape(NCOEF, ext, width)],

time: 124 us -> 122 us (0.984)
  Pallas kernels: 66 us -> 64 us
    pallas_call x2, Pallas kernels: 5.13 us -> 3.2 us  [the longest x1 2.26 us: body(): pl.pallas_call(functools.partial(columns_kernel, merged, height), grid=(c...]
  transfers between devices with their start and end apart: 6 -> 6, of which waited for: 3 -> 3; matrix products, arithmetic and copies ran while one was open for 0% -> 0% of each run, Pallas kernels for 4% -> 3%
where the time goes in v4:
time: 122 us
  Pallas kernels  64 us (52%)
  blocking collectives  25.9 us (21%)
  waiting for transfers between devices  18.5 us (15%)
  starting transfers between devices  12.8 us (10%)
    pallas_call x1, Pallas kernels, body(): pl.pallas_call(functools.partial(first_kernel, height), grid=(groups // P...  27.2 us
    all_to_all x2, blocking collectives, gathered(): lax.all_to_all(jnp.broadcast_to(x[None], (n,) + x.shape), ('gx', 'gy'), 0...  25.9 us
    pallas_call x1, Pallas kernels, body(): pl.pallas_call(functools.partial(second_kernel, height), grid=(groups //...  22.3 us
    ppermute x6, waiting for transfers between devices, moved(): lax.ppermute(block, axis, [(i, i + distance) for i in range(n) if 0 <= i...  18.5 us
    ppermute x6, starting transfers between devices, moved(): lax.ppermute(block, axis, [(i, i + distance) for i in range(n) if 0 <= i...  12.8 us
    pallas_call x1, Pallas kernels, body(): pl.pallas_call(functools.partial(last_kernel, height), grid=(groups,), in...  7.23 us
    pallas_call x1, Pallas kernels, body(): pl.pallas_call(rows_kernel, grid=(1,), in_specs=[end_block(x, at) for at...  2.58 us
  transfers between devices with their start and end apart: 6, of which 3 were waited for; matrix products, arithmetic and copies ran while one was open for 0% of the time, Pallas kernels for 3%

profile of v4, /device:TPU:0, one launch (start us, length us, event | category | flops | bytes accessed | tf_op | source)
XLA Modules:
  0.0 122.1 jit_solution(232254092553024567)
XLA Ops:
  0.6 0.0 copy-start.5
  0.6 0.0 copy-start.4
  0.7 0.0 copy-start.1
  0.7 0.0 copy-start.3
  0.7 0.0 copy-start.2
  0.7 0.0 copy-start
  0.7 2.6 %shard_map.77 = (f32[972,128]{1,0:T(8,128)}, f32[972,128]{1,0:T(8,128)}) custom-call(f32[144,32,128]{2,1,0:T(8,128)} %bitcast.3, f32[2,32,128]{2,1,0:T(8,128)} %stiffness.1, f32[2,32,128]{2,1,0:T(8,128)} %coupling.1, f32[12,32,128]{2,1,0:T(8,128)} %edges.1, s32[32,128]{1,0:T(8,128)} %flip.1, s32[32,128]{1,0:T(8,128)} %pinned.1, f32[144,32,128]{2,1,0:T(8,128)} %bitcast.4, ...), custom_call_target="tpu_custom_call" | custom-call | tf_op jit(solution)/shard_map/pallas_call | solution.py:727
  3.3 1.3 %collective-permute-start = (f32[972,128]{1,0:T(8,128)}, f32[972,128]{1,0:T(8,128)S(1)}, u32[]{:S(2)}, u32[]{:S(2)}) collective-permute-start(f32[972,128]{1,0:T(8,128)} %get-tuple-element.27), channel_id=1, source_target_pairs={{4,0},{8,4},{12,8},{16,12},{20,16},{24,20},{28,24},{5,1},{9,5},{13... | collective-permute-start | bytes 1493000 | tf_op jit(solution)/shard_map/ppermute | solution.py:697
  4.6 5.5 %collective-permute-start.1 = (f32[972,128]{1,0:T(8,128)}, f32[972,128]{1,0:T(8,128)S(1)}, u32[]{:S(2)}, u32[]{:S(2)}) collective-permute-start(f32[972,128]{1,0:T(8,128)} %get-tuple-element.28), channel_id=1, source_target_pairs={{0,4},{4,8},{8,12},{12,16},{16,20},{20,24},{24,28},{1,5},{5,9},{9,... | collective-permute-start | bytes 1493000 | tf_op jit(solution)/shard_map/ppermute | solution.py:697
  10.1 0.0 copy-done.5
  10.1 0.0 copy-done.4
  10.1 0.0 copy-done.1
  10.1 0.0 copy-done.3
  10.1 0.0 copy-done.2
  10.1 0.0 copy-done
  10.1 2.3 %shard_map.78 = (f32[5,3,32,128]{3,2,1,0:T(8,128)S(1)}, f32[5,3,32,128]{3,2,1,0:T(8,128)S(1)}) custom-call(f32[144,32,128]{2,1,0:T(8,128)S(1)} %bitcast.5, f32[2,32,128]{2,1,0:T(8,128)S(1)} %copy-done.2, f32[2,32,128]{2,1,0:T(8,128)S(1)} %copy-done.3, f32[12,32,128]{2,1,0:T(8,128)S(1)} %copy-done.1, s32[32,128]{1,0:T(8,128)S(1)} %copy-done.4, ...), custom_call_target="tpu_custom_call" | custom-call | tf_op jit(solution)/shard_map/pallas_call | solution.py:746
  12.4 1.5 %collective-permute-start.2 = (f32[5,3,32,128]{3,2,1,0:T(8,128)S(1)}, f32[5,3,32,128]{3,2,1,0:T(8,128)S(1)}, u32[]{:S(2)}, u32[]{:S(2)}) collective-permute-start(f32[5,3,32,128]{3,2,1,0:T(8,128)S(1)} %get-tuple-element.29), channel_id=1, source_target_pairs={{0,1},{1,2},{2,3},{4,5},{5,6},{6,7},{8,9},{9,10},{10,11},{12,13},{... | collective-permute-start | bytes 737288 | tf_op jit(solution)/shard_map/ppermute | solution.py:697
  13.9 1.3 %collective-permute-start.3 = (f32[5,3,32,128]{3,2,1,0:T(8,128)S(1)}, f32[5,3,32,128]{3,2,1,0:T(8,128)S(1)}, u32[]{:S(2)}, u32[]{:S(2)}) collective-permute-start(f32[5,3,32,128]{3,2,1,0:T(8,128)S(1)} %get-tuple-element.30), channel_id=1, source_target_pairs={{1,0},{2,1},{3,2},{5,4},{6,5},{7,6},{9,8},{10,9},{11,10},{13,12},{... | collective-permute-start | bytes 737288 | tf_op jit(solution)/shard_map/ppermute | solution.py:697
  15.2 4.5 %collective-permute-done.up_ref = f32[972,128]{1,0:T(8,128)S(1)} collective-permute-done((f32[972,128]{1,0:T(8,128)}, f32[972,128]{1,0:T(8,128)S(1)}, u32[]{:S(2)}, u32[]{:S(2)}) %collective-permute-start) | collective-permute-done | bytes 497696 | tf_op jit(solution)/shard_map/ppermute | solution.py:697
  19.7 11.0 %collective-permute-done.1.down_ref = f32[972,128]{1,0:T(8,128)S(1)} collective-permute-done((f32[972,128]{1,0:T(8,128)}, f32[972,128]{1,0:T(8,128)S(1)}, u32[]{:S(2)}, u32[]{:S(2)}) %collective-permute-start.1) | collective-permute-done | bytes 497696 | tf_op jit(solution)/shard_map/ppermute | solution.py:697
  30.7 0.9 shard_map.79
  31.6 1.9 %collective-permute-start.4 = (f32[5,3,16,128]{3,2,1,0:T(8,128)S(1)}, f32[5,3,16,128]{3,2,1,0:T(8,128)S(1)}, u32[]{:S(2)}, u32[]{:S(2)}) collective-permute-start(f32[5,3,16,128]{3,2,1,0:T(8,128)S(1)} %get-tuple-element.31), channel_id=1, source_target_pairs={{0,1},{1,2},{2,3},{4,5},{5,6},{6,7},{8,9},{9,10},{10,11},{12,13},{... | collective-permute-start | bytes 368648 | tf_op jit(solution)/shard_map/ppermute | solution.py:697
  33.6 1.3 %collective-permute-start.5 = (f32[5,3,16,128]{3,2,1,0:T(8,128)S(1)}, f32[5,3,16,128]{3,2,1,0:T(8,128)S(1)}, u32[]{:S(2)}, u32[]{:S(2)}) collective-permute-start(f32[5,3,16,128]{3,2,1,0:T(8,128)S(1)} %get-tuple-element.32), channel_id=1, source_target_pairs={{1,0},{2,1},{3,2},{5,4},{6,5},{7,6},{9,8},{10,9},{11,10},{13,12},{... | collective-permute-start | bytes 368648 | tf_op jit(solution)/shard_map/ppermute | solution.py:697
  34.9 0.0 collective-permute-done.2.left_ref
  34.9 0.0 collective-permute-done.3.right_ref
  34.9 0.0 collective-permute-done.4.left_ends
  34.9 3.0 %collective-permute-done.5.right_ends = f32[5,3,16,128]{3,2,1,0:T(8,128)S(1)} collective-permute-done((f32[5,3,16,128]{3,2,1,0:T(8,128)S(1)}, f32[5,3,16,128]{3,2,1,0:T(8,128)S(1)}, u32[]{:S(2)}, u32[]{:S(2)}) %collective-permute-start.5) | collective-permute-done | bytes 122912 | tf_op jit(solution)/shard_map/ppermute | solution.py:697
  37.9 1.5 %shard_map.80 = (f32[20,56,128]{2,1,0:T(8,128)S(1)}, f32[20,56,128]{2,1,0:T(8,128)S(1)}) custom-call(f32[2,32,128]{2,1,0:T(8,128)S(1)} %copy-done.2, f32[2,32,128]{2,1,0:T(8,128)S(1)} %copy-done.3, f32[12,32,128]{2,1,0:T(8,128)S(1)} %copy-done.1, s32[32,128]{1,0:T(8,128)S(1)} %copy-done.4, s32[32,128]{1,0:T(8,128)S(1)} %copy-done.5, ...), custom_call_target="tpu_custom_call" | custom-call | tf_op jit(solution)/shard_map/pallas_call | solution.py:759
  39.4 27.2 %shard_map.81 = (f32[144,56,128]{2,1,0:T(8,128)S(1)}, f32[144,56,128]{2,1,0:T(8,128)S(1)}, f32[144,56,128]{2,1,0:T(8,128)S(1)}, f32[144,56,128]{2,1,0:T(8,128)S(...) custom-call(f32[144,32,128]{2,1,0:T(8,128)S(1)} %bitcast.6, ...), custom_call_target="tpu_custom_call" | custom-call | tf_op jit(solution)/shard_map/pallas_call | solution.py:778
  66.7 15.9 %all_to_all.10.totals_ref = f32[32,8,128]{2,1,0:T(8,128)S(1)} all-to-all(f32[32,8,128]{2,1,0:T(8,128)S(1)} %broadcast_in_dim.4), channel_id=1, replica_groups=mesh['gx'=8,'gy'=4] {'gx','gy'}, dimensions={0} | all-to-all | bytes 262144 | tf_op jit(solution)/shard_map/all_to_all | solution.py:702
  82.5 22.3 %shard_map.82 = (f32[144,56,128]{2,1,0:T(8,128)S(1)}, f32[144,56,128]{2,1,0:T(8,128)S(1)}, f32[144,56,128]{2,1,0:T(8,128)S(1)}, f32[144,56,128]{2,1,0:T(8,128)S(...) custom-call(f32[32,8,128]{2,1,0:T(8,128)S(1)} %all_to_all.10.totals_ref, f32[144,56,128]{2,1,0:T(8,128)S(1)} %get-tuple-element.36.u0_all, ...), custom_call_target="tpu_custom_call" | custom-call | tf_op jit(solution)/shard_map/pallas_call | solution.py:790
  104.8 10.0 %all_to_all.11.totals_ref = f32[32,8,128]{2,1,0:T(8,128)S(1)} all-to-all(f32[32,8,128]{2,1,0:T(8,128)S(1)} %broadcast_in_dim.5), channel_id=1, replica_groups=mesh['gx'=8,'gy'=4] {'gx','gy'}, dimensions={0} | all-to-all | bytes 262144 | tf_op jit(solution)/shard_map/all_to_all | solution.py:702
  114.8 7.2 %shard_map.83 = (f32[144,32,128]{2,1,0:T(8,128)}, f32[144,32,128]{2,1,0:T(8,128)}) custom-call(f32[32,8,128]{2,1,0:T(8,128)S(1)} %all_to_all.11.totals_ref, f32[32,128]{1,0:T(8,128)S(1)} %get-tuple-element.45.keep_ref, f32[144,32,128]{2,1,0:T(8,128)S(1)} %bitcast.7, f32[144,56,128]{2,1,0:T(8,128)S(1)} %get-tuple-element.36.u0_all, ...), custom_call_target="tpu_custom_call" | custom-call | tf_op jit(solution)/shard_map/pallas_call | solution.py:801
  (2 shorter events, 0.0 us)
Async XLA Ops:
  0.6 9.4 %copy-start.5 = (s32[32,128]{1,0:T(8,128)S(1)}, s32[32,128]{1,0:T(8,128)}, u32[]{:S(2)}) copy-start(s32[32,128]{1,0:T(8,128)} %pinned.1) | copy-start | bytes 49156
  0.6 9.4 %copy-start.4 = (s32[32,128]{1,0:T(8,128)S(1)}, s32[32,128]{1,0:T(8,128)}, u32[]{:S(2)}) copy-start(s32[32,128]{1,0:T(8,128)} %flip.1) | copy-start | bytes 49156
  0.7 9.4 %copy-start.1 = (f32[12,32,128]{2,1,0:T(8,128)S(1)}, f32[12,32,128]{2,1,0:T(8,128)}, u32[]{:S(2)}) copy-start(f32[12,32,128]{2,1,0:T(8,128)} %edges.1) | copy-start | bytes 589828
  0.7 9.4 %copy-start.3 = (f32[2,32,128]{2,1,0:T(8,128)S(1)}, f32[2,32,128]{2,1,0:T(8,128)}, u32[]{:S(2)}) copy-start(f32[2,32,128]{2,1,0:T(8,128)} %coupling.1) | copy-start | bytes 98308
  0.7 9.4 %copy-start.2 = (f32[2,32,128]{2,1,0:T(8,128)S(1)}, f32[2,32,128]{2,1,0:T(8,128)}, u32[]{:S(2)}) copy-start(f32[2,32,128]{2,1,0:T(8,128)} %stiffness.1) | copy-start | bytes 98308
  0.7 9.4 %copy-start = (f32[48,3,32,128]{3,2,1,0:T(8,128)S(1)}, f32[48,3,32,128]{3,2,1,0:T(8,128)}, u32[]{:S(2)}) copy-start(f32[48,3,32,128]{3,2,1,0:T(8,128)} %param.6) | copy-start | bytes 7077892
  3.3 16.4 %collective-permute-start = (f32[972,128]{1,0:T(8,128)}, f32[972,128]{1,0:T(8,128)S(1)}, u32[]{:S(2)}, u32[]{:S(2)}) collective-permute-start(f32[972,128]{1,0:T(8,128)} %get-tuple-element.27), channel_id=1, source_target_pairs={{4,0},{8,4},{12,8},{16,12},{20,16},{24,20},{28,24},{5,1},{9,5},{13... | collective-permute-start | bytes 1493000 | tf_op jit(solution)/shard_map/ppermute | solution.py:697
  4.6 26.1 %collective-permute-start.1 = (f32[972,128]{1,0:T(8,128)}, f32[972,128]{1,0:T(8,128)S(1)}, u32[]{:S(2)}, u32[]{:S(2)}) collective-permute-start(f32[972,128]{1,0:T(8,128)} %get-tuple-element.28), channel_id=1, source_target_pairs={{0,4},{4,8},{8,12},{12,16},{16,20},{20,24},{24,28},{1,5},{5,9},{9,... | collective-permute-start | bytes 1493000 | tf_op jit(solution)/shard_map/ppermute | solution.py:697
  12.4 22.5 %collective-permute-start.2 = (f32[5,3,32,128]{3,2,1,0:T(8,128)S(1)}, f32[5,3,32,128]{3,2,1,0:T(8,128)S(1)}, u32[]{:S(2)}, u32[]{:S(2)}) collective-permute-start(f32[5,3,32,128]{3,2,1,0:T(8,128)S(1)} %get-tuple-element.29), channel_id=1, source_target_pairs={{0,1},{1,2},{2,3},{4,5},{5,6},{6,7},{8,9},{9,10},{10,11},{12,13},{... | collective-permute-start | bytes 737288 | tf_op jit(solution)/shard_map/ppermute | solution.py:697
  13.9 21.0 %collective-permute-start.3 = (f32[5,3,32,128]{3,2,1,0:T(8,128)S(1)}, f32[5,3,32,128]{3,2,1,0:T(8,128)S(1)}, u32[]{:S(2)}, u32[]{:S(2)}) collective-permute-start(f32[5,3,32,128]{3,2,1,0:T(8,128)S(1)} %get-tuple-element.30), channel_id=1, source_target_pairs={{1,0},{2,1},{3,2},{5,4},{6,5},{7,6},{9,8},{10,9},{11,10},{13,12},{... | collective-permute-start | bytes 737288 | tf_op jit(solution)/shard_map/ppermute | solution.py:697
  31.6 3.3 %collective-permute-start.4 = (f32[5,3,16,128]{3,2,1,0:T(8,128)S(1)}, f32[5,3,16,128]{3,2,1,0:T(8,128)S(1)}, u32[]{:S(2)}, u32[]{:S(2)}) collective-permute-start(f32[5,3,16,128]{3,2,1,0:T(8,128)S(1)} %get-tuple-element.31), channel_id=1, source_target_pairs={{0,1},{1,2},{2,3},{4,5},{5,6},{6,7},{8,9},{9,10},{10,11},{12,13},{... | collective-permute-start | bytes 368648 | tf_op jit(solution)/shard_map/ppermute | solution.py:697
  33.6 4.3 %collective-permute-start.5 = (f32[5,3,16,128]{3,2,1,0:T(8,128)S(1)}, f32[5,3,16,128]{3,2,1,0:T(8,128)S(1)}, u32[]{:S(2)}, u32[]{:S(2)}) collective-permute-start(f32[5,3,16,128]{3,2,1,0:T(8,128)S(1)} %get-tuple-element.32), channel_id=1, source_target_pairs={{1,0},{2,1},{3,2},{5,4},{6,5},{7,6},{9,8},{10,9},{11,10},{13,12},{... | collective-permute-start | bytes 368648 | tf_op jit(solution)/shard_map/ppermute | solution.py:697

commit v5 on v4

--- a/solution.py
+++ b/solution.py
@@ -609,10 +609,11 @@
         last_scalars(keep_ref, totals_ref, rows)
         transposed(rows, square, table)
 
-    mine = pl.ds(group * 3 * PER, 3 * PER)
+    count = rhs_ref.shape[0] // 3
+    mine = pl.ds(group * 3 * count, 3 * count)
     basis = [ref.at[mine] for ref in (u0_all, u1_all, u2_all, w0_all, w1_all, w2_all, w3_all)]
-    for i in range(PER):
-        f = [spread(table, group * PER + i, j) for j in range(16)]
+    for i in range(count):
+        f = [spread(table, group * count + i, j) for j in range(16)]
         for c in range(3):
             k = 3 * i + c
             for r in range(0, height, 8):
@@ -763,7 +764,6 @@
         compiler_params=params(),
     )(*raw, up, down, from_left, from_right, left_ends, right_ends)
 
-    own_tile = pl.BlockSpec((3 * PER, height, width), lambda g: (g, 0, 0))
     own_tiles = pl.BlockSpec((3 * PER * PAIR, height, width), lambda g: (g, 0, 0))
     line = pl.BlockSpec((3 * PER * PAIR * HALO, width), lambda g: (g, 0))
     quarter = pl.BlockSpec((1, 3, height, width), lambda g: (PAIR * g // 4, 0, 0, 0))
@@ -800,9 +800,9 @@
     totals = gathered(sums)
     x, r = pl.pallas_call(
         functools.partial(last_kernel, height),
-        grid=(groups,),
-        in_specs=[fixed, kept, own_tile] + [resident] * 7,
-        out_specs=[own_tile] * 2,
+        grid=(groups // PAIR,),
+        in_specs=[fixed, kept, own_tiles] + [resident] * 7,
+        out_specs=[own_tiles] * 2,
         out_shape=[own_shape] * 2,
         scratch_shapes=[pltpu.VMEM((32, 128), F32), pltpu.VMEM((128, 128), F32), pltpu.VMEM((128, 128), F32)],
         compiler_params=params(),

time: 122 us -> 121 us (level)
  Pallas kernels: 64 us -> 62.2 us
    pallas_call x1, Pallas kernels: 7.23 us -> 5.45 us  [body(): pl.pallas_call(functools.partial(last_kernel, height), grid=(groups // PA...]
where the time goes in v5:
time: 121 us; the launch traced here: 120 us
  Pallas kernels  62.2 us (51%)
  blocking collectives  25.9 us (21%)
  waiting for transfers between devices  18.5 us (15%)
  starting transfers between devices  12.8 us (11%)
    pallas_call x1, Pallas kernels, body(): pl.pallas_call(functools.partial(first_kernel, height), grid=(groups // P...  27.2 us
    all_to_all x2, blocking collectives, gathered(): lax.all_to_all(jnp.broadcast_to(x[None], (n,) + x.shape), ('gx', 'gy'), 0...  25.9 us
    pallas_call x1, Pallas kernels, body(): pl.pallas_call(functools.partial(second_kernel, height), grid=(groups //...  22.3 us
    ppermute x6, waiting for transfers between devices, moved(): lax.ppermute(block, axis, [(i, i + distance) for i in range(n) if 0 <= i...  18.5 us
    ppermute x6, starting transfers between devices, moved(): lax.ppermute(block, axis, [(i, i + distance) for i in range(n) if 0 <= i...  12.8 us
    pallas_call x1, Pallas kernels, body(): pl.pallas_call(functools.partial(last_kernel, height), grid=(groups // PA...  5.45 us
    pallas_call x1, Pallas kernels, body(): pl.pallas_call(rows_kernel, grid=(1,), in_specs=[end_block(x, at) for at...  2.58 us
  transfers between devices with their start and end apart: 6, of which 3 were waited for; matrix products, arithmetic and copies ran while one was open for 0% of the time, Pallas kernels for 3%

profile of v5, /device:TPU:0, one launch (start us, length us, event | category | flops | bytes accessed | tf_op | source)
XLA Modules:
  0.0 120.3 jit_solution(10207160708195360725)
XLA Ops:
  0.6 0.0 copy-start.5
  0.6 0.0 copy-start.4
  0.7 0.0 copy-start.1
  0.7 0.0 copy-start.3
  0.7 0.0 copy-start.2
  0.7 0.0 copy-start
  0.7 2.6 %shard_map.77 = (f32[972,128]{1,0:T(8,128)}, f32[972,128]{1,0:T(8,128)}) custom-call(f32[144,32,128]{2,1,0:T(8,128)} %bitcast.3, f32[2,32,128]{2,1,0:T(8,128)} %stiffness.1, f32[2,32,128]{2,1,0:T(8,128)} %coupling.1, f32[12,32,128]{2,1,0:T(8,128)} %edges.1, s32[32,128]{1,0:T(8,128)} %flip.1, s32[32,128]{1,0:T(8,128)} %pinned.1, f32[144,32,128]{2,1,0:T(8,128)} %bitcast.4, ...), custom_call_target="tpu_custom_call" | custom-call | tf_op jit(solution)/shard_map/pallas_call | solution.py:728
  3.3 1.3 %collective-permute-start = (f32[972,128]{1,0:T(8,128)}, f32[972,128]{1,0:T(8,128)S(1)}, u32[]{:S(2)}, u32[]{:S(2)}) collective-permute-start(f32[972,128]{1,0:T(8,128)} %get-tuple-element.27), channel_id=1, source_target_pairs={{4,0},{8,4},{12,8},{16,12},{20,16},{24,20},{28,24},{5,1},{9,5},{13... | collective-permute-start | bytes 1493000 | tf_op jit(solution)/shard_map/ppermute | solution.py:698
  4.6 5.5 %collective-permute-start.1 = (f32[972,128]{1,0:T(8,128)}, f32[972,128]{1,0:T(8,128)S(1)}, u32[]{:S(2)}, u32[]{:S(2)}) collective-permute-start(f32[972,128]{1,0:T(8,128)} %get-tuple-element.28), channel_id=1, source_target_pairs={{0,4},{4,8},{8,12},{12,16},{16,20},{20,24},{24,28},{1,5},{5,9},{9,... | collective-permute-start | bytes 1493000 | tf_op jit(solution)/shard_map/ppermute | solution.py:698
  10.1 0.0 copy-done.5
  10.1 0.0 copy-done.4
  10.1 0.0 copy-done.1
  10.1 0.0 copy-done.3
  10.1 0.0 copy-done.2
  10.1 0.0 copy-done
  10.1 2.3 %shard_map.78 = (f32[5,3,32,128]{3,2,1,0:T(8,128)S(1)}, f32[5,3,32,128]{3,2,1,0:T(8,128)S(1)}) custom-call(f32[144,32,128]{2,1,0:T(8,128)S(1)} %bitcast.5, f32[2,32,128]{2,1,0:T(8,128)S(1)} %copy-done.2, f32[2,32,128]{2,1,0:T(8,128)S(1)} %copy-done.3, f32[12,32,128]{2,1,0:T(8,128)S(1)} %copy-done.1, s32[32,128]{1,0:T(8,128)S(1)} %copy-done.4, ...), custom_call_target="tpu_custom_call" | custom-call | tf_op jit(solution)/shard_map/pallas_call | solution.py:747
  12.4 1.5 %collective-permute-start.2 = (f32[5,3,32,128]{3,2,1,0:T(8,128)S(1)}, f32[5,3,32,128]{3,2,1,0:T(8,128)S(1)}, u32[]{:S(2)}, u32[]{:S(2)}) collective-permute-start(f32[5,3,32,128]{3,2,1,0:T(8,128)S(1)} %get-tuple-element.29), channel_id=1, source_target_pairs={{0,1},{1,2},{2,3},{4,5},{5,6},{6,7},{8,9},{9,10},{10,11},{12,13},{... | collective-permute-start | bytes 737288 | tf_op jit(solution)/shard_map/ppermute | solution.py:698
  13.9 1.3 %collective-permute-start.3 = (f32[5,3,32,128]{3,2,1,0:T(8,128)S(1)}, f32[5,3,32,128]{3,2,1,0:T(8,128)S(1)}, u32[]{:S(2)}, u32[]{:S(2)}) collective-permute-start(f32[5,3,32,128]{3,2,1,0:T(8,128)S(1)} %get-tuple-element.30), channel_id=1, source_target_pairs={{1,0},{2,1},{3,2},{5,4},{6,5},{7,6},{9,8},{10,9},{11,10},{13,12},{... | collective-permute-start | bytes 737288 | tf_op jit(solution)/shard_map/ppermute | solution.py:698
  15.2 4.5 %collective-permute-done.up_ref = f32[972,128]{1,0:T(8,128)S(1)} collective-permute-done((f32[972,128]{1,0:T(8,128)}, f32[972,128]{1,0:T(8,128)S(1)}, u32[]{:S(2)}, u32[]{:S(2)}) %collective-permute-start) | collective-permute-done | bytes 497696 | tf_op jit(solution)/shard_map/ppermute | solution.py:698
  19.7 11.0 %collective-permute-done.1.down_ref = f32[972,128]{1,0:T(8,128)S(1)} collective-permute-done((f32[972,128]{1,0:T(8,128)}, f32[972,128]{1,0:T(8,128)S(1)}, u32[]{:S(2)}, u32[]{:S(2)}) %collective-permute-start.1) | collective-permute-done | bytes 497696 | tf_op jit(solution)/shard_map/ppermute | solution.py:698
  30.7 0.9 shard_map.79
  31.6 1.9 %collective-permute-start.4 = (f32[5,3,16,128]{3,2,1,0:T(8,128)S(1)}, f32[5,3,16,128]{3,2,1,0:T(8,128)S(1)}, u32[]{:S(2)}, u32[]{:S(2)}) collective-permute-start(f32[5,3,16,128]{3,2,1,0:T(8,128)S(1)} %get-tuple-element.31), channel_id=1, source_target_pairs={{0,1},{1,2},{2,3},{4,5},{5,6},{6,7},{8,9},{9,10},{10,11},{12,13},{... | collective-permute-start | bytes 368648 | tf_op jit(solution)/shard_map/ppermute | solution.py:698
  33.6 1.3 %collective-permute-start.5 = (f32[5,3,16,128]{3,2,1,0:T(8,128)S(1)}, f32[5,3,16,128]{3,2,1,0:T(8,128)S(1)}, u32[]{:S(2)}, u32[]{:S(2)}) collective-permute-start(f32[5,3,16,128]{3,2,1,0:T(8,128)S(1)} %get-tuple-element.32), channel_id=1, source_target_pairs={{1,0},{2,1},{3,2},{5,4},{6,5},{7,6},{9,8},{10,9},{11,10},{13,12},{... | collective-permute-start | bytes 368648 | tf_op jit(solution)/shard_map/ppermute | solution.py:698
  34.9 0.0 collective-permute-done.2.left_ref
  34.9 0.0 collective-permute-done.3.right_ref
  34.9 0.0 collective-permute-done.4.left_ends
  34.9 3.0 %collective-permute-done.5.right_ends = f32[5,3,16,128]{3,2,1,0:T(8,128)S(1)} collective-permute-done((f32[5,3,16,128]{3,2,1,0:T(8,128)S(1)}, f32[5,3,16,128]{3,2,1,0:T(8,128)S(1)}, u32[]{:S(2)}, u32[]{:S(2)}) %collective-permute-start.5) | collective-permute-done | bytes 122912 | tf_op jit(solution)/shard_map/ppermute | solution.py:698
  37.9 1.5 %shard_map.80 = (f32[20,56,128]{2,1,0:T(8,128)S(1)}, f32[20,56,128]{2,1,0:T(8,128)S(1)}) custom-call(f32[2,32,128]{2,1,0:T(8,128)S(1)} %copy-done.2, f32[2,32,128]{2,1,0:T(8,128)S(1)} %copy-done.3, f32[12,32,128]{2,1,0:T(8,128)S(1)} %copy-done.1, s32[32,128]{1,0:T(8,128)S(1)} %copy-done.4, s32[32,128]{1,0:T(8,128)S(1)} %copy-done.5, ...), custom_call_target="tpu_custom_call" | custom-call | tf_op jit(solution)/shard_map/pallas_call | solution.py:760
  39.4 27.2 %shard_map.81 = (f32[144,56,128]{2,1,0:T(8,128)S(1)}, f32[144,56,128]{2,1,0:T(8,128)S(1)}, f32[144,56,128]{2,1,0:T(8,128)S(1)}, f32[144,56,128]{2,1,0:T(8,128)S(...) custom-call(f32[144,32,128]{2,1,0:T(8,128)S(1)} %bitcast.6, ...), custom_call_target="tpu_custom_call" | custom-call | tf_op jit(solution)/shard_map/pallas_call | solution.py:778
  66.7 15.9 %all_to_all.10.totals_ref = f32[32,8,128]{2,1,0:T(8,128)S(1)} all-to-all(f32[32,8,128]{2,1,0:T(8,128)S(1)} %broadcast_in_dim.4), channel_id=1, replica_groups=mesh['gx'=8,'gy'=4] {'gx','gy'}, dimensions={0} | all-to-all | bytes 262144 | tf_op jit(solution)/shard_map/all_to_all | solution.py:703
  82.5 22.3 %shard_map.82 = (f32[144,56,128]{2,1,0:T(8,128)S(1)}, f32[144,56,128]{2,1,0:T(8,128)S(1)}, f32[144,56,128]{2,1,0:T(8,128)S(1)}, f32[144,56,128]{2,1,0:T(8,128)S(...) custom-call(f32[32,8,128]{2,1,0:T(8,128)S(1)} %all_to_all.10.totals_ref, f32[144,56,128]{2,1,0:T(8,128)S(1)} %get-tuple-element.36.u0_all, ...), custom_call_target="tpu_custom_call" | custom-call | tf_op jit(solution)/shard_map/pallas_call | solution.py:790
  104.8 10.0 %all_to_all.11.totals_ref = f32[32,8,128]{2,1,0:T(8,128)S(1)} all-to-all(f32[32,8,128]{2,1,0:T(8,128)S(1)} %broadcast_in_dim.5), channel_id=1, replica_groups=mesh['gx'=8,'gy'=4] {'gx','gy'}, dimensions={0} | all-to-all | bytes 262144 | tf_op jit(solution)/shard_map/all_to_all | solution.py:703
  114.8 5.5 %shard_map.83 = (f32[144,32,128]{2,1,0:T(8,128)}, f32[144,32,128]{2,1,0:T(8,128)}) custom-call(f32[32,8,128]{2,1,0:T(8,128)S(1)} %all_to_all.11.totals_ref, f32[32,128]{1,0:T(8,128)S(1)} %get-tuple-element.45.keep_ref, f32[144,32,128]{2,1,0:T(8,128)S(1)} %bitcast.7, f32[144,56,128]{2,1,0:T(8,128)S(1)} %get-tuple-element.36.u0_all, ...), custom_call_target="tpu_custom_call" | custom-call | tf_op jit(solution)/shard_map/pallas_call | solution.py:801
  (2 shorter events, 0.0 us)
Async XLA Ops:
  0.6 9.4 %copy-start.5 = (s32[32,128]{1,0:T(8,128)S(1)}, s32[32,128]{1,0:T(8,128)}, u32[]{:S(2)}) copy-start(s32[32,128]{1,0:T(8,128)} %pinned.1) | copy-start | bytes 49156
  0.6 9.4 %copy-start.4 = (s32[32,128]{1,0:T(8,128)S(1)}, s32[32,128]{1,0:T(8,128)}, u32[]{:S(2)}) copy-start(s32[32,128]{1,0:T(8,128)} %flip.1) | copy-start | bytes 49156
  0.7 9.4 %copy-start.1 = (f32[12,32,128]{2,1,0:T(8,128)S(1)}, f32[12,32,128]{2,1,0:T(8,128)}, u32[]{:S(2)}) copy-start(f32[12,32,128]{2,1,0:T(8,128)} %edges.1) | copy-start | bytes 589828
  0.7 9.4 %copy-start.3 = (f32[2,32,128]{2,1,0:T(8,128)S(1)}, f32[2,32,128]{2,1,0:T(8,128)}, u32[]{:S(2)}) copy-start(f32[2,32,128]{2,1,0:T(8,128)} %coupling.1) | copy-start | bytes 98308
  0.7 9.4 %copy-start.2 = (f32[2,32,128]{2,1,0:T(8,128)S(1)}, f32[2,32,128]{2,1,0:T(8,128)}, u32[]{:S(2)}) copy-start(f32[2,32,128]{2,1,0:T(8,128)} %stiffness.1) | copy-start | bytes 98308
  0.7 9.4 %copy-start = (f32[48,3,32,128]{3,2,1,0:T(8,128)S(1)}, f32[48,3,32,128]{3,2,1,0:T(8,128)}, u32[]{:S(2)}) copy-start(f32[48,3,32,128]{3,2,1,0:T(8,128)} %param.6) | copy-start | bytes 7077892
  3.3 16.4 %collective-permute-start = (f32[972,128]{1,0:T(8,128)}, f32[972,128]{1,0:T(8,128)S(1)}, u32[]{:S(2)}, u32[]{:S(2)}) collective-permute-start(f32[972,128]{1,0:T(8,128)} %get-tuple-element.27), channel_id=1, source_target_pairs={{4,0},{8,4},{12,8},{16,12},{20,16},{24,20},{28,24},{5,1},{9,5},{13... | collective-permute-start | bytes 1493000 | tf_op jit(solution)/shard_map/ppermute | solution.py:698
  4.6 26.1 %collective-permute-start.1 = (f32[972,128]{1,0:T(8,128)}, f32[972,128]{1,0:T(8,128)S(1)}, u32[]{:S(2)}, u32[]{:S(2)}) collective-permute-start(f32[972,128]{1,0:T(8,128)} %get-tuple-element.28), channel_id=1, source_target_pairs={{0,4},{4,8},{8,12},{12,16},{16,20},{20,24},{24,28},{1,5},{5,9},{9,... | collective-permute-start | bytes 1493000 | tf_op jit(solution)/shard_map/ppermute | solution.py:698
  12.4 22.5 %collective-permute-start.2 = (f32[5,3,32,128]{3,2,1,0:T(8,128)S(1)}, f32[5,3,32,128]{3,2,1,0:T(8,128)S(1)}, u32[]{:S(2)}, u32[]{:S(2)}) collective-permute-start(f32[5,3,32,128]{3,2,1,0:T(8,128)S(1)} %get-tuple-element.29), channel_id=1, source_target_pairs={{0,1},{1,2},{2,3},{4,5},{5,6},{6,7},{8,9},{9,10},{10,11},{12,13},{... | collective-permute-start | bytes 737288 | tf_op jit(solution)/shard_map/ppermute | solution.py:698
  13.9 21.0 %collective-permute-start.3 = (f32[5,3,32,128]{3,2,1,0:T(8,128)S(1)}, f32[5,3,32,128]{3,2,1,0:T(8,128)S(1)}, u32[]{:S(2)}, u32[]{:S(2)}) collective-permute-start(f32[5,3,32,128]{3,2,1,0:T(8,128)S(1)} %get-tuple-element.30), channel_id=1, source_target_pairs={{1,0},{2,1},{3,2},{5,4},{6,5},{7,6},{9,8},{10,9},{11,10},{13,12},{... | collective-permute-start | bytes 737288 | tf_op jit(solution)/shard_map/ppermute | solution.py:698
  31.6 3.3 %collective-permute-start.4 = (f32[5,3,16,128]{3,2,1,0:T(8,128)S(1)}, f32[5,3,16,128]{3,2,1,0:T(8,128)S(1)}, u32[]{:S(2)}, u32[]{:S(2)}) collective-permute-start(f32[5,3,16,128]{3,2,1,0:T(8,128)S(1)} %get-tuple-element.31), channel_id=1, source_target_pairs={{0,1},{1,2},{2,3},{4,5},{5,6},{6,7},{8,9},{9,10},{10,11},{12,13},{... | collective-permute-start | bytes 368648 | tf_op jit(solution)/shard_map/ppermute | solution.py:698
  33.6 4.3 %collective-permute-start.5 = (f32[5,3,16,128]{3,2,1,0:T(8,128)S(1)}, f32[5,3,16,128]{3,2,1,0:T(8,128)S(1)}, u32[]{:S(2)}, u32[]{:S(2)}) collective-permute-start(f32[5,3,16,128]{3,2,1,0:T(8,128)S(1)} %get-tuple-element.32), channel_id=1, source_target_pairs={{1,0},{2,1},{3,2},{5,4},{6,5},{7,6},{9,8},{10,9},{11,10},{13,12},{... | collective-permute-start | bytes 368648 | tf_op jit(solution)/shard_map/ppermute | solution.py:698
